TPU v7x, 32 devices: a whole 2x2x4 slice. The times are simulated.
32 devices in a mesh: section: 2 (over core), tensor: 4 (over y, x), dp: 4 (over z).
Axes of the slice: x: 2, y: 2, z: 4, core: 2. Of those that a mesh axis runs over, the one named last changes fastest.
Arguments:
- latents: bfloat16 [2, 4, 256, 768], P(None, 'dp', 'tensor'), may hold values from -6 to 6
- cotangent: bfloat16 [2, 4, 256, 768], P(None, 'dp', 'tensor'), may hold values from -6 to 6
- labels: int32 [2, 4], P(None, 'dp'), may hold values from 0 to 1000
- timesteps: int32 [2, 4], P(None, 'dp'), may hold values from 0 to 999
- occupied: int32 [2, 4], P(None, 'dp'), may hold values from 0 to 1, as said below
- class_table: bfloat16 [1001, 768], replicated, may hold values from -6 to 6
- time_weight: bfloat16 [256, 768], replicated, may hold values from -0.5 to 0.5
- project_in: bfloat16 [2, 768, 3, 768], P('section', 'dp', None, 'tensor'), may hold values from -0.21875 to 0.21875
- project_in_bias: bfloat16 [2, 2, 768], P('section', None, ('tensor', 'dp')), may hold values from -3 to 3
- project_out: bfloat16 [2, 768, 768], P('section', 'tensor', 'dp'), may hold values from -0.625 to 0.625
- project_out_bias: bfloat16 [2, 768], P('section', 'dp'), may hold values from -2 to 2
- up_weight: bfloat16 [2, 768, 3072], P('section', 'dp', 'tensor'), may hold values from -0.21875 to 0.21875
- up_bias: bfloat16 [2, 3072], P('section', ('tensor', 'dp')), may hold values from -3 to 3
- down_weight: bfloat16 [2, 3072, 768], P('section', 'tensor', 'dp'), may hold values from -0.109375 to 0.109375
- down_bias: bfloat16 [2, 768], P('section', 'dp'), may hold values from -2 to 2
- modulate_weight: bfloat16 [2, 768, 6, 768], P('section', 'dp', None, 'tensor'), may hold values from -0.21875 to 0.21875
- modulate_bias: bfloat16 [2, 6, 768], P('section', None, ('tensor', 'dp')), may hold values from -3 to 3
Outputs:
- activations: bfloat16 [2, 2, 4, 256, 768], P('section', None, 'dp', 'tensor')
- input_grads: float32 [2, 2, 4, 256, 768], P('section', None, 'dp', 'tensor')
- class_table_grad: float32 [1001, 768], replicated
- time_weight_grad: float32 [256, 768], replicated
- project_in_grad: float32 [2, 768, 3, 768], P('section', 'dp', None, 'tensor')
- project_in_bias_grad: float32 [2, 2, 768], P('section', None, ('tensor', 'dp'))
- project_out_grad: float32 [2, 768, 768], P('section', 'tensor', 'dp')
- project_out_bias_grad: float32 [2, 768], P('section', 'dp')
- up_weight_grad: float32 [2, 768, 3072], P('section', 'dp', 'tensor')
- up_bias_grad: float32 [2, 3072], P('section', ('tensor', 'dp'))
- down_weight_grad: float32 [2, 3072, 768], P('section', 'tensor', 'dp')
- down_bias_grad: float32 [2, 768], P('section', 'dp')
- modulate_weight_grad: float32 [2, 768, 6, 768], P('section', 'dp', None, 'tensor')
- modulate_bias_grad: float32 [2, 6, 768], P('section', None, ('tensor', 'dp'))
Inputs may be any that keep to these rules, and one draw needn't show every extreme that they name: 1 where the slot holds a latent of the micro-batch, 0 where it is empty; every micro-batch has an empty slot and an occupied one.
All inputs are finite; a program needn't handle non-finite values.
Results may differ from a plain program's by a relative error of at most 0.028.
Values may be sent and summed in bfloat16 or wider, within the bound.
No kernel may reach another device: no remote copies, remote signals or barrier semaphores. Data moves between devices by JAX's collectives and lax.ppermute only.
A program may use at most 128 MiB of HBM per device.

v0:
```python
from functools import partial
import math

import jax
import jax.numpy as jnp
from jax import lax
from jax.sharding import PartitionSpec as P

HD = 64


epsilon = 1e-06
highest = lax.Precision.HIGHEST


def passed_along(value, axis, by):
    length = lax.axis_size(axis)
    pairs = [(i, i + by) for i in range(length) if 0 <= i + by < length]
    return lax.ppermute(value, axis, pairs)


def norm_rows(values):
    average = jnp.mean(values, axis=-1, keepdims=True)
    centred = values - average
    spread = jnp.mean(centred * centred, axis=-1, keepdims=True)
    return centred * lax.rsqrt(spread + epsilon)


def gelu_tanh(values):
    return jax.nn.gelu(values, approximate=True)


def sinus_features(stamps, columns):
    halfway = columns // 2
    frequency = jnp.exp(-math.log(10000.0) * jnp.arange(halfway, dtype=jnp.float32) / halfway)
    angles = stamps.astype(jnp.float32)[:, None] * frequency[None, :]
    return jnp.concatenate([jnp.cos(angles), jnp.sin(angles)], axis=-1)


def split_heads(matrix):
    return matrix.reshape(matrix.shape[0], matrix.shape[1], matrix.shape[2] // HD, HD)


def choose_rows(active_flag, first_value, second_value):
    return jnp.where(active_flag, first_value, second_value)


def add_active(active_flag, running, addend):
    return running + jnp.where(active_flag, addend, 0.0)


def fetch_weights(pieces):
    return (
        lax.all_gather(pieces[0], "dp", axis=0, tiled=True),
        lax.all_gather(pieces[1], "dp", axis=1, tiled=True),
        lax.all_gather(pieces[2], "dp", axis=1, tiled=True),
        lax.all_gather(pieces[3], "dp", axis=0, tiled=True),
        lax.all_gather(pieces[4], "dp", axis=0, tiled=True),
        lax.all_gather(pieces[5], "dp", axis=0, tiled=True),
        lax.all_gather(pieces[6], "dp", axis=1, tiled=True),
        lax.all_gather(pieces[7], "dp", axis=0, tiled=True),
        lax.all_gather(pieces[8], "dp", axis=0, tiled=True),
        lax.all_gather(pieces[9], "dp", axis=1, tiled=True),
    )


def modulate(cond_rows, gathered):
    partial_mod = jnp.einsum(
        "lc,ckd->lkd", cond_rows, gathered[8], preferred_element_type=jnp.float32
    ) + gathered[9].astype(jnp.float32)
    return lax.all_gather(partial_mod, "tensor", axis=2, tiled=True)


def gather_normed(rows):
    return lax.all_gather(rows, "tensor", axis=1, tiled=True)


def sum_branch(terms):
    return lax.psum_scatter(terms, "tensor", scatter_dimension=1, tiled=True)


def gather_grads(rows):
    return lax.all_gather(rows, "tensor", axis=1, tiled=True)


def sum_normed(terms):
    return lax.psum_scatter(terms, "tensor", scatter_dimension=1, tiled=True)


def send_forward(rows):
    return passed_along(rows, "section", 1)


def send_backward(rows):
    return passed_along(rows, "section", -1)


def attention_forward(queries, key_rows, value_rows):
    scale_factor = HD ** (-0.5)
    scores = (
        jnp.einsum("lqhe,lkhe->lhqk", queries, key_rows, preferred_element_type=jnp.float32)
        * scale_factor
    )
    largest = jnp.max(scores, axis=-1, keepdims=True)
    log_total = largest + jnp.log(jnp.sum(jnp.exp(scores - largest), axis=-1, keepdims=True))
    attention = jnp.exp(scores - log_total).astype(jnp.bfloat16)
    mixed_heads = jnp.einsum(
        "lhqk,lkhe->lqhe", attention, value_rows, preferred_element_type=jnp.float32
    )
    return (mixed_heads.astype(jnp.bfloat16), log_total)


def attention_backward(queries, key_rows, value_rows, log_total, mixed_grad):
    scale_factor = HD ** (-0.5)
    scores = (
        jnp.einsum("lqhe,lkhe->lhqk", queries, key_rows, preferred_element_type=jnp.float32)
        * scale_factor
    )
    attention = jnp.exp(scores - log_total)
    weight_grad = jnp.einsum(
        "lqhe,lkhe->lhqk", mixed_grad, value_rows, preferred_element_type=jnp.float32
    )
    value_grad = jnp.einsum(
        "lhqk,lqhe->lkhe",
        attention.astype(jnp.bfloat16),
        mixed_grad,
        preferred_element_type=jnp.float32,
    )
    row_dot = jnp.sum(attention * weight_grad, axis=-1, keepdims=True)
    score_grad = (attention * (weight_grad - row_dot)).astype(jnp.bfloat16)
    query_grad = (
        jnp.einsum("lhqk,lkhe->lqhe", score_grad, key_rows, preferred_element_type=jnp.float32)
        * scale_factor
    )
    key_grad = (
        jnp.einsum("lhqk,lqhe->lkhe", score_grad, queries, preferred_element_type=jnp.float32)
        * scale_factor
    )
    return (
        query_grad.astype(jnp.bfloat16),
        key_grad.astype(jnp.bfloat16),
        value_grad.astype(jnp.bfloat16),
    )


def layer_forward(inputs, modulation, weights):
    (
        inner_weight,
        inner_bias,
        outer_weight,
        outer_bias,
        upper_weight,
        upper_bias,
        lower_weight,
        lower_bias,
    ) = weights
    shift_one = modulation[:, 0][:, None, :]
    scale_one = modulation[:, 1][:, None, :]
    gate_one = modulation[:, 2][:, None, :]
    shift_two = modulation[:, 3][:, None, :]
    scale_two = modulation[:, 4][:, None, :]
    gate_two = modulation[:, 5][:, None, :]
    local_in = (norm_rows(inputs) * (1.0 + scale_one) + shift_one).astype(jnp.bfloat16)
    attn_in = gather_normed(local_in)
    projected = jnp.einsum(
        "ltd,dch->clth", attn_in, inner_weight, preferred_element_type=jnp.float32
    )
    queries = (projected[0] + inner_bias[0].astype(jnp.float32)).astype(jnp.bfloat16)
    key_rows = projected[1].astype(jnp.bfloat16)
    value_rows = (projected[2] + inner_bias[1].astype(jnp.float32)).astype(jnp.bfloat16)
    mixed_heads, log_total = attention_forward(
        split_heads(queries), split_heads(key_rows), split_heads(value_rows)
    )
    mixed_heads = mixed_heads.reshape(queries.shape)
    branch_part = jnp.einsum(
        "lth,hd->ltd", mixed_heads, outer_weight, preferred_element_type=jnp.float32
    )
    attn_out = sum_branch(branch_part) + outer_bias.astype(jnp.float32)
    middle = inputs + gate_one * attn_out
    local_mid = (norm_rows(middle) * (1.0 + scale_two) + shift_two).astype(jnp.bfloat16)
    mlp_in = gather_normed(local_mid)
    hidden_pre = jnp.einsum(
        "ltd,df->ltf", mlp_in, upper_weight, preferred_element_type=jnp.float32
    ) + upper_bias.astype(jnp.float32)
    hidden = gelu_tanh(hidden_pre).astype(jnp.bfloat16)
    mlp_part = jnp.einsum("ltf,fd->ltd", hidden, lower_weight, preferred_element_type=jnp.float32)
    mlp_out = sum_branch(mlp_part) + lower_bias.astype(jnp.float32)
    output = middle + gate_two * mlp_out
    kept_values = (
        inputs,
        attn_in,
        queries,
        key_rows,
        value_rows,
        log_total,
        mixed_heads,
        attn_out,
        middle,
        mlp_in,
        hidden_pre,
        hidden,
        mlp_out,
        modulation,
    )
    return (output, kept_values)


def layer_backward(grad_out, weights, kept_values):
    (
        inner_weight,
        inner_bias,
        outer_weight,
        outer_bias,
        upper_weight,
        upper_bias,
        lower_weight,
        lower_bias,
    ) = weights
    (
        inputs,
        attn_in,
        queries,
        key_rows,
        value_rows,
        log_total,
        mixed_heads,
        attn_out,
        middle,
        mlp_in,
        hidden_pre,
        hidden,
        mlp_out,
        modulation,
    ) = kept_values
    scale_one = modulation[:, 1][:, None, :]
    gate_one = modulation[:, 2][:, None, :]
    scale_two = modulation[:, 4][:, None, :]
    gate_two = modulation[:, 5][:, None, :]
    d_gate_two = jnp.sum(grad_out * mlp_out, axis=1)
    lower_local = (grad_out * gate_two).astype(jnp.bfloat16)
    grad_lower_bias = jnp.sum(lower_local.astype(jnp.float32), axis=(0, 1))
    lower_grad = gather_grads(lower_local)
    hidden_grad = jnp.einsum(
        "ltd,fd->ltf", lower_grad, lower_weight, preferred_element_type=jnp.float32
    )
    pre_grad = jax.vjp(gelu_tanh, hidden_pre)[1](hidden_grad)[0].astype(jnp.bfloat16)
    grad_upper_bias = jnp.sum(pre_grad.astype(jnp.float32), axis=(0, 1))
    mid_normed_grad = sum_normed(
        jnp.einsum("ltf,df->ltd", pre_grad, upper_weight, preferred_element_type=jnp.float32)
    )
    normed_two, second_pull = jax.vjp(norm_rows, middle)
    d_shift_two = jnp.sum(mid_normed_grad, axis=1)
    d_scale_two = jnp.sum(mid_normed_grad * normed_two, axis=1)
    middle_grad = grad_out + second_pull(mid_normed_grad * (1.0 + scale_two))[0]
    d_gate_one = jnp.sum(middle_grad * attn_out, axis=1)
    outer_local = (middle_grad * gate_one).astype(jnp.bfloat16)
    grad_outer_bias = jnp.sum(outer_local.astype(jnp.float32), axis=(0, 1))
    outer_grad = gather_grads(outer_local)
    mixed_grad = jnp.einsum(
        "ltd,hd->lth", outer_grad, outer_weight, preferred_element_type=jnp.float32
    ).astype(jnp.bfloat16)
    query_grad, key_grad, value_grad = attention_backward(
        split_heads(queries),
        split_heads(key_rows),
        split_heads(value_rows),
        log_total,
        split_heads(mixed_grad),
    )
    stacked = jnp.stack(
        [
            query_grad.reshape(queries.shape),
            key_grad.reshape(queries.shape),
            value_grad.reshape(queries.shape),
        ],
        axis=0,
    )
    grad_inner_bias = jnp.stack(
        [
            jnp.sum(stacked[0].astype(jnp.float32), axis=(0, 1)),
            jnp.sum(stacked[2].astype(jnp.float32), axis=(0, 1)),
        ]
    )
    in_normed_grad = sum_normed(
        jnp.einsum("clth,dch->ltd", stacked, inner_weight, preferred_element_type=jnp.float32)
    )
    normed_one, first_pull = jax.vjp(norm_rows, inputs)
    d_shift_one = jnp.sum(in_normed_grad, axis=1)
    d_scale_one = jnp.sum(in_normed_grad * normed_one, axis=1)
    input_grad = middle_grad + first_pull(in_normed_grad * (1.0 + scale_one))[0]
    mod_grad = jnp.stack(
        [d_shift_one, d_scale_one, d_gate_one, d_shift_two, d_scale_two, d_gate_two], axis=1
    )
    bias_grads = (grad_inner_bias, grad_outer_bias, grad_upper_bias, grad_lower_bias)
    operands = (attn_in, stacked, mixed_heads, outer_grad, mlp_in, pre_grad, hidden, lower_grad)
    return (input_grad, mod_grad, bias_grads, operands)


def mask_grads(active_flag, operands):
    return tuple(
        (
            jnp.where(active_flag, member, jnp.zeros_like(member)) if position % 2 == 1 else member
            for position, member in enumerate(operands)
        )
    )


def body(
    latents,
    cotangent,
    labels,
    timesteps,
    occupied,
    class_table,
    time_weight,
    project_in,
    project_in_bias,
    project_out,
    project_out_bias,
    up_weight,
    up_bias,
    down_weight,
    down_bias,
    modulate_weight,
    modulate_bias,
):
    section_index = lax.axis_index("section")
    is_first = section_index == 0
    micro_count = latents.shape[0]
    slot_count = latents.shape[1]
    width_model = latents.shape[3]
    class_count = class_table.shape[0]
    flat_labels = labels.reshape(-1)
    class_hot = (flat_labels[:, None] == jnp.arange(class_count, dtype=jnp.int32)[None, :]).astype(
        jnp.bfloat16
    )
    time_feats = sinus_features(timesteps.reshape(-1), time_weight.shape[0]).astype(jnp.bfloat16)
    condition = jnp.dot(class_hot, class_table, preferred_element_type=jnp.float32) + jnp.dot(
        time_feats, time_weight, preferred_element_type=jnp.float32
    )
    cond_act = (
        jax.nn.silu(condition).astype(jnp.bfloat16).reshape(micro_count, slot_count, width_model)
    )
    local_pieces = (
        project_in[0],
        project_in_bias[0],
        project_out[0],
        project_out_bias[0],
        up_weight[0],
        up_bias[0],
        down_weight[0],
        down_bias[0],
        modulate_weight[0],
        modulate_bias[0],
    )
    gathered = fetch_weights(local_pieces)
    received = jnp.zeros(latents.shape[1:], jnp.bfloat16)
    outputs = []
    kept_steps = []
    for step_index in range(micro_count + 1):
        fresh_rows = latents[min(step_index, micro_count - 1)]
        inputs = jnp.where(is_first, fresh_rows, received).astype(jnp.float32)
        micro_index = jnp.clip(step_index - section_index, 0, micro_count - 1)
        modulation = modulate(cond_act[micro_index], gathered)
        result, kept_values = layer_forward(inputs, modulation, gathered[:8])
        sent_rows = result.astype(jnp.bfloat16)
        outputs.append(sent_rows)
        kept_steps.append(kept_values)
        if step_index < micro_count:
            received = send_forward(sent_rows)
    back_weights = fetch_weights(local_pieces)
    bias_totals = (
        jnp.zeros(back_weights[1].shape, jnp.float32),
        jnp.zeros(back_weights[3].shape, jnp.float32),
        jnp.zeros(back_weights[5].shape, jnp.float32),
        jnp.zeros(back_weights[7].shape, jnp.float32),
    )
    mod_total = jnp.zeros((micro_count, slot_count, 6, width_model), jnp.float32)
    grad_received = jnp.zeros(latents.shape[1:], jnp.bfloat16)
    input_grads = []
    step_operands = []
    for step_index in range(micro_count + 1):
        later_micro = min(step_index, micro_count - 1)
        earlier_micro = max(step_index - 1, 0)
        kept_values = jax.tree.map(
            partial(choose_rows, is_first), kept_steps[earlier_micro], kept_steps[later_micro + 1]
        )
        masked = (
            cotangent[later_micro].astype(jnp.float32)
            * occupied[later_micro].astype(jnp.float32)[:, None, None]
        )
        grad_out = jnp.where(is_first, grad_received.astype(jnp.float32), masked)
        input_grad, mod_grad, bias_grads, operands = layer_backward(
            grad_out, back_weights[:8], kept_values
        )
        active = jnp.where(is_first, step_index >= 1, step_index < micro_count)
        bias_totals = jax.tree.map(partial(add_active, active), bias_totals, bias_grads)
        step_operands.append(mask_grads(active, operands))
        micro_index = jnp.where(is_first, earlier_micro, later_micro)
        mod_total = mod_total.at[micro_index].add(jnp.where(active, mod_grad, 0.0))
        input_grads.append(input_grad)
        if step_index < micro_count:
            grad_received = send_backward(input_grad.astype(jnp.bfloat16))
    all_operands = tuple(
        (jnp.stack([entry[position] for entry in step_operands]) for position in range(8))
    )
    grad_inner = jnp.einsum(
        "sltd,sclth->dch", all_operands[0], all_operands[1], preferred_element_type=jnp.float32
    )
    grad_outer = jnp.einsum(
        "slth,sltd->hd", all_operands[2], all_operands[3], preferred_element_type=jnp.float32
    )
    grad_upper = jnp.einsum(
        "sltd,sltf->df", all_operands[4], all_operands[5], preferred_element_type=jnp.float32
    )
    grad_lower = jnp.einsum(
        "sltf,sltd->fd", all_operands[6], all_operands[7], preferred_element_type=jnp.float32
    )
    totals = (
        grad_inner,
        bias_totals[0],
        grad_outer,
        bias_totals[1],
        grad_upper,
        bias_totals[2],
        grad_lower,
        bias_totals[3],
    )
    activations = jnp.stack(
        [
            jnp.where(is_first, outputs[position], outputs[position + 1])
            for position in range(micro_count)
        ]
    )[None]
    grads_in = jnp.stack(
        [
            jnp.where(is_first, input_grads[position + 1], input_grads[position])
            for position in range(micro_count)
        ]
    )[None]
    mod_sum, outer_bias_sum, lower_bias_sum = (
        lax.psum(mod_total.astype(jnp.bfloat16), "tensor").astype(jnp.float32),
        lax.psum(totals[3].astype(jnp.bfloat16), "tensor").astype(jnp.float32),
        lax.psum(totals[7].astype(jnp.bfloat16), "tensor").astype(jnp.float32),
    )
    shard_width = back_weights[8].shape[-1]
    shard_start = lax.axis_index("tensor") * shard_width
    mod_shard = lax.dynamic_slice_in_dim(mod_sum, shard_start, shard_width, 3)
    grad_mod_weight = jnp.einsum(
        "mlc,mlkd->ckd", cond_act.astype(jnp.float32), mod_shard, precision=highest
    )
    grad_mod_bias = jnp.sum(mod_shard, axis=(0, 1))
    act_grad = jnp.einsum(
        "mlkd,ckd->mlc", mod_shard, back_weights[8].astype(jnp.float32), precision=highest
    )
    cond_grad = jax.vjp(jax.nn.silu, condition)[1](act_grad.reshape(-1, width_model))[0]
    table_part = jnp.dot(class_hot.astype(jnp.float32).T, cond_grad, precision=highest)
    time_part = jnp.dot(time_feats.astype(jnp.float32).T, cond_grad, precision=highest)
    table_grad, time_grad = lax.psum((table_part, time_part), ("section", "tensor", "dp"))
    reduced = (
        lax.psum_scatter(
            totals[0].astype(jnp.bfloat16), "dp", scatter_dimension=0, tiled=True
        ).astype(jnp.float32),
        lax.psum_scatter(
            totals[1].astype(jnp.bfloat16), "dp", scatter_dimension=1, tiled=True
        ).astype(jnp.float32),
        lax.psum_scatter(
            totals[2].astype(jnp.bfloat16), "dp", scatter_dimension=1, tiled=True
        ).astype(jnp.float32),
        lax.psum_scatter(
            outer_bias_sum.astype(jnp.bfloat16), "dp", scatter_dimension=0, tiled=True
        ).astype(jnp.float32),
        lax.psum_scatter(
            totals[4].astype(jnp.bfloat16), "dp", scatter_dimension=0, tiled=True
        ).astype(jnp.float32),
        lax.psum_scatter(
            totals[5].astype(jnp.bfloat16), "dp", scatter_dimension=0, tiled=True
        ).astype(jnp.float32),
        lax.psum_scatter(
            totals[6].astype(jnp.bfloat16), "dp", scatter_dimension=1, tiled=True
        ).astype(jnp.float32),
        lax.psum_scatter(
            lower_bias_sum.astype(jnp.bfloat16), "dp", scatter_dimension=0, tiled=True
        ).astype(jnp.float32),
        lax.psum_scatter(
            grad_mod_weight.astype(jnp.bfloat16), "dp", scatter_dimension=0, tiled=True
        ).astype(jnp.float32),
        lax.psum_scatter(
            grad_mod_bias.astype(jnp.bfloat16), "dp", scatter_dimension=1, tiled=True
        ).astype(jnp.float32),
    )
    return (
        activations,
        grads_in,
        table_grad,
        time_grad,
        reduced[0][None],
        reduced[1][None],
        reduced[2][None],
        reduced[3][None],
        reduced[4][None],
        reduced[5][None],
        reduced[6][None],
        reduced[7][None],
        reduced[8][None],
        reduced[9][None],
    )


def solution(mesh):
    in_specs = (
        P(None, "dp", "tensor", None),
        P(None, "dp", "tensor", None),
        P(None, "dp"),
        P(None, "dp"),
        P(None, "dp"),
        P(),
        P(),
        P("section", "dp", None, "tensor"),
        P("section", None, ("tensor", "dp")),
        P("section", "tensor", "dp"),
        P("section", "dp"),
        P("section", "dp", "tensor"),
        P("section", ("tensor", "dp")),
        P("section", "tensor", "dp"),
        P("section", "dp"),
        P("section", "dp", None, "tensor"),
        P("section", None, ("tensor", "dp")),
    )
    out_specs = (
        P("section", None, "dp", "tensor", None),
        P("section", None, "dp", "tensor", None),
        P(),
        P(),
        P("section", "dp", None, "tensor"),
        P("section", None, ("tensor", "dp")),
        P("section", "tensor", "dp"),
        P("section", "dp"),
        P("section", "dp", "tensor"),
        P("section", ("tensor", "dp")),
        P("section", "tensor", "dp"),
        P("section", "dp"),
        P("section", "dp", None, "tensor"),
        P("section", None, ("tensor", "dp")),
    )
    return jax.shard_map(body, mesh=mesh, in_specs=in_specs, out_specs=out_specs, check_vma=False)
```

profile of v0, /device:TPU:0, one launch (start us, length us, event | category | flops | bytes accessed | tf_op | source)
XLA Modules:
  0.0 1044.3 jit_solution(3103155331452718971)
XLA Ops:
  10.0 51.6 %all-gather.3 = bf16[1,768,3,192]{3,2,0,1:T(4,128)(2,1)} all-gather(bf16[1,192,3,192]{3,2,0,1:T(4,128)(2,1)S(1)} %copy.162), channel_id=5, replica_groups=mesh['section'=2,'tensor'=4,'dp'=4] {'dp'}, dimensions={1}, use_global_device_ids=true | all-gather | bytes 1105920 | tf_op jit(solution)/shard_map/all_gather | solution.py:54
  64.4 14.6 %all-gather.1 = bf16[1,6,192]{1,0,2:T(2,128)(2,1)S(1)} all-gather(bf16[1,6,48]{1,0,2:T(2,128)(2,1)S(1)} %copy.159), channel_id=3, replica_groups=mesh['section'=2,'tensor'=4,'dp'=4] {'dp'}, dimensions={2}, use_global_device_ids=true | all-gather | bytes 2880 | tf_op jit(solution)/shard_map/all_gather | solution.py:63
  79.2 14.0 %all-gather.4 = bf16[1,2,192]{1,0,2:T(2,128)(2,1)S(1)} all-gather(bf16[1,2,48]{1,0,2:T(2,128)(2,1)S(1)} %copy.164), channel_id=6, replica_groups=mesh['section'=2,'tensor'=4,'dp'=4] {'dp'}, dimensions={2}, use_global_device_ids=true | all-gather | bytes 960 | tf_op jit(solution)/shard_map/all_gather | solution.py:55
  96.6 18.5 %all-gather.5 = bf16[1,192,768]{1,0,2:T(2,128)(2,1)} all-gather(bf16[1,192,192]{1,0,2:T(2,128)(2,1)S(1)} %copy.166), channel_id=7, replica_groups=mesh['section'=2,'tensor'=4,'dp'=4] {'dp'}, dimensions={2}, use_global_device_ids=true | all-gather | bytes 368640 | tf_op jit(solution)/shard_map/all_gather | solution.py:56
  155.1 12.7 %all-reduce.9 = (bf16[768]{0:T(1024)(128)(2,1)S(1)}, bf16[768]{0:T(1024)(128)(2,1)S(1)}, bf16[768]{0:T(1024)(128)(2,1)}) all-reduce(bf16[768]{0:T(1024)(128)(2,1)S(1)} %dynamic-update-slice.9, bf16[768]{0:T(1024)(128)(2,1)S(1)} %dynamic-update-slice.10, ...), channel_id=8, replica_groups=mesh['section'=2,'tensor'=4,'dp'=4] {'dp'}, use_global_device_ids=true, to_apply=%add.1 | all-reduce | flops 2304 | bytes 9216
  167.8 10.4 reduce-scatter.26.cloned.1.call-done
  190.4 19.9 %all-gather.22.cloned.1.call-done = bf16[1,768,768]{2,1,0:T(8,128)(2,1)} async-done(((bf16[1,192,768]{2,1,0:T(8,128)(2,1)}), bf16[1,768,768]{2,1,0:T(8,128)(2,1)}) %all-gather.22.cloned.1.call-update) | async-done | bytes 1179664 | tf_op jit(solution)/shard_map/all_gather | solution.py:58
  213.0 28.3 %all-gather.24.cloned.1.call-done = bf16[1,768,768]{1,2,0:T(8,128)(2,1)} async-done(((bf16[1,768,192]{1,2,0:T(8,128)(2,1)}), bf16[1,768,768]{1,2,0:T(8,128)(2,1)}) %all-gather.24.cloned.1.call-update) | async-done | bytes 1179664 | tf_op jit(solution)/shard_map/all_gather | solution.py:60
  254.6 15.2 %reduce-scatter.28.cloned.1.call-done = f32[1,64,768]{2,1,0:T(8,128)} async-done(((f32[1,256,768]{2,1,0:T(8,128)}), f32[1,64,768]{2,1,0:T(8,128)}) %reduce-scatter.28.cloned.1.call-update) | async-done | bytes 196624 | tf_op jit(solution)/shard_map/reduce_scatter | solution.py:79
  341.1 21.9 %reduce-scatter.38.cloned.1.call-done = f32[1,64,768]{2,1,0:T(8,128)} async-done(((f32[1,256,768]{2,1,0:T(8,128)}), f32[1,64,768]{2,1,0:T(8,128)}) %reduce-scatter.38.cloned.1.call-update) | async-done | bytes 196624 | tf_op jit(solution)/shard_map/reduce_scatter | solution.py:87
  367.8 11.6 %all_gather.100 = bf16[1,256,768]{2,1,0:T(8,128)(2,1)S(1)} all-gather(bf16[1,64,768]{2,1,0:T(8,128)(2,1)S(1)} %get-tuple-element.188), channel_id=1, replica_groups=mesh['section'=2,'tensor'=4,'dp'=4] {'tensor'}, dimensions={1}, use_global_device_ids=true | all-gather | bytes 491520 | tf_op jit(solution)/shard_map/all_gather | solution.py:83
  400.0 21.9 %reduce-scatter.40.cloned.1.call-done = f32[1,64,768]{2,1,0:T(8,128)} async-done(((f32[1,256,768]{2,1,0:T(8,128)}), f32[1,64,768]{2,1,0:T(8,128)}) %reduce-scatter.40.cloned.1.call-update) | async-done | bytes 196624 | tf_op jit(solution)/shard_map/reduce_scatter | solution.py:87
  493.9 22.2 %reduce-scatter.42.cloned.1.call-done = f32[1,64,768]{2,1,0:T(8,128)} async-done(((f32[1,256,768]{2,1,0:T(8,128)}), f32[1,64,768]{2,1,0:T(8,128)}) %reduce-scatter.42.cloned.1.call-update) | async-done | bytes 196624 | tf_op jit(solution)/shard_map/reduce_scatter | solution.py:87
  537.6 26.1 %reduce-scatter.44.cloned.1.call-done = f32[1,64,768]{2,1,0:T(8,128)} async-done(((f32[1,256,768]{2,1,0:T(8,128)}), f32[1,64,768]{2,1,0:T(8,128)}) %reduce-scatter.44.cloned.1.call-update) | async-done | bytes 196624 | tf_op jit(solution)/shard_map/reduce_scatter | solution.py:87
  589.2 22.9 %reduce-scatter.46.cloned.1.call-done = f32[1,64,768]{2,1,0:T(8,128)} async-done(((f32[1,256,768]{2,1,0:T(8,128)}), f32[1,64,768]{2,1,0:T(8,128)}) %reduce-scatter.46.cloned.1.call-update) | async-done | bytes 196624 | tf_op jit(solution)/shard_map/reduce_scatter | solution.py:87
  615.4 25.6 %reduce-scatter.36.cloned.1.call-done = f32[1,64,768]{2,1,0:T(8,128)} async-done(((f32[1,256,768]{2,1,0:T(8,128)}), f32[1,64,768]{2,1,0:T(8,128)}) %reduce-scatter.36.cloned.1.call-update) | async-done | bytes 196624 | tf_op jit(solution)/shard_map/reduce_scatter | solution.py:79
  682.3 12.5 %all-reduce.8 = (bf16[768]{0:T(1024)(128)(2,1)}, bf16[768]{0:T(1024)(128)(2,1)}, bf16[768]{0:T(1024)(128)(2,1)}) all-reduce(bf16[768]{0:T(1024)(128)(2,1)} %add_convert_fusion.14, bf16[768]{0:T(1024)(128)(2,1)} %add_convert_fusion.13, bf16[768]{0:T(1024)(128)(2,1)} %add_convert_fusion.12), channel_id=30, replica_groups=mesh['section'=2,'tensor'=4,'dp'=4] {'dp'}, use_global_device_ids=true, to_apply=%region_92.93.clone | all-reduce | flops 2304 | bytes 9216
  705.4 15.3 %all-reduce.10 = (bf16[2,1,6,768]{3,0,2,1:T(2,128)(2,1)S(1)}, bf16[192]{0:T(256)(128)(2,1)S(1)}, bf16[192]{0:T(256)(128)(2,1)S(1)}) all-reduce(bf16[2,1,6,768]{3,0,2,1:T(2,128)(2,1)S(1)} %convert_element_type.738, bf16[192]{0:T(256)(128)(2,1)S(1)} %copy-done.193, ...), channel_id=1, replica_groups=mesh['section'=2,'tensor'=4,'dp'=4] {'tensor'}, use_global_device_ids=true, to_apply=%region_76.77 | all-reduce | flops 9600 | bytes 38400 | tf_op jit(solution)/shard_map/psum | solution.py:441
  739.8 16.0 %reduce-scatter.52.cloned.1.call-done = bf16[192,768]{1,0:T(8,128)(2,1)} async-done(((bf16[768,768]{1,0:T(8,128)(2,1)}), bf16[192,768]{1,0:T(8,128)(2,1)}) %reduce-scatter.52.cloned.1.call-update) | async-done | bytes 294928 | tf_op jit(solution)/shard_map/reduce_scatter | solution.py:472
  757.6 28.4 %reduce-scatter.54.cloned.1.call-done = bf16[768,192]{0,1:T(8,128)(2,1)} async-done(((bf16[768,768]{0,1:T(8,128)(2,1)}), bf16[768,192]{0,1:T(8,128)(2,1)}) %reduce-scatter.54.cloned.1.call-update) | async-done | bytes 294928 | tf_op jit(solution)/shard_map/reduce_scatter | solution.py:478
  789.8 16.1 %reduce-scatter.62.cloned.1.call-done = bf16[48,6]{1,0:T(8,128)(2,1)} async-done(((bf16[192,6]{1,0:T(8,128)(2,1)}), bf16[48,6]{1,0:T(8,128)(2,1)}) %reduce-scatter.62.cloned.1.call-update) | async-done | bytes 592
  807.3 29.0 %reduce-scatter.50.cloned.1.call-done = bf16[192,3,192]{2,0,1:T(8,128)(2,1)} async-done(((bf16[768,3,192]{2,0,1:T(8,128)(2,1)}), bf16[192,3,192]{2,0,1:T(8,128)(2,1)}) %reduce-scatter.50.cloned.1.call-update) | async-done | bytes 221200 | tf_op jit(solution)/shard_map/reduce_scatter | solution.py:460
  838.1 47.4 %reduce-scatter.56.cloned.1.call-done = bf16[192,6,192]{2,0,1:T(8,128)(2,1)} async-done(((bf16[768,6,192]{2,0,1:T(8,128)(2,1)}), bf16[192,6,192]{2,0,1:T(8,128)(2,1)}) %reduce-scatter.56.cloned.1.call-update) | async-done | bytes 442384 | tf_op jit(solution)/shard_map/reduce_scatter | solution.py:484
  887.6 145.0 %all-reduce.13.cloned.1.call-done = (f32[1001,768]{1,0:T(8,128)}, f32[256,768]{1,0:T(8,128)}) async-done(((f32[1001,768]{1,0:T(8,128)}, f32[256,768]{1,0:T(8,128)}), (f32[1001,768]{1,0:T(8,128)}, f32[256,768]{1,0:T(8,128)})) %all-reduce.13.cloned.1.call-update) | async-done | bytes 3861520 | tf_op jit(solution)/shard_map/psum | solution.py:458
  (764 shorter events, 377.8 us)
Async XLA Ops:
  7.2 113.5 %all-gather.20.cloned.1.call-start = ((), (), s32[]{:S(2)}) async-start(), calls=%async_computation.35 | async-start | bytes 3932160 | tf_op jit(solution)/shard_map/all_gather | solution.py:62
  9.7 168.5 %reduce-scatter.26.cloned.1.call-start = ((), (), s32[]{:S(2)}) async-start(), calls=%async_computation.19 | async-start | bytes 983040 | tf_op jit(solution)/shard_map/reduce_scatter | solution.py:79
  151.7 58.5 %all-gather.22.cloned.1.call-start = ((), (), s32[]{:S(2)}) async-start(), calls=%async_computation.36 | async-start | bytes 1474560 | tf_op jit(solution)/shard_map/all_gather | solution.py:58
  152.4 88.8 %all-gather.24.cloned.1.call-start = ((), (), s32[]{:S(2)}) async-start(), calls=%async_computation.37 | async-start | bytes 1474560 | tf_op jit(solution)/shard_map/all_gather | solution.py:60
  153.0 116.8 %reduce-scatter.28.cloned.1.call-start = ((), (), s32[]{:S(2)}) async-start(), calls=%async_computation.20 | async-start | bytes 983040 | tf_op jit(solution)/shard_map/reduce_scatter | solution.py:79
  244.3 72.0 %reduce-scatter.30.cloned.1.call-start = ((), (), s32[]{:S(2)}) async-start(), calls=%async_computation.21 | async-start | bytes 983040 | tf_op jit(solution)/shard_map/reduce_scatter | solution.py:79
  270.8 3.4 collective-permute-start
  289.4 73.7 %reduce-scatter.38.cloned.1.call-start = ((), (), s32[]{:S(2)}) async-start(), calls=%async_computation.25 | async-start | bytes 983040 | tf_op jit(solution)/shard_map/reduce_scatter | solution.py:87
  336.8 56.0 %reduce-scatter.32.cloned.1.call-start = ((), (), s32[]{:S(2)}) async-start(), calls=%async_computation.22 | async-start | bytes 983040 | tf_op jit(solution)/shard_map/reduce_scatter | solution.py:79
  341.1 80.8 %reduce-scatter.40.cloned.1.call-start = ((), (), s32[]{:S(2)}) async-start(), calls=%async_computation.26 | async-start | bytes 983040 | tf_op jit(solution)/shard_map/reduce_scatter | solution.py:87
  384.9 81.1 %reduce-scatter.34.cloned.1.call-start = ((), (), s32[]{:S(2)}) async-start(), calls=%async_computation.23 | async-start | bytes 983040 | tf_op jit(solution)/shard_map/reduce_scatter | solution.py:79
  438.8 77.3 %reduce-scatter.42.cloned.1.call-start = ((), (), s32[]{:S(2)}) async-start(), calls=%async_computation.27 | async-start | bytes 983040 | tf_op jit(solution)/shard_map/reduce_scatter | solution.py:87
  489.9 73.9 %reduce-scatter.44.cloned.1.call-start = ((), (), s32[]{:S(2)}) async-start(), calls=%async_computation.28 | async-start | bytes 983040 | tf_op jit(solution)/shard_map/reduce_scatter | solution.py:87
  537.5 74.6 %reduce-scatter.46.cloned.1.call-start = ((), (), s32[]{:S(2)}) async-start(), calls=%async_computation.29 | async-start | bytes 983040 | tf_op jit(solution)/shard_map/reduce_scatter | solution.py:87
  585.9 55.1 %reduce-scatter.36.cloned.1.call-start = ((), (), s32[]{:S(2)}) async-start(), calls=%async_computation.24 | async-start | bytes 983040 | tf_op jit(solution)/shard_map/reduce_scatter | solution.py:79
  589.0 110.0 %reduce-scatter.48.cloned.1.call-start = ((), (), s32[]{:S(2)}) async-start(), calls=%async_computation.30 | async-start | bytes 983040 | tf_op jit(solution)/shard_map/reduce_scatter | solution.py:87
  657.2 79.5 %reduce-scatter.58.cloned.1.call-start = ((), (), s32[]{:S(2)}) async-start(), calls=%async_computation.38 | async-start | bytes 61440
  660.9 77.2 %reduce-scatter.60.cloned.1.call-start = ((), (), s32[]{:S(2)}) async-start(), calls=%async_computation.39 | async-start | bytes 491520
  665.2 90.6 %reduce-scatter.52.cloned.1.call-start = ((), (), s32[]{:S(2)}) async-start(), calls=%async_computation.32 | async-start | bytes 1474560 | tf_op jit(solution)/shard_map/reduce_scatter | solution.py:472
  669.0 117.1 %reduce-scatter.54.cloned.1.call-start = ((), (), s32[]{:S(2)}) async-start(), calls=%async_computation.33 | async-start | bytes 1474560 | tf_op jit(solution)/shard_map/reduce_scatter | solution.py:478
  678.3 127.6 %reduce-scatter.62.cloned.1.call-start = ((), (), s32[]{:S(2)}) async-start(), calls=%async_computation.40 | async-start | bytes 61440
  721.5 114.7 %reduce-scatter.50.cloned.1.call-start = ((), (), s32[]{:S(2)}) async-start(), calls=%async_computation.31 | async-start | bytes 1474560 | tf_op jit(solution)/shard_map/reduce_scatter | solution.py:460
  725.2 160.2 %reduce-scatter.56.cloned.1.call-start = ((), (), s32[]{:S(2)}) async-start(), calls=%async_computation.34 | async-start | bytes 2949120 | tf_op jit(solution)/shard_map/reduce_scatter | solution.py:484
  727.6 305.0 %all-reduce.13.cloned.1.call-start = ((), (), s32[]{:S(2)}) async-start(), calls=%async_computation.41 | async-start | bytes 7766016 | tf_op jit(solution)/shard_map/psum | solution.py:458
  (206 other events, 2090.9 us)
Sparse Core Ops, SparseCore 0:
  10.2 87.2 all-gather.19
  151.8 26.3 reduce-scatter.25
  179.8 30.4 all-gather.21
  211.7 29.5 all-gather.23
  244.6 25.2 reduce-scatter.27
  289.5 26.6 reduce-scatter.29
  336.9 26.0 reduce-scatter.37
  366.0 26.8 reduce-scatter.31
  395.8 26.0 reduce-scatter.39
  438.9 27.0 reduce-scatter.33
  490.0 26.0 reduce-scatter.41
  537.7 26.0 reduce-scatter.43
  586.0 26.1 reduce-scatter.45
  614.9 26.0 reduce-scatter.35
  657.3 26.0 reduce-scatter.47
  685.6 18.9 reduce-scatter.57
  707.4 18.7 reduce-scatter.59
  728.3 27.4 reduce-scatter.51
  758.1 27.8 reduce-scatter.53
  788.1 17.7 reduce-scatter.61
  808.9 27.3 reduce-scatter.49
  838.6 46.7 reduce-scatter.55
  892.6 139.9 all-reduce.12
where the time goes:
time: 1060 us; the launch traced here: 1040 us
  waiting for transfers between devices  521 us (49%)
  blocking collectives  281 us (27%)
  other arithmetic  104 us (10%)
  matrix products  62.7 us (6%)
  local copies, waits for them, and re-layouts  48.7 us (5%)
  between operations  19.6 us (2%)
    psum x1, waiting for transfers between devices, body(): lax.psum((table_part, time_part), ('section', 'tensor', 'dp'))  145 us
    reduce_scatter x6, waiting for transfers between devices, sum_normed(): return lax.psum_scatter(terms, 'tensor', scatter_dimension=1, tiled=True)  115 us
    reduce_scatter x6, waiting for transfers between devices, sum_branch(): return lax.psum_scatter(terms, 'tensor', scatter_dimension=1, tiled=True)  71.2 us
    all_gather x6, blocking collectives, gather_grads(): return lax.all_gather(rows, 'tensor', axis=1, tiled=True)  60.6 us
    all_gather x6, blocking collectives, gather_normed(): return lax.all_gather(rows, 'tensor', axis=1, tiled=True)  57.9 us
    all_gather x1, blocking collectives, fetch_weights(): lax.all_gather(pieces[0], 'dp', axis=0, tiled=True)  51.6 us
    reduce_scatter x1, waiting for transfers between devices, body(): lax.psum_scatter(grad_mod_weight.astype(jnp.bfloat16), 'dp', scatter_dime...  47.4 us
    unnamed x450, local copies, waits for them, and re-layouts  37.5 us
  transfers between devices with their start and end apart: 27, of which 22 were waited for; matrix products, arithmetic and copies ran while one was open for 11% of the time, Pallas kernels for 0%

commit v1 on v0

v1 whole, which is shorter than its diff:
```python
import math

import jax
import jax.numpy as jnp
from jax import lax
from jax.sharding import PartitionSpec as P

HD = 64
EPS = 1e-06
HIGH = lax.Precision.HIGHEST
F32 = jnp.float32
BF16 = jnp.bfloat16


def partner(axis, k):
    size = lax.axis_size(axis)
    here = lax.axis_index(axis)
    if size & (size - 1) == 0:
        return here ^ k
    return (here - k) % size


def exchange(value, axis, k):
    size = lax.axis_size(axis)
    if size & (size - 1) == 0:
        return lax.ppermute(value, axis, [(i, i ^ k) for i in range(size)])
    return lax.ppermute(value, axis, [(i, (i - k) % size) for i in range(size)])


def fetch(value, axis, k):
    size = lax.axis_size(axis)
    if size & (size - 1) == 0:
        return lax.ppermute(value, axis, [(i, i ^ k) for i in range(size)])
    return lax.ppermute(value, axis, [(i, (i + k) % size) for i in range(size)])


def swap(value):
    return lax.ppermute(value, "section", [(0, 1), (1, 0)])


def gather_list(value, axis):
    return [value] + [fetch(value, axis, k) for k in range(1, lax.axis_size(axis))]


def place(pieces, axis):
    out = jnp.zeros((len(pieces),) + pieces[0].shape, pieces[0].dtype)
    for k, piece in enumerate(pieces):
        out = lax.dynamic_update_index_in_dim(out, piece, partner(axis, k), 0)
    return out


def gather_tokens(rows):
    return jnp.concatenate(gather_list(rows, "tensor"), axis=0)


def scatter_tokens(terms):
    count = lax.axis_size("tensor")
    blocks = terms.reshape(count, terms.shape[0] // count, terms.shape[1])
    total = blocks[0]
    for k in range(1, count):
        total = total + exchange(blocks[k].astype(BF16), "tensor", k).astype(F32)
    return total


def after(value, other):
    zero = jnp.minimum(jnp.abs(other.reshape(-1)[0].astype(F32)), 0.0)
    return value + zero.astype(value.dtype)


def gather_weights(stack, layer):
    count = lax.axis_size("dp")
    if count <= 8:
        pieces = [stack]
        for k in range(1, count):
            pieces.append(
                lax.ppermute(
                    stack,
                    ("section", "dp"),
                    [(layer * count + i, layer * count + (i ^ k if count & (count - 1) == 0 else (i + k) % count)) for i in range(count)],
                )
            )
        whole = place(pieces, "dp")
    else:
        whole = lax.all_gather(stack, "dp", axis=0)
    other = lax.ppermute(whole, "section", [(layer, 1 - layer)])
    whole = jnp.where(lax.axis_index("section") == layer, whole, other)
    whole = jnp.moveaxis(whole, 0, 1)
    return whole.reshape(whole.shape[0], -1, whole.shape[3])


def scatter_grads(parts):
    core = lax.axis_index("section")
    count = lax.axis_size("dp")
    n = parts.shape[0]
    halves = parts.reshape(n, count, 2, -1, parts.shape[2])
    kept = jnp.where(core == 0, halves[:, :, 0], halves[:, :, 1])
    given = jnp.where(core == 0, halves[:, :, 1], halves[:, :, 0]).astype(BF16)
    kept = kept + swap(given).astype(F32)
    if count <= 8:
        sent = kept.astype(BF16)
        total = lax.dynamic_index_in_dim(kept, partner("dp", 0), 1, False)
        for k in range(1, count):
            block = lax.dynamic_index_in_dim(sent, partner("dp", k), 1, False)
            total = total + exchange(block, "dp", k).astype(F32)
        return total
    return lax.psum_scatter(kept.astype(BF16), "dp", scatter_dimension=1, tiled=False).astype(F32)


def norm_parts(values):
    average = jnp.mean(values, axis=-1, keepdims=True)
    centred = values - average
    spread = jnp.mean(centred * centred, axis=-1, keepdims=True)
    scale = lax.rsqrt(spread + EPS)
    return centred * scale, scale


def norm_pull(grad, normed, scale):
    first = jnp.mean(grad, axis=-1, keepdims=True)
    second = jnp.mean(grad * normed, axis=-1, keepdims=True)
    return scale * (grad - first - normed * second)


def gelu_parts(values):
    root = math.sqrt(2.0 / math.pi)
    square = values * values
    bent = jnp.tanh(root * (values + 0.044715 * values * square))
    result = 0.5 * values * (1.0 + bent)
    slope = 0.5 * (1.0 + bent) + 0.5 * values * (1.0 - bent * bent) * root * (1.0 + 0.134145 * square)
    return result.astype(BF16), slope


def sinus_features(stamps, columns):
    halfway = columns // 2
    frequency = jnp.exp(-math.log(10000.0) * jnp.arange(halfway, dtype=F32) / halfway)
    angles = stamps.astype(F32)[:, None] * frequency[None, :]
    return jnp.concatenate([jnp.cos(angles), jnp.sin(angles)], axis=-1)


def dot(left, right, left_dim, right_dim):
    return lax.dot_general(
        left, right, (((left_dim,), (right_dim,)), ((), ())), preferred_element_type=F32
    )


def split_heads(matrix):
    return matrix.reshape(matrix.shape[0], matrix.shape[1] // HD, HD)


def attention_forward(queries, key_rows, value_rows):
    scores = jnp.einsum("qhe,khe->hqk", queries, key_rows, preferred_element_type=F32) * HD**-0.5
    largest = jnp.max(scores, axis=-1, keepdims=True)
    raised = jnp.exp(scores - largest)
    attention = raised / jnp.sum(raised, axis=-1, keepdims=True)
    rounded = attention.astype(BF16)
    mixed = jnp.einsum("hqk,khe->qhe", rounded, value_rows, preferred_element_type=F32)
    return mixed.astype(BF16), attention


def attention_backward(queries, key_rows, value_rows, attention, mixed_grad):
    weight_grad = jnp.einsum("qhe,khe->hqk", mixed_grad, value_rows, preferred_element_type=F32)
    value_grad = jnp.einsum(
        "hqk,qhe->khe", attention.astype(BF16), mixed_grad, preferred_element_type=F32
    )
    row_dot = jnp.sum(attention * weight_grad, axis=-1, keepdims=True)
    score_grad = (attention * (weight_grad - row_dot)).astype(BF16)
    query_grad = (
        jnp.einsum("hqk,khe->qhe", score_grad, key_rows, preferred_element_type=F32) * HD**-0.5
    )
    key_grad = (
        jnp.einsum("hqk,qhe->khe", score_grad, queries, preferred_element_type=F32) * HD**-0.5
    )
    return query_grad.astype(BF16), key_grad.astype(BF16), value_grad.astype(BF16)


def attend(attn_in, packed, in_bias):
    width = packed.shape[1] // 4
    projected = dot(attn_in, packed[:, : 3 * width], 1, 0)
    queries = (projected[:, :width] + in_bias[0]).astype(BF16)
    key_rows = projected[:, width : 2 * width].astype(BF16)
    value_rows = (projected[:, 2 * width :] + in_bias[1]).astype(BF16)
    heads = (split_heads(queries), split_heads(key_rows), split_heads(value_rows))
    mixed, attention = attention_forward(*heads)
    mixed = mixed.reshape(queries.shape)
    return dot(mixed, packed[:, 3 * width :], 1, 1), (heads, attention, mixed)


def attend_back(outer_grad, packed, kept):
    heads, attention, mixed = kept
    width = packed.shape[1] // 4
    mixed_grad = dot(outer_grad, packed[:, 3 * width :], 1, 0).astype(BF16)
    grads = attention_backward(*heads, attention, split_heads(mixed_grad))
    stacked = jnp.concatenate([member.reshape(mixed.shape) for member in grads], axis=1)
    return dot(stacked, packed[:, : 3 * width], 1, 1), stacked


def body(
    latents,
    cotangent,
    labels,
    timesteps,
    occupied,
    class_table,
    time_weight,
    project_in,
    project_in_bias,
    project_out,
    project_out_bias,
    up_weight,
    up_bias,
    down_weight,
    down_bias,
    modulate_weight,
    modulate_bias,
):
    core = lax.axis_index("section")
    shards = lax.axis_size("dp")
    cuts = lax.axis_size("tensor")
    micro_count = latents.shape[0]
    width = latents.shape[3]
    part = width // cuts
    rows = width // shards

    def pick(first, second):
        return jnp.where(core == 0, first, second)

    tokens_own = pick(latents[0, 0], latents[1, 0])
    seed_own = pick(
        cotangent[0, 0] * occupied[0, 0].astype(BF16), cotangent[1, 0] * occupied[1, 0].astype(BF16)
    )
    tokens_all = gather_tokens(tokens_own).astype(F32)
    seed_all = gather_tokens(seed_own).astype(F32)

    packed_own = jnp.concatenate(
        [project_in[0, :, 0], project_in[0, :, 1], project_in[0, :, 2], project_out[0].T], axis=1
    )
    first_a = gather_weights(packed_own[None], 0)[0]
    mlp_own = jnp.stack([up_weight[0], down_weight[0].T])
    first_u, first_d = gather_weights(after(mlp_own, first_a), 0)
    second_a = gather_weights(after(packed_own, first_u)[None], 1)[0]
    second_u, second_d = gather_weights(after(mlp_own, second_a), 1)
    weights = ((first_a, first_u, first_d), (second_a, second_u, second_d))

    stamps = jnp.concatenate([labels.reshape(-1), timesteps.reshape(-1)])
    if shards <= 8:
        stamps = place(gather_list(stamps, "dp"), "dp")
    else:
        stamps = lax.all_gather(stamps, "dp", axis=0)
    flat_labels = stamps[:, :micro_count].reshape(-1)
    flat_times = stamps[:, micro_count:].reshape(-1)
    class_count = class_table.shape[0]
    class_hot = flat_labels[:, None] == jnp.arange(class_count, dtype=jnp.int32)[None, :]
    time_feats = sinus_features(flat_times, time_weight.shape[0]).astype(BF16)
    condition = dot(class_hot.astype(BF16), class_table, 1, 0) + dot(time_feats, time_weight, 1, 0)
    cond_act = jax.nn.silu(condition).astype(BF16)
    act_rows = lax.dynamic_slice_in_dim(cond_act, lax.axis_index("dp") * rows, rows, 1)

    mod_weight = modulate_weight[0].reshape(rows, -1)
    mod_terms = dot(act_rows, mod_weight, 1, 0).reshape(shards, micro_count, 6, part)
    bias_cols = modulate_bias.shape[2]
    bias_full = lax.dynamic_update_slice_in_dim(
        jnp.zeros((6, part), F32), modulate_bias[0].astype(F32), lax.axis_index("dp") * bias_cols, 1
    )
    mod_terms = (mod_terms + bias_full).reshape(shards, -1)
    bias_own = jnp.concatenate(
        [
            member.astype(F32).reshape(-1)
            for member in (project_in_bias, up_bias, project_out_bias, down_bias)
        ]
    )
    mod_size = mod_terms.shape[1]
    if shards <= 8:
        mod_sum = lax.dynamic_index_in_dim(mod_terms, partner("dp", 0), 0, False)
        bias_list = [bias_own]
        for k in range(1, shards):
            block = lax.dynamic_index_in_dim(mod_terms, partner("dp", k), 0, False)
            if shards & (shards - 1) == 0:
                both = exchange(jnp.concatenate([block, bias_own]), "dp", k)
                mod_sum = mod_sum + both[:mod_size]
                bias_list.append(both[mod_size:])
            else:
                mod_sum = mod_sum + exchange(block, "dp", k)
                bias_list.append(fetch(bias_own, "dp", k))
        bias_all = place(bias_list, "dp")
    else:
        mod_sum = lax.psum_scatter(mod_terms, "dp", scatter_dimension=0, tiled=False)
        bias_all = lax.all_gather(bias_own, "dp", axis=0)
    mod_sum = mod_sum.reshape(micro_count, -1)
    half_size = mod_size // micro_count
    received = swap(jnp.concatenate([pick(mod_sum[1], mod_sum[0]), bias_all.reshape(-1)]))
    mod_kept = pick(mod_sum[0], mod_sum[1])
    mod_got = received[:half_size]
    bias_got = received[half_size:].reshape(bias_all.shape)
    mod_both = jnp.stack([pick(mod_kept, mod_got), pick(mod_got, mod_kept)]).reshape(-1, part)
    mod_all = place(gather_list(mod_both, "tensor"), "tensor")
    modulation = jnp.moveaxis(mod_all, 0, 1).reshape(2, 6, width)
    biases = []
    for member in (pick(bias_all, bias_got), pick(bias_got, bias_all)):
        cols = project_in_bias.shape[2]
        in_bias = jnp.moveaxis(member[:, : 2 * cols].reshape(shards, 2, cols), 0, 1).reshape(2, part)
        rest = member[:, 2 * cols :]
        up_len, out_len = up_bias.shape[1], project_out_bias.shape[1]
        biases.append(
            (
                in_bias,
                rest[:, :up_len].reshape(-1),
                rest[:, up_len : up_len + out_len].reshape(-1),
                rest[:, up_len + out_len :].reshape(-1),
            )
        )

    kept_layers = []
    outputs = []
    inputs = tokens_own.astype(F32)
    for layer in range(2):
        shift_one, scale_one, gate_one, shift_two, scale_two, gate_two = [
            modulation[layer, k][None] for k in range(6)
        ]
        packed, upper, lower = weights[layer]
        in_bias, upper_bias, outer_bias, lower_bias = biases[layer]
        normed_one, scale_in = norm_parts(inputs)
        if layer == 0:
            normed_all = norm_parts(tokens_all)[0]
            attn_in = (normed_all * (1.0 + scale_one) + shift_one).astype(BF16)
        else:
            normed_all = None
            attn_in = gather_tokens((normed_one * (1.0 + scale_one) + shift_one).astype(BF16))
        branch, attn_kept = attend(attn_in, packed, in_bias)
        attn_out = scatter_tokens(branch) + outer_bias
        middle = inputs + gate_one * attn_out
        normed_two, scale_mid = norm_parts(middle)
        mlp_in = gather_tokens((normed_two * (1.0 + scale_two) + shift_two).astype(BF16))
        hidden, slope = gelu_parts(dot(mlp_in, upper, 1, 0) + upper_bias)
        mlp_out = scatter_tokens(dot(hidden, lower, 1, 1)) + lower_bias
        output = middle + gate_two * mlp_out
        outputs.append(output.astype(BF16))
        kept_layers.append(
            (normed_one, scale_in, normed_all, attn_in, attn_kept, attn_out, normed_two, scale_mid, mlp_in, hidden, slope, mlp_out)
        )
        inputs = outputs[-1].astype(F32)

    grad_own = seed_own.astype(F32)
    mod_grads = [None, None]
    bias_grads = [None, None]
    shard_grads = [None, None]
    input_grads = [None, None]
    for layer in (1, 0):
        shift_one, scale_one, gate_one, shift_two, scale_two, gate_two = [
            modulation[layer, k][None] for k in range(6)
        ]
        packed, upper, lower = weights[layer]
        (normed_one, scale_in, normed_all, attn_in, attn_kept, attn_out, normed_two, scale_mid, mlp_in, hidden, slope, mlp_out) = kept_layers[layer]
        if layer == 1:
            lower_grad = (seed_all * gate_two).astype(BF16)
        else:
            lower_grad = gather_tokens((grad_own * gate_two).astype(BF16))
        pre_grad = (dot(lower_grad, lower, 1, 0) * slope).astype(BF16)
        mid_grad = scatter_tokens(dot(pre_grad, upper, 1, 1))
        d_gate_two = jnp.sum(grad_own * mlp_out, axis=0)
        d_shift_two = jnp.sum(mid_grad, axis=0)
        d_scale_two = jnp.sum(mid_grad * normed_two, axis=0)
        middle_grad = grad_own + norm_pull(mid_grad * (1.0 + scale_two), normed_two, scale_mid)
        d_gate_one = jnp.sum(middle_grad * attn_out, axis=0)
        outer_grad = gather_tokens((middle_grad * gate_one).astype(BF16))
        in_terms, stacked = attend_back(outer_grad, packed, attn_kept)
        in_grad = scatter_tokens(in_terms)
        if layer == 0:
            d_shift_one = jnp.sum(in_terms, axis=0)
            d_scale_one = jnp.sum(in_terms * normed_all, axis=0)
        else:
            d_shift_one = jnp.sum(in_grad, axis=0)
            d_scale_one = jnp.sum(in_grad * normed_one, axis=0)
        input_grad = middle_grad + norm_pull(in_grad * (1.0 + scale_one), normed_one, scale_in)
        input_grads[layer] = input_grad
        grad_own = input_grad.astype(BF16).astype(F32)
        mod_grads[layer] = jnp.stack(
            [d_shift_one, d_scale_one, d_gate_one, d_shift_two, d_scale_two, d_gate_two]
        )
        mlp_grads = jnp.stack([dot(mlp_in, pre_grad, 0, 0), dot(lower_grad, hidden, 0, 0)])
        attn_grads = jnp.concatenate(
            [dot(attn_in, stacked, 0, 0), dot(outer_grad, attn_kept[2], 0, 0)], axis=1
        )
        shard_grads[layer] = jnp.concatenate(
            [scatter_grads(mlp_grads), scatter_grads(attn_grads[None])]
        )
        d_stacked = jnp.sum(stacked.astype(F32), axis=0)
        in_bias_grad = jnp.stack([d_stacked[:part], d_stacked[2 * part :]])
        in_bias_grad = jnp.moveaxis(in_bias_grad.reshape(2, shards, -1), 1, 0).reshape(shards, -1)
        bias_grads[layer] = jnp.concatenate(
            [in_bias_grad]
            + [
                jnp.sum(member.astype(F32), axis=0).reshape(shards, -1)
                for member in (pre_grad, outer_grad, lower_grad)
            ],
            axis=1,
        )

    given = swap(pick(shard_grads[1], shard_grads[0]))
    own = pick(shard_grads[0], shard_grads[1])
    grads = jnp.concatenate([pick(own, given), pick(given, own)], axis=1)
    grad_upper, grad_lower = grads[0], grads[1].T
    grad_inner = grads[2, :, : 3 * part].reshape(rows, 3, part)
    grad_outer = grads[2, :, 3 * part :].T

    mod_part = jnp.stack(mod_grads).reshape(2 * 6, cuts, part)
    mod_part = jnp.moveaxis(mod_part, 1, 0)
    mod_shard = lax.dynamic_index_in_dim(mod_part, partner("tensor", 0), 0, False)
    for k in range(1, cuts):
        block = lax.dynamic_index_in_dim(mod_part, partner("tensor", k), 0, False)
        mod_shard = mod_shard + exchange(block, "tensor", k)
    mod_shard = mod_shard.reshape(2, 6 * part)
    bias_len = bias_grads[0].shape[1]
    received = swap(
        jnp.concatenate(
            [pick(mod_shard[1], mod_shard[0]), pick(bias_grads[1], bias_grads[0]).reshape(-1)]
        )
    )
    mod_kept = pick(mod_shard[0], mod_shard[1])
    mod_got = received[: 6 * part]
    mod_micro = jnp.concatenate([pick(mod_kept, mod_got), pick(mod_got, mod_kept)])
    bias_sum = pick(bias_grads[0], bias_grads[1]) + received[6 * part :].reshape(shards, bias_len)
    if shards <= 8 and shards & (shards - 1) == 0:
        mod_list = [mod_micro]
        bias_total = lax.dynamic_index_in_dim(bias_sum, partner("dp", 0), 0, False)
        for k in range(1, shards):
            block = lax.dynamic_index_in_dim(bias_sum, partner("dp", k), 0, False)
            both = exchange(jnp.concatenate([mod_micro, block]), "dp", k)
            mod_list.append(both[: mod_micro.shape[0]])
            bias_total = bias_total + both[mod_micro.shape[0] :]
        mod_slots = place(mod_list, "dp")
    else:
        mod_slots = lax.all_gather(mod_micro, "dp", axis=0)
        bias_total = lax.psum_scatter(bias_sum, "dp", scatter_dimension=0, tiled=False)
    mod_slots = mod_slots.reshape(shards * micro_count, 6 * part)
    grad_mod_weight = lax.dot_general(
        act_rows.astype(F32), mod_slots, (((0,), (0,)), ((), ())), precision=HIGH
    ).reshape(rows, 6, part)
    mod_bias_sum = jnp.sum(mod_slots, axis=0).reshape(6, part)
    grad_mod_bias = lax.dynamic_slice_in_dim(
        mod_bias_sum, lax.axis_index("dp") * bias_cols, bias_cols, 1
    )
    act_grad = lax.dot_general(
        mod_slots, mod_weight.astype(F32), (((1,), (1,)), ((), ())), precision=HIGH
    )
    act_grad = act_grad + swap(act_grad)
    act_grad = sum(gather_list(act_grad, "tensor"))
    if shards <= 8:
        act_all = place(gather_list(act_grad, "dp"), "dp")
    else:
        act_all = lax.all_gather(act_grad, "dp", axis=0)
    act_all = jnp.moveaxis(act_all, 0, 1).reshape(-1, width)
    cond_grad = jax.vjp(jax.nn.silu, condition)[1](act_all)[0]
    table_grad = lax.dot_general(
        class_hot.astype(F32), cond_grad, (((0,), (0,)), ((), ())), precision=HIGH
    )
    time_grad = lax.dot_general(
        time_feats.astype(F32), cond_grad, (((0,), (0,)), ((), ())), precision=HIGH
    )
    cols = project_in_bias.shape[2]
    up_len, out_len = up_bias.shape[1], project_out_bias.shape[1]
    grad_in_bias = bias_total[: 2 * cols].reshape(2, cols)
    rest = bias_total[2 * cols :]

    def by_micro(first, second):
        got = swap(pick(second, first))
        held = pick(first, second)
        return jnp.stack([pick(held, got), pick(got, held)])[None, :, None]

    return (
        by_micro(outputs[0], outputs[1]),
        by_micro(input_grads[0], input_grads[1]),
        table_grad,
        time_grad,
        grad_inner[None],
        grad_in_bias[None],
        grad_outer[None],
        rest[up_len : up_len + out_len][None],
        grad_upper[None],
        rest[:up_len][None],
        grad_lower[None],
        rest[up_len + out_len :][None],
        grad_mod_weight[None],
        grad_mod_bias[None],
    )


def solution(mesh):
    in_specs = (
        P(None, "dp", "tensor", None),
        P(None, "dp", "tensor", None),
        P(None, "dp"),
        P(None, "dp"),
        P(None, "dp"),
        P(),
        P(),
        P("section", "dp", None, "tensor"),
        P("section", None, ("tensor", "dp")),
        P("section", "tensor", "dp"),
        P("section", "dp"),
        P("section", "dp", "tensor"),
        P("section", ("tensor", "dp")),
        P("section", "tensor", "dp"),
        P("section", "dp"),
        P("section", "dp", None, "tensor"),
        P("section", None, ("tensor", "dp")),
    )
    out_specs = (
        P("section", None, "dp", "tensor", None),
        P("section", None, "dp", "tensor", None),
        P(),
        P(),
        P("section", "dp", None, "tensor"),
        P("section", None, ("tensor", "dp")),
        P("section", "tensor", "dp"),
        P("section", "dp"),
        P("section", "dp", "tensor"),
        P("section", ("tensor", "dp")),
        P("section", "tensor", "dp"),
        P("section", "dp"),
        P("section", "dp", None, "tensor"),
        P("section", None, ("tensor", "dp")),
    )
    return jax.shard_map(body, mesh=mesh, in_specs=in_specs, out_specs=out_specs, check_vma=False)
```

time: 1060 us -> 512 us (0.48)
  waiting for transfers between devices: 521 us -> 91 us
  blocking collectives: 281 us -> 0 us
  starting transfers between devices: 7.21 us -> 173 us
  local copies, waits for them, and re-layouts: 48.7 us -> 95.9 us
  other arithmetic: 104 us -> 75.1 us
  between operations: 19.6 us -> 6.41 us
    reduce_scatter x16 -> x0, waiting for transfers between devices: 307 us -> none  [the longest x6 115 us: sum_normed(): return lax.psum_scatter(terms, 'tensor', scatter_dimension=1, tiled=True)]
    all_gather x19 -> x0, blocking collectives: 241 us -> none  [the longest x6 60.6 us: gather_grads(): return lax.all_gather(rows, 'tensor', axis=1, tiled=True)]
    ppermute x4 -> x107, starting transfers between devices: 6.01 us -> 173 us  [the longest x45 74.8 us: exchange(): return lax.ppermute(value, axis, [(i, i ^ k) for i in range(size)])]
    psum x1 -> x0, waiting for transfers between devices: 145 us -> none  [body(): lax.psum((table_part, time_part), ('section', 'tensor', 'dp'))]
    ppermute x4 -> x107, waiting for transfers between devices: 2.78 us -> 91 us  [the longest x45 60.5 us: exchange(): return lax.ppermute(value, axis, [(i, i ^ k) for i in range(size)])]
    all_gather x3 -> x0, waiting for transfers between devices: 48.1 us -> none  [the longest x1 28.3 us: fetch_weights(): lax.all_gather(pieces[6], 'dp', axis=1, tiled=True)]
    unnamed x2 -> x0, blocking collectives: 25.2 us -> none
    reduce_sum x40 -> x24, other arithmetic: 46 us -> 23.3 us  [the longest x5 4.49 us: norm_parts(): average = jnp.mean(values, axis=-1, keepdims=True)]
  transfers between devices with their start and end apart: 27 -> 107, of which waited for: 22 -> 31; matrix products, arithmetic and copies ran while one was open for 11% -> 40% of each run, Pallas kernels for 0% -> 0%
where the time goes in v1:
time: 512 us; the launch traced here: 503 us
  starting transfers between devices  173 us (34%)
  local copies, waits for them, and re-layouts  95.9 us (19%)
  waiting for transfers between devices  91 us (18%)
  other arithmetic  75.1 us (15%)
  matrix products  60.8 us (12%)
  between operations  6.41 us (1%)
    ppermute x45, starting transfers between devices, exchange(): return lax.ppermute(value, axis, [(i, i ^ k) for i in range(size)])  74.8 us
    ppermute x45, waiting for transfers between devices, exchange(): return lax.ppermute(value, axis, [(i, i ^ k) for i in range(size)])  60.5 us
    ppermute x36, starting transfers between devices, fetch(): return lax.ppermute(value, axis, [(i, i ^ k) for i in range(size)])  47.7 us
    dot_general x27, matrix products, dot(): lax.dot_general(left, right, (((left_dim,), (right_dim,)), ((), ())), pre...  36.1 us
    ppermute x12, starting transfers between devices, gather_weights(): lax.ppermute(stack, ('section', 'dp'), [(layer * count + i, layer * count...  25.2 us
    ppermute x12, waiting for transfers between devices, gather_weights(): lax.ppermute(stack, ('section', 'dp'), [(layer * count + i, layer * count...  18.7 us
    ppermute x10, starting transfers between devices, swap(): return lax.ppermute(value, 'section', [(0, 1), (1, 0)])  18.5 us
    unnamed x392, local copies, waits for them, and re-layouts  15.9 us
  transfers between devices with their start and end apart: 107, of which 31 were waited for; matrix products, arithmetic and copies ran while one was open for 40% of the time, Pallas kernels for 0%

profile of v1, /device:TPU:0, one launch (start us, length us, event | category | flops | bytes accessed | tf_op | source)
XLA Modules:
  0.0 502.7 jit_solution(16716948985088226828)
XLA Ops:
  13.8 5.4 %collective-permute-start.14 = (bf16[1,192,768]{2,1,0:T(8,128)(2,1)}, bf16[1,192,768]{2,1,0:T(8,128)(2,1)}, u32[]{:S(2)}, u32[]{:S(2)}) collective-permute-start(bf16[1,192,768]{2,1,0:T(8,128)(2,1)} %fusion.152), channel_id=1, source_target_pairs={{0,2},{1,3},{2,0},{3,1},{4,6},{5,7},{6,4},{7,5},{8,10},{9,11},{10,... | collective-permute-start | bytes 884744 | tf_op jit(solution)/shard_map/ppermute | solution.py:76
  26.6 3.8 collective-permute-start.5
  38.3 3.5 collective-permute-done.15
  65.0 5.4 %collective-permute-start.25 = (bf16[2,192,768]{2,1,0:T(8,128)(2,1)S(1)}, bf16[2,192,768]{2,1,0:T(8,128)(2,1)S(1)}, u32[]{:S(2)}, u32[]{:S(2)}) collective-permute-start(bf16[2,192,768]{2,1,0:T(8,128)(2,1)S(1)} %fusion.51), channel_id=1, source_target_pairs={{0,3},{1,2},{2,1},{3,0},{4,7},{5,6},{6,5},{7,4},{8,11},{9,10},{10,... | collective-permute-start | bytes 1769480 | tf_op jit(solution)/shard_map/ppermute | solution.py:76
  72.2 3.2 collective-permute-done.23
  75.5 12.0 %collective-permute-done.24 = bf16[2,192,768]{2,1,0:T(8,128)(2,1)S(1)} collective-permute-done((bf16[2,192,768]{2,1,0:T(8,128)(2,1)S(1)}, bf16[2,192,768]{2,1,0:T(8,128)(2,1)S(1)}, u32[]{:S(2)}, u32[]{:S(2)}) %collective-permute-start.24) | collective-permute-done | bytes 589856 | tf_op jit(solution)/shard_map/ppermute | solution.py:76
  87.6 3.1 collective-permute-start.26
  181.2 4.7 collective-permute-done.46
  202.5 16.5 %collective-permute-start.50 = (bf16[64,768]{1,0:T(8,128)(2,1)S(1)}, bf16[64,768]{1,0:T(8,128)(2,1)S(1)}, u32[]{:S(2)}, u32[]{:S(2)}) collective-permute-start(bf16[64,768]{1,0:T(8,128)(2,1)S(1)} %get-tuple-element.134), channel_id=1, source_target_pairs={{0,16},{16,0},{1,17},{17,1},{2,18},{18,2},{3,19},{19,3},{4,20},{20... | collective-permute-start | bytes 294920 | tf_op jit(solution)/shard_map/ppermute | solution.py:38
  263.1 3.3 copy.218
  287.7 3.0 convert_reduce_fusion.3
  296.3 3.2 fusion.170
  311.7 3.1 fusion.14
  338.1 3.1 copy.210
  346.5 6.9 %collective-permute-start.80 = (f32[2976]{0:T(1024)S(1)}, f32[2976]{0:T(1024)S(1)}, u32[]{:S(2)}, u32[]{:S(2)}) collective-permute-start(f32[2976]{0:T(1024)S(1)} %get-tuple-element.217), channel_id=1, source_target_pairs={{0,1},{1,0},{2,3},{3,2},{4,5},{5,4},{6,7},{7,6},{8,9},{9,8},{10,11... | collective-permute-start | bytes 35720 | tf_op jit(solution)/shard_map/ppermute | solution.py:26
  377.4 3.2 fusion.125
  387.8 4.0 collective-permute-done.105
  391.8 4.6 collective-permute-start.103
  398.6 3.1 collective-permute-done.103
  401.9 3.2 fusion.179
  410.3 3.3 fusion.180
  436.6 11.3 %collective-permute-start.91 = (bf16[2,96,768]{1,2,0:T(8,128)(2,1)}, bf16[2,96,768]{1,2,0:T(8,128)(2,1)}, u32[]{:S(2)}, u32[]{:S(2)}) collective-permute-start(bf16[2,96,768]{1,2,0:T(8,128)(2,1)} %bitcast.477), channel_id=1, source_target_pairs={{0,1},{1,0},{2,3},{3,2},{4,5},{5,4},{6,7},{7,6},{8,9},{9,8},{10,11... | collective-permute-start | bytes 884744 | tf_op jit(solution)/shard_map/ppermute | solution.py:26
  448.3 23.2 %collective-permute-done.100 = bf16[2,96,768]{1,2,0:T(8,128)(2,1)} collective-permute-done((bf16[2,96,768]{1,2,0:T(8,128)(2,1)}, bf16[2,96,768]{1,2,0:T(8,128)(2,1)}, u32[]{:S(2)}, u32[]{:S(2)}) %collective-permute-start.100) | collective-permute-done | bytes 294944 | tf_op jit(solution)/shard_map/ppermute | solution.py:26
  472.8 15.1 %collective-permute-done.92 = bf16[2,96,768]{1,2,0:T(8,128)(2,1)} collective-permute-done((bf16[2,96,768]{1,2,0:T(8,128)(2,1)}, bf16[2,96,768]{1,2,0:T(8,128)(2,1)}, u32[]{:S(2)}, u32[]{:S(2)}) %collective-permute-start.92) | collective-permute-done | bytes 294944 | tf_op jit(solution)/shard_map/ppermute | solution.py:26
  (929 shorter events, 345.2 us)
Async XLA Ops:
  1.6 20.3 %collective-permute-start = (s32[4]{0:T(128)S(1)}, s32[4]{0:T(128)S(1)}, u32[]{:S(2)}, u32[]{:S(2)}) collective-permute-start(s32[4]{0:T(128)S(1)} %pad_add_fusion), channel_id=1, source_target_pairs={{0,1},{1,0},{2,3},{3,2},{4,5},{5,4},{6,7},{7,6},{8,9},{9,8},{10,11... | collective-permute-start | bytes 56 | tf_op jit(solution)/shard_map/ppermute | solution.py:33
  11.0 25.3 %collective-permute-start.13 = (bf16[1,192,768]{2,1,0:T(8,128)(2,1)}, bf16[1,192,768]{2,1,0:T(8,128)(2,1)}, u32[]{:S(2)}, u32[]{:S(2)}) collective-permute-start(bf16[1,192,768]{2,1,0:T(8,128)(2,1)} %fusion.152), channel_id=1, source_target_pairs={{0,1},{1,0},{2,3},{3,2},{4,5},{5,4},{6,7},{7,6},{8,9},{9,8},{10,11... | collective-permute-start | bytes 884744 | tf_op jit(solution)/shard_map/ppermute | solution.py:76
  13.8 23.5 %collective-permute-start.14 = (bf16[1,192,768]{2,1,0:T(8,128)(2,1)}, bf16[1,192,768]{2,1,0:T(8,128)(2,1)}, u32[]{:S(2)}, u32[]{:S(2)}) collective-permute-start(bf16[1,192,768]{2,1,0:T(8,128)(2,1)} %fusion.152), channel_id=1, source_target_pairs={{0,2},{1,3},{2,0},{3,1},{4,6},{5,7},{6,4},{7,5},{8,10},{9,11},{10,... | collective-permute-start | bytes 884744 | tf_op jit(solution)/shard_map/ppermute | solution.py:76
  33.1 20.3 %collective-permute-start.12 = (bf16[64,768]{1,0:T(8,128)(2,1)S(1)}, bf16[64,768]{1,0:T(8,128)(2,1)S(1)}, u32[]{:S(2)}, u32[]{:S(2)}) collective-permute-start(bf16[64,768]{1,0:T(8,128)(2,1)S(1)} %get-tuple-element.130), channel_id=1, source_target_pairs={{0,12},{4,8},{8,4},{12,0},{1,13},{5,9},{9,5},{13,1},{2,14},{6,10},... | collective-permute-start | bytes 294920 | tf_op jit(solution)/shard_map/ppermute | solution.py:33
  62.1 25.4 %collective-permute-start.24 = (bf16[2,192,768]{2,1,0:T(8,128)(2,1)S(1)}, bf16[2,192,768]{2,1,0:T(8,128)(2,1)S(1)}, u32[]{:S(2)}, u32[]{:S(2)}) collective-permute-start(bf16[2,192,768]{2,1,0:T(8,128)(2,1)S(1)} %fusion.51), channel_id=1, source_target_pairs={{0,2},{1,3},{2,0},{3,1},{4,6},{5,7},{6,4},{7,5},{8,10},{9,11},{10,... | collective-permute-start | bytes 1769480 | tf_op jit(solution)/shard_map/ppermute | solution.py:76
  65.0 22.6 %collective-permute-start.25 = (bf16[2,192,768]{2,1,0:T(8,128)(2,1)S(1)}, bf16[2,192,768]{2,1,0:T(8,128)(2,1)S(1)}, u32[]{:S(2)}, u32[]{:S(2)}) collective-permute-start(bf16[2,192,768]{2,1,0:T(8,128)(2,1)S(1)} %fusion.51), channel_id=1, source_target_pairs={{0,3},{1,2},{2,1},{3,0},{4,7},{5,6},{6,5},{7,4},{8,11},{9,10},{10,... | collective-permute-start | bytes 1769480 | tf_op jit(solution)/shard_map/ppermute | solution.py:76
  87.6 25.2 %collective-permute-start.26 = (bf16[4,2,192,768]{3,2,1,0:T(8,128)(2,1)S(1)}, bf16[4,2,192,768]{3,2,1,0:T(8,128)(2,1)}, u32[]{:S(2)}, u32[]{:S(2)}) collective-permute-start(bf16[4,2,192,768]{3,2,1,0:T(8,128)(2,1)S(1)} %bitcast_dynamic-update-slice_fusion.3), channel_id=1, source_target_pairs={{0,16},{1,17},{2,18},{3,19},{4,20},{5,21},{6,22},{7,23},{8,24},{9,... | collective-permute-start | bytes 7077896 | tf_op jit(solution)/shard_map/ppermute | solution.py:85
  155.9 29.9 %collective-permute-start.46 = (bf16[4,2,192,768]{3,2,1,0:T(8,128)(2,1)S(1)}, bf16[4,2,192,768]{3,2,1,0:T(8,128)(2,1)}, u32[]{:S(2)}, u32[]{:S(2)}) collective-permute-start(bf16[4,2,192,768]{3,2,1,0:T(8,128)(2,1)S(1)} %bitcast_dynamic-update-slice_fusion), channel_id=1, source_target_pairs={{16,0},{17,1},{18,2},{19,3},{20,4},{21,5},{22,6},{23,7},{24,8},{25... | collective-permute-start | bytes 7077896 | tf_op jit(solution)/shard_map/ppermute | solution.py:85
  198.8 20.8 %collective-permute-start.53 = (bf16[64,768]{1,0:T(8,128)(2,1)S(1)}, bf16[64,768]{1,0:T(8,128)(2,1)S(1)}, u32[]{:S(2)}, u32[]{:S(2)}) collective-permute-start(bf16[64,768]{1,0:T(8,128)(2,1)S(1)} %get-tuple-element.123), channel_id=1, source_target_pairs={{0,12},{4,8},{8,4},{12,0},{1,13},{5,9},{9,5},{13,1},{2,14},{6,10},... | collective-permute-start | bytes 294920 | tf_op jit(solution)/shard_map/ppermute | solution.py:33
  200.3 19.3 %collective-permute-start.52 = (bf16[64,768]{1,0:T(8,128)(2,1)S(1)}, bf16[64,768]{1,0:T(8,128)(2,1)S(1)}, u32[]{:S(2)}, u32[]{:S(2)}) collective-permute-start(bf16[64,768]{1,0:T(8,128)(2,1)S(1)} %get-tuple-element.123), channel_id=1, source_target_pairs={{0,8},{4,12},{8,0},{12,4},{1,9},{5,13},{9,1},{13,5},{2,10},{6,14},... | collective-permute-start | bytes 294920 | tf_op jit(solution)/shard_map/ppermute | solution.py:33
  202.5 28.7 %collective-permute-start.50 = (bf16[64,768]{1,0:T(8,128)(2,1)S(1)}, bf16[64,768]{1,0:T(8,128)(2,1)S(1)}, u32[]{:S(2)}, u32[]{:S(2)}) collective-permute-start(bf16[64,768]{1,0:T(8,128)(2,1)S(1)} %get-tuple-element.134), channel_id=1, source_target_pairs={{0,16},{16,0},{1,17},{17,1},{2,18},{18,2},{3,19},{19,3},{4,20},{20... | collective-permute-start | bytes 294920 | tf_op jit(solution)/shard_map/ppermute | solution.py:38
  230.1 180.3 %collective-permute-start.98 = (bf16[2,4,96,768]{3,2,1,0:T(8,128)(2,1)}, bf16[2,4,96,768]{3,2,1,0:T(8,128)(2,1)}, u32[]{:S(2)}, u32[]{:S(2)}) collective-permute-start(bf16[2,4,96,768]{3,2,1,0:T(8,128)(2,1)} %fusion.15), channel_id=1, source_target_pairs={{0,16},{16,0},{1,17},{17,1},{2,18},{18,2},{3,19},{19,3},{4,20},{20... | collective-permute-start | bytes 3538952 | tf_op jit(solution)/shard_map/ppermute | solution.py:38
  283.7 96.9 %collective-permute-start.102 = (bf16[1,4,96,768]{3,2,1,0:T(8,128)(2,1)}, bf16[1,4,96,768]{3,2,1,0:T(8,128)(2,1)}, u32[]{:S(2)}, u32[]{:S(2)}) collective-permute-start(bf16[1,4,96,768]{3,2,1,0:T(8,128)(2,1)} %fusion.47), channel_id=1, source_target_pairs={{0,16},{16,0},{1,17},{17,1},{2,18},{18,2},{3,19},{19,3},{4,20},{20... | collective-permute-start | bytes 1769480 | tf_op jit(solution)/shard_map/ppermute | solution.py:38
  373.6 40.0 %collective-permute-start.90 = (bf16[2,4,96,768]{3,2,1,0:T(8,128)(2,1)}, bf16[2,4,96,768]{3,2,1,0:T(8,128)(2,1)}, u32[]{:S(2)}, u32[]{:S(2)}) collective-permute-start(bf16[2,4,96,768]{3,2,1,0:T(8,128)(2,1)} %fusion.14), channel_id=1, source_target_pairs={{0,16},{16,0},{1,17},{17,1},{2,18},{18,2},{3,19},{19,3},{4,20},{20... | collective-permute-start | bytes 3538952 | tf_op jit(solution)/shard_map/ppermute | solution.py:38
  383.1 18.8 %collective-permute-start.94 = (bf16[1,4,96,768]{3,2,1,0:T(8,128)(2,1)}, bf16[1,4,96,768]{3,2,1,0:T(8,128)(2,1)}, u32[]{:S(2)}, u32[]{:S(2)}) collective-permute-start(bf16[1,4,96,768]{3,2,1,0:T(8,128)(2,1)} %fusion.46), channel_id=1, source_target_pairs={{0,16},{16,0},{1,17},{17,1},{2,18},{18,2},{3,19},{19,3},{4,20},{20... | collective-permute-start | bytes 1769480 | tf_op jit(solution)/shard_map/ppermute | solution.py:38
  405.9 19.4 %collective-permute-start.97 = (bf16[1,96,768]{2,1,0:T(8,128)(2,1)}, bf16[1,96,768]{2,1,0:T(8,128)(2,1)}, u32[]{:S(2)}, u32[]{:S(2)}) collective-permute-start(bf16[1,96,768]{2,1,0:T(8,128)(2,1)} %get-tuple-element.158), channel_id=1, source_target_pairs={{0,3},{1,2},{2,1},{3,0},{4,7},{5,6},{6,5},{7,4},{8,11},{9,10},{10,... | collective-permute-start | bytes 442376 | tf_op jit(solution)/shard_map/ppermute | solution.py:26
  407.8 20.0 %collective-permute-start.96 = (bf16[1,96,768]{2,1,0:T(8,128)(2,1)}, bf16[1,96,768]{2,1,0:T(8,128)(2,1)}, u32[]{:S(2)}, u32[]{:S(2)}) collective-permute-start(bf16[1,96,768]{2,1,0:T(8,128)(2,1)} %get-tuple-element.159), channel_id=1, source_target_pairs={{0,2},{1,3},{2,0},{3,1},{4,6},{5,7},{6,4},{7,5},{8,10},{9,11},{10,... | collective-permute-start | bytes 442376 | tf_op jit(solution)/shard_map/ppermute | solution.py:26
  407.8 20.0 %collective-permute-start.95 = (bf16[1,96,768]{2,1,0:T(8,128)(2,1)}, bf16[1,96,768]{2,1,0:T(8,128)(2,1)}, u32[]{:S(2)}, u32[]{:S(2)}) collective-permute-start(bf16[1,96,768]{2,1,0:T(8,128)(2,1)} %get-tuple-element.157), channel_id=1, source_target_pairs={{0,1},{1,0},{2,3},{3,2},{4,5},{5,4},{6,7},{7,6},{8,9},{9,8},{10,11... | collective-permute-start | bytes 442376 | tf_op jit(solution)/shard_map/ppermute | solution.py:26
  417.4 19.2 %collective-permute-start.101 = (bf16[2,96,768]{1,2,0:T(8,128)(2,1)}, bf16[2,96,768]{1,2,0:T(8,128)(2,1)}, u32[]{:S(2)}, u32[]{:S(2)}) collective-permute-start(bf16[2,96,768]{1,2,0:T(8,128)(2,1)} %bitcast.474), channel_id=1, source_target_pairs={{0,3},{1,2},{2,1},{3,0},{4,7},{5,6},{6,5},{7,4},{8,11},{9,10},{10,... | collective-permute-start | bytes 884744 | tf_op jit(solution)/shard_map/ppermute | solution.py:26
  423.4 48.0 %collective-permute-start.100 = (bf16[2,96,768]{1,2,0:T(8,128)(2,1)}, bf16[2,96,768]{1,2,0:T(8,128)(2,1)}, u32[]{:S(2)}, u32[]{:S(2)}) collective-permute-start(bf16[2,96,768]{1,2,0:T(8,128)(2,1)} %bitcast.142), channel_id=1, source_target_pairs={{0,2},{1,3},{2,0},{3,1},{4,6},{5,7},{6,4},{7,5},{8,10},{9,11},{10,... | collective-permute-start | bytes 884744 | tf_op jit(solution)/shard_map/ppermute | solution.py:26
  425.3 46.1 %collective-permute-start.99 = (bf16[2,96,768]{1,2,0:T(8,128)(2,1)}, bf16[2,96,768]{1,2,0:T(8,128)(2,1)}, u32[]{:S(2)}, u32[]{:S(2)}) collective-permute-start(bf16[2,96,768]{1,2,0:T(8,128)(2,1)} %bitcast.141), channel_id=1, source_target_pairs={{0,1},{1,0},{2,3},{3,2},{4,5},{5,4},{6,7},{7,6},{8,9},{9,8},{10,11... | collective-permute-start | bytes 884744 | tf_op jit(solution)/shard_map/ppermute | solution.py:26
  431.9 40.9 %collective-permute-start.93 = (bf16[2,96,768]{1,2,0:T(8,128)(2,1)}, bf16[2,96,768]{1,2,0:T(8,128)(2,1)}, u32[]{:S(2)}, u32[]{:S(2)}) collective-permute-start(bf16[2,96,768]{1,2,0:T(8,128)(2,1)} %bitcast.475), channel_id=1, source_target_pairs={{0,3},{1,2},{2,1},{3,0},{4,7},{5,6},{6,5},{7,4},{8,11},{9,10},{10,... | collective-permute-start | bytes 884744 | tf_op jit(solution)/shard_map/ppermute | solution.py:26
  435.7 52.3 %collective-permute-start.92 = (bf16[2,96,768]{1,2,0:T(8,128)(2,1)}, bf16[2,96,768]{1,2,0:T(8,128)(2,1)}, u32[]{:S(2)}, u32[]{:S(2)}) collective-permute-start(bf16[2,96,768]{1,2,0:T(8,128)(2,1)} %bitcast.476), channel_id=1, source_target_pairs={{0,2},{1,3},{2,0},{3,1},{4,6},{5,7},{6,4},{7,5},{8,10},{9,11},{10,... | collective-permute-start | bytes 884744 | tf_op jit(solution)/shard_map/ppermute | solution.py:26
  436.6 51.3 %collective-permute-start.91 = (bf16[2,96,768]{1,2,0:T(8,128)(2,1)}, bf16[2,96,768]{1,2,0:T(8,128)(2,1)}, u32[]{:S(2)}, u32[]{:S(2)}) collective-permute-start(bf16[2,96,768]{1,2,0:T(8,128)(2,1)} %bitcast.477), channel_id=1, source_target_pairs={{0,1},{1,0},{2,3},{3,2},{4,5},{5,4},{6,7},{7,6},{8,9},{9,8},{10,11... | collective-permute-start | bytes 884744 | tf_op jit(solution)/shard_map/ppermute | solution.py:26
  (275 other events, 1905.8 us)

commit v2 on v1

v2 whole, which is shorter than its diff:
```python
import math
from types import SimpleNamespace as Named

import jax
import jax.numpy as jnp
from jax import lax
from jax.experimental import pallas as pl
from jax.experimental.pallas import tpu as pltpu
from jax.sharding import PartitionSpec as P

HD = 64
EPS = 1e-06
HIGH = lax.Precision.HIGHEST
F32 = jnp.float32
BF16 = jnp.bfloat16
SECTION, TENSOR, SLOTS = "section", "tensor", "dp"
ROWS = (SLOTS, SECTION)
SPACE = 40 * 1024 * 1024


def cyclic(axis):
    size = lax.axis_size(axis)
    return size & (size - 1) != 0


def exchange(value, axis, k):
    size = lax.axis_size(axis)
    if cyclic(axis):
        return lax.ppermute(value, axis, [(i, (i - k) % size) for i in range(size)])
    return lax.ppermute(value, axis, [(i, i ^ k) for i in range(size)])


def fetch(value, axis, k):
    size = lax.axis_size(axis)
    if cyclic(axis):
        return lax.ppermute(value, axis, [(i, (i + k) % size) for i in range(size)])
    return lax.ppermute(value, axis, [(i, i ^ k) for i in range(size)])


def partner(axis, k):
    here = lax.axis_index(axis)
    if cyclic(axis):
        return (here - k) % lax.axis_size(axis)
    return here ^ k


def swap(value):
    return lax.ppermute(value, SECTION, [(0, 1), (1, 0)])


def gather_list(value, axis):
    return [value] + [fetch(value, axis, k) for k in range(1, lax.axis_size(axis))]


def exchange_list(values, axis):
    return [values[0]] + [exchange(values[k], axis, k) for k in range(1, lax.axis_size(axis))]


def place(pieces, axis):
    out = jnp.zeros((len(pieces),) + pieces[0].shape, pieces[0].dtype)
    for k, piece in enumerate(pieces):
        out = lax.dynamic_update_index_in_dim(out, piece, partner(axis, k), 0)
    return out


def shaped(shape, dtype):
    return jax.ShapeDtypeStruct(shape, dtype)


class Part:
    def __init__(self, value, at=None):
        self.value, self.at = value, at
        self.shape, self.dtype = value.shape, value.dtype


def run(kernel, outs, *args, flops=0, wait=()):
    def leafy(value):
        return isinstance(value, Part)

    names = list(vars(outs))
    out_flat, out_tree = jax.tree.flatten([vars(outs)[name] for name in names])
    flat, tree = jax.tree.flatten(args, is_leaf=leafy)
    moved = sum(math.prod(leaf.shape) * leaf.dtype.itemsize for leaf in flat + out_flat)

    def inner(*refs):
        ins = list(refs[: len(flat)])
        for k, leaf in enumerate(flat):
            if leafy(leaf) and leaf.at is not None:
                ins[k] = Named(ref=ins[k], at=leaf.at)
        results = jax.tree.unflatten(out_tree, refs[len(flat) + len(wait) :])
        kernel(*jax.tree.unflatten(tree, ins), Named(**dict(zip(names, results))))

    result = pl.pallas_call(
        inner,
        out_shape=out_flat,
        in_specs=[
            pl.BlockSpec(memory_space=pltpu.SMEM if leaf.dtype == jnp.int32 else pltpu.VMEM)
            for leaf in flat
        ]
        + [pl.BlockSpec(memory_space=pl.ANY)] * len(wait),
        out_specs=[pl.BlockSpec(memory_space=pltpu.VMEM)] * len(out_flat),
        compiler_params=pltpu.CompilerParams(vmem_limit_bytes=SPACE),
        cost_estimate=pl.CostEstimate(flops=flops, bytes_accessed=moved, transcendentals=0),
    )(*[leaf.value if leafy(leaf) else leaf for leaf in flat], *wait)
    return Named(**dict(zip(names, jax.tree.unflatten(out_tree, result))))


def matrix(ref):
    if isinstance(ref, Named):
        value = ref.ref[:, ref.at]
        return value.reshape(-1, value.shape[-1])
    return ref[...]


def norm_parts(values):
    average = jnp.mean(values, axis=-1, keepdims=True)
    centred = values - average
    spread = jnp.mean(centred * centred, axis=-1, keepdims=True)
    scale = lax.rsqrt(spread + EPS)
    return centred * scale, scale


def norm_pull(grad, normed, scale):
    first = jnp.mean(grad, axis=-1, keepdims=True)
    second = jnp.mean(grad * normed, axis=-1, keepdims=True)
    return scale * (grad - first - normed * second)


def dot(left, right, left_dim, right_dim):
    return lax.dot_general(
        left, right, (((left_dim,), (right_dim,)), ((), ())), preferred_element_type=F32
    )


def joined(refs):
    return jnp.concatenate([ref[...] for ref in refs], axis=0)


def summed(refs):
    total = refs[0][...].astype(F32)
    for ref in refs[1:]:
        total = total + ref[...].astype(F32)
    return total


def spread_out(terms, refs):
    rows = refs[0].shape[0]
    for k, ref in enumerate(refs):
        ref[...] = terms[k * rows : (k + 1) * rows].astype(ref.dtype)


def column_sum(values):
    return jnp.sum(values.astype(F32), axis=0, keepdims=True)


def softmax_parts(query, key):
    scores = dot(query, key, 1, 1) * HD**-0.5
    raised = jnp.exp(scores - jnp.max(scores, axis=-1, keepdims=True))
    return raised / jnp.sum(raised, axis=-1, keepdims=True)


def assemble(spot, pieces, ref):
    own, other = pieces
    rows = own[0].shape[0]
    for k, piece in enumerate(own):
        for half, block in ((spot[0], piece[...]), (1 - spot[0], other[k])):
            at = pl.multiple_of((2 * spot[3 + k] + half) * rows, rows)
            ref[pl.ds(at, rows), :] = block


def attend(first, mods, packed, in_bias, refs, layer):
    width = packed.shape[1] // 4
    attn_in = joined(first)
    if layer == 0:
        refs.kept[:, 2 * packed.shape[1] :] = attn_in
        normed = norm_parts(attn_in.astype(F32))[0]
        attn_in = (normed * (1.0 + mods[1:2]) + mods[0:1]).astype(BF16)
    refs.kept[:, : packed.shape[1]] = attn_in
    projected = dot(attn_in, packed[:, : 3 * width], 1, 0)
    queries = (projected[:, :width] + in_bias[0:1]).astype(BF16)
    keys = projected[:, width : 2 * width].astype(BF16)
    values = (projected[:, 2 * width :] + in_bias[1:2]).astype(BF16)
    mixed = []
    for at in range(0, width, HD):
        attention = softmax_parts(queries[:, at : at + HD], keys[:, at : at + HD])
        mixed.append(dot(attention.astype(BF16), values[:, at : at + HD], 1, 0))
    mixed = jnp.concatenate(mixed, axis=1).astype(BF16)
    refs.kept[:, packed.shape[1] : 2 * packed.shape[1]] = jnp.concatenate(
        [queries, keys, values, mixed], axis=1
    )
    spread_out(dot(mixed, packed[:, 3 * width :], 1, 1), refs.terms)


def attend_kernel(layer):
    def kernel(spot, first, mods_ref, packed_ref, bias_ref, refs):
        if isinstance(packed_ref, tuple):
            assemble(spot, packed_ref, refs.packed)
            packed_ref = refs.packed
        attend(first, mods_ref[6 * layer : 6 * layer + 6], matrix(packed_ref), bias_ref[...], refs, layer)

    return kernel


def middle_kernel(layer):
    def kernel(terms, inputs, mods_ref, bias_ref, refs):
        mods = mods_ref[6 * layer : 6 * layer + 6]
        attn_out = summed(terms) + bias_ref[2:3]
        rows = attn_out.shape[0]
        refs.kept[:rows] = attn_out
        middle = inputs[...].astype(F32) + mods[2:3] * attn_out
        refs.kept[rows:] = middle
        normed = norm_parts(middle)[0]
        refs.mlp_in[...] = (normed * (1.0 + mods[4:5]) + mods[3:4]).astype(BF16)

    return kernel


def mlp_kernel(pieces, upper, lower, bias_ref, refs):
    mlp_in = joined(pieces)
    size = upper.ref.shape[-1] if isinstance(upper, Named) else upper.shape[-1]
    wide = mlp_in.shape[1]
    refs.kept[:, :wide] = mlp_in
    values = dot(mlp_in, matrix(upper), 1, 0) + bias_ref[1:2]
    root = math.sqrt(2.0 / math.pi)
    square = values * values
    bent = jnp.tanh(root * (values + 0.044715 * values * square))
    hidden = (0.5 * values * (1.0 + bent)).astype(BF16)
    refs.kept[:, wide : wide + size] = hidden
    slope = 0.5 * (1.0 + bent) + 0.5 * values * (1.0 - bent * bent) * root * (
        1.0 + 0.134145 * square
    )
    refs.kept[:, wide + size :] = slope.astype(BF16)
    spread_out(dot(hidden, matrix(lower), 1, 1), refs.terms)


def last_kernel(layer):
    def kernel(terms, kept, mods_ref, bias_ref, refs):
        mlp_out = summed(terms) + bias_ref[3:4]
        refs.mlp_out[...] = mlp_out
        output = (kept[kept.shape[0] // 2 :] + mods_ref[6 * layer + 5 : 6 * layer + 6] * mlp_out).astype(BF16)
        refs.output[...] = output
        if layer == 0:
            normed = norm_parts(output.astype(F32))[0]
            refs.attn_in[...] = (normed * (1.0 + mods_ref[7:8]) + mods_ref[6:7]).astype(BF16)

    return kernel


def mlp_back_kernel(layer):
    def kernel(pieces, mods_ref, upper, lower, kept, refs):
        lower_grad = joined(pieces)
        if layer == 1:
            lower_grad = (lower_grad.astype(F32) * mods_ref[11:12]).astype(BF16)
        wide = lower_grad.shape[1]
        refs.grads[:, :wide] = lower_grad
        pre_grad = dot(lower_grad, matrix(lower), 1, 0)
        slope = kept[:, wide + pre_grad.shape[1] :].astype(F32)
        pre_grad = (pre_grad * slope).astype(BF16)
        refs.grads[:, wide:] = pre_grad
        spread_out(dot(pre_grad, matrix(upper), 1, 1), refs.terms)
        refs.bias[0:1] = column_sum(pre_grad)
        refs.bias[1:2] = column_sum(lower_grad)

    return kernel


def middle_back_kernel(layer):
    def kernel(terms, grad_ref, kept, mlp_out, mods_ref, refs):
        mods = mods_ref[6 * layer : 6 * layer + 6]
        grad = grad_ref[...].astype(F32)
        mid_grad = summed(terms)
        normed, scale = norm_parts(kept[kept.shape[0] // 2 :])
        middle_grad = grad + norm_pull(mid_grad * (1.0 + mods[4:5]), normed, scale)
        refs.middle_grad[...] = middle_grad
        refs.outer[...] = (middle_grad * mods[2:3]).astype(BF16)
        refs.rows[0:1] = column_sum(middle_grad * kept[: kept.shape[0] // 2])
        refs.rows[1:2] = column_sum(mid_grad)
        refs.rows[2:3] = column_sum(mid_grad * normed)
        refs.rows[3:4] = column_sum(grad * mlp_out[...])

    return kernel


def attend_back_kernel(layer):
    def kernel(pieces, packed, kept, refs):
        outer_grad = joined(pieces)
        wide = outer_grad.shape[1]
        refs.grads[:, :wide] = outer_grad
        packed = matrix(packed)
        width = packed.shape[1] // 4
        mixed_grad = dot(outer_grad, packed[:, 3 * width :], 1, 0).astype(BF16)
        queries, keys, values = [
            kept[:, wide + k * width : wide + (k + 1) * width] for k in range(3)
        ]
        d_queries, d_keys, d_values = [], [], []
        for at in range(0, width, HD):
            query, key = queries[:, at : at + HD], keys[:, at : at + HD]
            grad = mixed_grad[:, at : at + HD]
            attention = softmax_parts(query, key)
            weight_grad = dot(grad, values[:, at : at + HD], 1, 1)
            d_values.append(dot(attention.astype(BF16), grad, 0, 0))
            row_dot = jnp.sum(attention * weight_grad, axis=-1, keepdims=True)
            score_grad = (attention * (weight_grad - row_dot)).astype(BF16)
            d_queries.append(dot(score_grad, key, 1, 0) * HD**-0.5)
            d_keys.append(dot(score_grad, query, 0, 0) * HD**-0.5)
        stacked = jnp.concatenate(d_queries + d_keys + d_values, axis=1).astype(BF16)
        refs.grads[:, wide:] = stacked
        terms = dot(stacked, packed[:, : 3 * width], 1, 1)
        spread_out(terms, refs.terms)
        refs.out_bias[...] = column_sum(outer_grad)
        refs.in_bias[...] = column_sum(stacked)
        if layer == 0:
            normed = norm_parts(kept[:, 2 * wide :].astype(F32))[0]
            refs.rows[0:1] = column_sum(terms)
            refs.rows[1:2] = column_sum(terms * normed)

    return kernel


def first_back_kernel(layer):
    def kernel(terms, middle_grad, inputs, mods_ref, refs):
        in_grad = summed(terms)
        normed, scale = norm_parts(inputs[...].astype(F32))
        scale_one = mods_ref[6 * layer + 1 : 6 * layer + 2]
        input_grad = middle_grad[...] + norm_pull(in_grad * (1.0 + scale_one), normed, scale)
        refs.input_grad[...] = input_grad
        if layer == 1:
            refs.rows[0:1] = column_sum(in_grad)
            refs.rows[1:2] = column_sum(in_grad * normed)
            rounded = input_grad.astype(BF16)
            refs.grad[...] = rounded
            refs.lower[...] = (rounded.astype(F32) * mods_ref[5:6]).astype(BF16)

    return kernel


def cut(grad, ref, at):
    count, rows, half = ref.shape[0], ref.shape[2], ref.shape[3]
    for block in range(count):
        place_at = block // 2 * rows
        ref[block, at] = grad[
            place_at : place_at + rows, block % 2 * half : block % 2 * half + half
        ].astype(BF16)


def mlp_grads_kernel(kept, grads, refs):
    wide = 2 * refs.grads.shape[3]
    size = grads.shape[1] - wide
    cut(dot(kept[:, :wide], grads[:, wide:], 0, 0), refs.grads, 0)
    cut(dot(grads[:, :wide], kept[:, wide : wide + size], 0, 0), refs.grads, 1)


def packed_grads(kept, grads, wide):
    width = wide // 4
    inner = dot(kept[:, :wide], grads[:, wide:], 0, 0)
    outer = dot(grads[:, :wide], kept[:, wide + 3 * width : 2 * wide], 0, 0)
    return jnp.concatenate([inner, outer], axis=1)


def attend_grads_kernel(kept, grads, refs):
    cut(packed_grads(kept, grads, 2 * refs.grads.shape[3]), refs.grads, 0)


def attend_halves_kernel(spot, kept, grads, refs):
    half = refs.kept.shape[1]
    grad = packed_grads(kept, grads, 2 * half)
    left, right = grad[:, :half], grad[:, half:]
    refs.kept[...] = jnp.where(spot[0] == 0, left, right)
    refs.given[...] = jnp.where(spot[0] == 0, right, left).astype(BF16)


def share_kernel(spot, kept, received, refs):
    rows = refs.own.shape[0]
    for k, ref in enumerate([refs.own] + refs.sent):
        at = pl.ds(pl.multiple_of(spot[3 + k] * rows, rows), rows)
        ref[...] = (kept[at, :] + received[at, :].astype(F32)).astype(ref.dtype)


def ordered(spot, at, pieces):
    result = []
    for j in range(len(pieces)):
        chosen = pieces[0]
        for k in range(1, len(pieces)):
            chosen = jnp.where(spot[at + k] == j, pieces[k], chosen)
        result.append(chosen)
    return result


def mods_kernel(spot, mod_pieces, kept, got, refs):
    count = len(kept)
    refs.mods[...] = jnp.concatenate(
        ordered(spot, 3 + count, [ref[...] for ref in mod_pieces]), axis=1
    )
    mine = ordered(spot, 3, [ref[...] for ref in kept])
    theirs = ordered(spot, 3, [got[4 * k : 4 * k + 4] for k in range(count)])
    cols = refs.inner[0].shape[1] // count
    for layer in range(2):
        pieces = [
            jnp.where(spot[0] == layer, first, second) for first, second in zip(mine, theirs)
        ]
        refs.biases[layer][...] = jnp.concatenate(pieces, axis=1)
        for k in range(2):
            refs.inner[layer][k : k + 1] = jnp.concatenate(
                [piece[0:1, k * cols : (k + 1) * cols] for piece in pieces], axis=1
            )


def pack_kernel(spot, mod_one, mod_two, bias_one, bias_two, refs):
    core, here, cycle = spot[0], spot[1], spot[2]
    mods = jnp.concatenate([ref[...] for ref in mod_one + mod_two], axis=0)
    cuts = len(refs.mods)
    part = mods.shape[1] // cuts
    blocks = [mods[:, j * part : (j + 1) * part] for j in range(cuts)]
    for k, ref in enumerate(refs.mods):
        index = jnp.where(cycle == 1, (here - k + cuts) % cuts, here ^ k)
        chosen = blocks[0]
        for j in range(1, cuts):
            chosen = jnp.where(index == j, blocks[j], chosen)
        ref[...] = chosen
    packs = []
    for in_bias, out_bias, mlp_bias in (bias_one, bias_two):
        shards = refs.kept.shape[0]
        rows = refs.kept.shape[2]
        cols = part // shards
        pieces = []
        for z in range(shards):
            start = jnp.concatenate(
                [
                    in_bias[:, z * cols : (z + 1) * cols],
                    in_bias[:, 2 * part + z * cols : 2 * part + (z + 1) * cols],
                    jnp.zeros((1, rows - 2 * cols), F32),
                ],
                axis=1,
            )
            here_rows = slice(z * rows, (z + 1) * rows)
            pieces.append(
                jnp.concatenate(
                    [start, mlp_bias[0:1, here_rows], out_bias[:, here_rows], mlp_bias[1:2, here_rows]],
                    axis=0,
                )
            )
        packs.append(pieces)
    for z in range(refs.kept.shape[0]):
        refs.kept[z] = jnp.where(core == 0, packs[0][z], packs[1][z])
        refs.given[z] = jnp.where(core == 0, packs[1][z], packs[0][z])


def bundle_kernel(layers):
    def kernel(spot, kept, got, refs):
        for k, layer in enumerate(layers):
            refs.rows[k] = jnp.where(spot[0] == layer, kept[k][...], got[k][...])

    return kernel


def stack_kernel(pieces, refs):
    for k, piece in enumerate(pieces):
        refs.stack[k] = piece[...]


def turn_kernel(spot, mod_pieces, given, refs):
    total = summed(mod_pieces)
    first, second = total[:6], total[6:]
    refs.kept[...] = jnp.where(spot[0] == 0, first, second)
    refs.given[:6] = jnp.where(spot[0] == 0, second, first)
    for z in range(given.shape[0]):
        refs.given[6 + 4 * z : 10 + 4 * z] = given[z]


def slots_kernel(spot, mod_kept, kept, received, refs):
    mine, theirs = mod_kept[...], received[:6]
    for k, ref in enumerate(refs.sent):
        ref[:6] = jnp.where(spot[0] == 0, mine, theirs)
        ref[6:12] = jnp.where(spot[0] == 0, theirs, mine)
        total = kept[0] + received[6:10]
        for z in range(1, kept.shape[0]):
            total = jnp.where(spot[3 + k] == z, kept[z] + received[6 + 4 * z : 10 + 4 * z], total)
        ref[12:16] = total


def sinus_features(stamps, columns):
    halfway = columns // 2
    frequency = jnp.exp(-math.log(10000.0) * jnp.arange(halfway, dtype=F32) / halfway)
    angles = stamps.astype(F32)[:, None] * frequency[None, :]
    return jnp.concatenate([jnp.cos(angles), jnp.sin(angles)], axis=-1)


def body(
    latents,
    cotangent,
    labels,
    timesteps,
    occupied,
    class_table,
    time_weight,
    project_in,
    project_in_bias,
    project_out,
    project_out_bias,
    up_weight,
    up_bias,
    down_weight,
    down_bias,
    modulate_weight,
    modulate_bias,
):
    core = lax.axis_index(SECTION)
    shard = lax.axis_index(SLOTS)
    shards = lax.axis_size(SLOTS)
    cuts = lax.axis_size(TENSOR)
    micro_count = latents.shape[0]
    width = latents.shape[3]
    own_tokens = latents.shape[2]
    tokens = own_tokens * cuts
    part = width // cuts
    rows = width // shards
    hidden_part = up_weight.shape[2]
    near = shards <= 8 and not cyclic(SLOTS) and rows == part

    def pick(first, second):
        return jnp.where(core == 0, first, second)

    spot = jnp.stack(
        [core, lax.axis_index(TENSOR), jnp.int32(1 if cyclic(TENSOR) else 0)]
        + [partner(SLOTS, k) for k in range(shards if near else 0)]
        + [partner(TENSOR, k) for k in range(cuts)]
    ).astype(jnp.int32)

    packed_own = jnp.concatenate(
        [project_in[0, :, 0], project_in[0, :, 1], project_in[0, :, 2], project_out[0].T], axis=1
    )
    stack = [packed_own, up_weight[0], down_weight[0].T]
    half = rows // 2
    given = swap(jnp.concatenate([pick(member[half:], member[:half]) for member in stack]))
    kept_halves = [pick(member[:half], member[half:]) for member in stack]
    got_halves = [given[k * half : (k + 1) * half] for k in range(3)]

    def bundle(members, wait):
        return run(
            bundle_kernel([layer for _, layer in members]),
            Named(rows=shaped((len(members), half, width), BF16)),
            spot,
            [kept_halves[k] for k, _ in members],
            [got_halves[k] for k, _ in members],
            wait=wait,
        ).rows

    def gather_blocks(members, wait=()):
        if near:
            whole = lax.all_gather(bundle(members, wait), ROWS, axis=0)
            return [Part(whole, k) for k in range(len(members))]
        return [
            gather_rows(
                pick(kept_halves[k], got_halves[k])
                if layer == 0
                else pick(got_halves[k], kept_halves[k])
            )
            for k, layer in members
        ]

    def gather_rows(value):
        return lax.all_gather(value, ROWS, axis=0, tiled=True)

    stamps = jnp.concatenate([labels.reshape(1, -1), timesteps.reshape(1, -1)], axis=1)
    if near:
        stamps = jnp.concatenate(gather_list(stamps, SLOTS), axis=0)
    else:
        stamps = lax.all_gather(stamps, SLOTS, axis=0, tiled=True)
    flat_labels = stamps[:, :micro_count].reshape(-1)
    flat_times = stamps[:, micro_count:].reshape(-1)
    class_count = class_table.shape[0]
    class_hot = flat_labels[:, None] == jnp.arange(class_count, dtype=jnp.int32)[None, :]
    time_feats = sinus_features(flat_times, time_weight.shape[0]).astype(BF16)
    condition = dot(class_hot.astype(BF16), class_table, 1, 0) + dot(time_feats, time_weight, 1, 0)
    cond_act = jax.nn.silu(condition).astype(BF16)
    act_rows = lax.dynamic_slice_in_dim(cond_act, shard * rows, rows, 1)

    if near:
        first_pieces = gather_list(pick(kept_halves[0], got_halves[0]), SLOTS)
    else:
        (first_a,) = gather_blocks([(0, 0)])

    tokens_own = pick(latents[0, 0], latents[1, 0])
    seed_own = pick(
        cotangent[0, 0] * occupied[0, 0].astype(BF16), cotangent[1, 0] * occupied[1, 0].astype(BF16)
    )
    token_list = gather_list(tokens_own, TENSOR)

    mod_weight = modulate_weight[0].reshape(rows, -1)
    bias_cols = modulate_bias.shape[2]
    bias_full = lax.dynamic_update_slice_in_dim(
        jnp.zeros((6, part), F32), modulate_bias[0].astype(F32), shard * bias_cols, 1
    )
    mod_terms = dot(act_rows, mod_weight, 1, 0) + bias_full.reshape(1, -1)
    mod_terms = mod_terms.reshape(shards, micro_count * 6, part)
    in_bias_own = project_in_bias.astype(F32).reshape(1, -1)
    bias_own = jnp.concatenate(
        [
            jnp.pad(in_bias_own, ((0, 0), (0, rows - in_bias_own.shape[1]))),
            up_bias.astype(F32),
            project_out_bias.astype(F32),
            down_bias.astype(F32),
        ],
        axis=0,
    )
    if near:
        got = exchange_list(
            [jnp.concatenate([mod_terms[k], bias_own], axis=0) for k in range(shards)], SLOTS
        )
        mod_sum = sum(member[: micro_count * 6] for member in got)
        bias_list = [member[micro_count * 6 :] for member in got]
    else:
        mod_sum = lax.psum_scatter(mod_terms, SLOTS, scatter_dimension=0, tiled=False)
        bias_all = lax.all_gather(bias_own, SLOTS, axis=0)
    if near:
        received = swap(jnp.concatenate([pick(mod_sum[6:], mod_sum[:6])] + bias_list, axis=0))
        mod_got, bias_got = received[:6], received[6:]
    else:
        mod_got, bias_got = swap(pick(mod_sum[6:], mod_sum[:6])), swap(bias_all)
    mod_kept = pick(mod_sum[:6], mod_sum[6:])
    mod_both = jnp.concatenate([pick(mod_kept, mod_got), pick(mod_got, mod_kept)], axis=0)
    mod_list = gather_list(mod_both, TENSOR)
    if near:
        ready = run(
            mods_kernel,
            Named(
                mods=shaped((12, width), F32),
                biases=[shaped((4, width), F32)] * 2,
                inner=[shaped((2, part), F32)] * 2,
            ),
            spot,
            mod_list,
            bias_list,
            bias_got,
        )
        mods, biases, in_biases = ready.mods, ready.biases, ready.inner
    else:
        mods = jnp.moveaxis(place(mod_list, TENSOR), 0, 1).reshape(12, width)
        in_biases, biases = [], []
        for member in (pick(bias_all, bias_got), pick(bias_got, bias_all)):
            cols = project_in_bias.shape[2]
            columns = member[:, 0, : 2 * cols].reshape(shards, 2, cols)
            in_biases.append(jnp.moveaxis(columns, 0, 1).reshape(2, part))
            biases.append(jnp.moveaxis(member, 0, 1).reshape(4, width))
    if near:
        stacked_pieces = run(
            stack_kernel,
            Named(stack=shaped((shards, half, width), BF16)),
            first_pieces,
            wait=tuple(mod_list[1:]),
        ).stack
        first_a = (first_pieces, swap(stacked_pieces))
    first_u, first_d, second_a = gather_blocks(
        [(1, 0), (2, 0), (0, 1)], tuple(bias_list[1:]) if near else ()
    )
    weights = [(first_a, first_u, first_d), None]

    def terms_out(count=1):
        return [shaped((own_tokens, width), F32)] + [
            shaped((own_tokens, width), BF16) for k in range(1, cuts)
        ]

    own_f32 = shaped((own_tokens, width), F32)
    both_f32 = shaped((2 * own_tokens, width), F32)
    own_b16 = shaped((own_tokens, width), BF16)
    attend_flops = 2 * tokens * width * width + 4 * tokens * tokens * part
    mlp_flops = 4 * tokens * width * hidden_part

    kept, packs = [], []
    inputs = tokens_own
    first = token_list
    for layer in range(2):
        packed, upper, lower = weights[layer]
        outs = Named(kept=shaped((tokens, (3 - layer) * width), BF16), terms=terms_out())
        if isinstance(packed, tuple):
            outs.packed = shaped((width, width), BF16)
        attn = run(
            attend_kernel(layer),
            outs,
            spot,
            first,
            mods,
            packed,
            in_biases[layer],
            flops=attend_flops,
        )
        packs.append(attn.packed if isinstance(packed, tuple) else packed)
        if layer == 0:
            second_u, second_d = gather_blocks([(1, 1), (2, 1)], (attn.kept,))
            weights[1] = (second_a, second_u, second_d)
        middle = run(
            middle_kernel(layer),
            Named(kept=both_f32, mlp_in=own_b16),
            exchange_list(attn.terms, TENSOR),
            inputs,
            mods,
            biases[layer],
        )
        mlp = run(
            mlp_kernel,
            Named(kept=shaped((tokens, width + 2 * hidden_part), BF16), terms=terms_out()),
            gather_list(middle.mlp_in, TENSOR),
            upper,
            lower,
            biases[layer],
            flops=mlp_flops,
        )
        outs = Named(mlp_out=own_f32, output=own_b16)
        if layer == 0:
            outs.attn_in = own_b16
        last = run(
            last_kernel(layer),
            outs,
            exchange_list(mlp.terms, TENSOR),
            middle.kept,
            mods,
            biases[layer],
        )
        kept.append((inputs, attn, middle, mlp, last))
        inputs = last.output
        if layer == 0:
            first = gather_list(last.attn_in, TENSOR)
            seed_list = gather_list(seed_own, TENSOR)

    row = shaped((1, width), F32)
    grad_own, pieces = seed_own, seed_list
    mod_rows, bias_rows, blocks, input_grads = [None] * 2, [None] * 2, [None] * 2, [None] * 2
    wait = ()
    for layer in (1, 0):
        packed, upper, lower = packs[layer], weights[layer][1], weights[layer][2]
        inputs, attn, middle, mlp, last = kept[layer]
        mlp_back = run(
            mlp_back_kernel(layer),
            Named(
                grads=shaped((tokens, width + hidden_part), BF16),
                terms=terms_out(),
                bias=shaped((2, hidden_part), F32),
            ),
            pieces,
            mods,
            upper,
            lower,
            mlp.kept,
            flops=mlp_flops,
        )
        mlp_grads = run(
            mlp_grads_kernel,
            Named(grads=shaped((2 * shards, 2, rows, width // 2), BF16)),
            mlp.kept,
            mlp_back.grads,
            flops=mlp_flops,
        ).grads
        middle_back = run(
            middle_back_kernel(layer),
            Named(
                middle_grad=own_f32,
                outer=own_b16,
                rows=shaped((4, width), F32),
            ),
            exchange_list(mlp_back.terms, TENSOR),
            grad_own,
            middle.kept,
            last.mlp_out,
            mods,
        )
        outs = Named(
            grads=shaped((tokens, width + 3 * part), BF16),
            terms=terms_out(),
            out_bias=row,
            in_bias=shaped((1, 3 * part), F32),
        )
        if layer == 0:
            outs.rows = shaped((2, width), F32)
        attn_back = run(
            attend_back_kernel(layer),
            outs,
            gather_list(middle_back.outer, TENSOR),
            packed,
            attn.kept,
            flops=2 * attend_flops,
            wait=wait,
        )
        operands = (attn.kept, attn_back.grads)
        if layer == 1 or not near:
            attn_grads = run(
                attend_grads_kernel,
                Named(grads=shaped((2 * shards, 1, rows, width // 2), BF16)),
                *operands,
                flops=2 * tokens * width * width,
            ).grads
        else:
            attn_grads = run(
                attend_halves_kernel,
                Named(kept=shaped((width, width // 2), F32), given=shaped((width, width // 2), BF16)),
                spot,
                *operands,
                flops=2 * tokens * width * width,
            )
        outs = Named(input_grad=own_f32)
        if layer == 1:
            outs.rows, outs.grad, outs.lower = shaped((2, width), F32), own_b16, own_b16
        first_back = run(
            first_back_kernel(layer),
            outs,
            exchange_list(attn_back.terms, TENSOR),
            middle_back.middle_grad,
            inputs,
            mods,
        )
        input_grads[layer] = first_back.input_grad
        mod_rows[layer] = [
            attn_back.rows if layer == 0 else first_back.rows,
            middle_back.rows,
        ]
        bias_rows[layer] = (attn_back.in_bias, attn_back.out_bias, mlp_back.bias)

        def scatter(grads):
            return lax.psum_scatter(grads, ROWS, scatter_dimension=0, tiled=False)

        if layer == 1:
            blocks[1] = scatter(jnp.concatenate([mlp_grads, attn_grads], axis=1))
            grad_own = first_back.grad
            pieces = gather_list(first_back.lower, TENSOR)
            wait = (blocks[1],)
        else:
            mlp_block = scatter(mlp_grads)
            if near:
                shares = run(
                    share_kernel,
                    Named(
                        own=shaped((rows, width // 2), F32),
                        sent=[shaped((rows, width // 2), BF16)] * (shards - 1),
                    ),
                    spot,
                    attn_grads.kept,
                    swap(attn_grads.given),
                )
                got = exchange_list([shares.own] + shares.sent, SLOTS)
                attn_block = sum(member.astype(F32) for member in got)[None].astype(BF16)
            else:
                attn_block = scatter(attn_grads)
            blocks[0] = jnp.concatenate([mlp_block, attn_block], axis=0)

    given = swap(pick(blocks[1], blocks[0]))
    own = pick(blocks[0], blocks[1])
    grads = jnp.concatenate([pick(own, given), pick(given, own)], axis=2).astype(F32)
    grad_upper, grad_lower = grads[0], grads[1].T
    grad_inner = grads[2, :, : 3 * part].reshape(rows, 3, part)
    grad_outer = grads[2, :, 3 * part :].T

    tail = run(
        pack_kernel,
        Named(mods=[shaped((12, part), F32) for k in range(cuts)],
            kept=shaped((shards, 4, rows), F32),
            given=shaped((shards, 4, rows), F32),
        ),
        spot,
        mod_rows[0],
        mod_rows[1],
        bias_rows[0],
        bias_rows[1],
    )
    mod_list = exchange_list(tail.mods, TENSOR)
    if near:
        turned = run(
            turn_kernel,
            Named(kept=shaped((6, part), F32), given=shaped((6 + 4 * shards, part), F32)),
            spot,
            mod_list,
            tail.given,
        )
        sent = run(
            slots_kernel,
            Named(sent=[shaped((16, part), F32)] * shards),
            spot,
            turned.kept,
            tail.kept,
            swap(turned.given),
            wait=(shares.own,),
        ).sent
        got = exchange_list(sent, SLOTS)
        mod_slots = jnp.concatenate([member[:12] for member in got], axis=0)
        bias_total = sum(member[12:] for member in got)
    else:
        mod_shard = sum(mod_list)
        mod_given, mod_kept = pick(mod_shard[6:], mod_shard[:6]), pick(mod_shard[:6], mod_shard[6:])
        mod_got, bias_got = swap(mod_given), swap(tail.given)
        mod_micro = jnp.concatenate([pick(mod_kept, mod_got), pick(mod_got, mod_kept)], axis=0)
        bias_sum = tail.kept + bias_got
        mod_slots = lax.all_gather(mod_micro, SLOTS, axis=0, tiled=True)
        bias_total = lax.psum_scatter(bias_sum, SLOTS, scatter_dimension=0, tiled=False)
    mod_slots = mod_slots.reshape(shards * micro_count, 6 * part)
    act_grad = lax.dot_general(
        mod_slots, mod_weight.astype(F32), (((1,), (1,)), ((), ())), precision=HIGH
    )
    act_grad = act_grad + swap(act_grad)
    act_grad = sum(gather_list(act_grad, TENSOR))
    if near:
        act_list = []
        for k, member in enumerate(gather_list(act_grad, SLOTS)):
            member = member.reshape(shards, micro_count, rows)
            act_list.append(jnp.concatenate([member[j ^ k] for j in range(shards)], axis=0))
        act_all = place(act_list, SLOTS)
    else:
        act_all = lax.all_gather(act_grad, SLOTS, axis=0)
    act_all = jnp.moveaxis(act_all, 0, 1).reshape(-1, width)
    cond_grad = jax.vjp(jax.nn.silu, condition)[1](act_all)[0]
    table_grad = lax.dot_general(
        class_hot.astype(F32), cond_grad, (((0,), (0,)), ((), ())), precision=HIGH
    )
    time_grad = lax.dot_general(
        time_feats.astype(F32), cond_grad, (((0,), (0,)), ((), ())), precision=HIGH
    )
    grad_mod_weight = lax.dot_general(
        act_rows.astype(F32), mod_slots, (((0,), (0,)), ((), ())), precision=HIGH
    ).reshape(rows, 6, part)
    mod_bias_sum = jnp.sum(mod_slots, axis=0).reshape(6, part)
    grad_mod_bias = lax.dynamic_slice_in_dim(mod_bias_sum, shard * bias_cols, bias_cols, 1)
    grad_in_bias = bias_total[0, : in_bias_own.shape[1]].reshape(2, -1)

    def by_micro(first, second):
        got = swap(pick(second, first))
        held = pick(first, second)
        return jnp.stack([pick(held, got), pick(got, held)])[None, :, None]

    return (
        by_micro(kept[0][4].output, kept[1][4].output),
        by_micro(input_grads[0], input_grads[1]),
        table_grad,
        time_grad,
        grad_inner[None],
        grad_in_bias[None],
        grad_outer[None],
        bias_total[2][None],
        grad_upper[None],
        bias_total[1][None],
        grad_lower[None],
        bias_total[3][None],
        grad_mod_weight[None],
        grad_mod_bias[None],
    )


def solution(mesh):
    in_specs = (
        P(None, SLOTS, TENSOR, None),
        P(None, SLOTS, TENSOR, None),
        P(None, SLOTS),
        P(None, SLOTS),
        P(None, SLOTS),
        P(),
        P(),
        P(SECTION, SLOTS, None, TENSOR),
        P(SECTION, None, (TENSOR, SLOTS)),
        P(SECTION, TENSOR, SLOTS),
        P(SECTION, SLOTS),
        P(SECTION, SLOTS, TENSOR),
        P(SECTION, (TENSOR, SLOTS)),
        P(SECTION, TENSOR, SLOTS),
        P(SECTION, SLOTS),
        P(SECTION, SLOTS, None, TENSOR),
        P(SECTION, None, (TENSOR, SLOTS)),
    )
    out_specs = (
        P(SECTION, None, SLOTS, TENSOR, None),
        P(SECTION, None, SLOTS, TENSOR, None),
        P(),
        P(),
        P(SECTION, SLOTS, None, TENSOR),
        P(SECTION, None, (TENSOR, SLOTS)),
        P(SECTION, TENSOR, SLOTS),
        P(SECTION, SLOTS),
        P(SECTION, SLOTS, TENSOR),
        P(SECTION, (TENSOR, SLOTS)),
        P(SECTION, TENSOR, SLOTS),
        P(SECTION, SLOTS),
        P(SECTION, SLOTS, None, TENSOR),
        P(SECTION, None, (TENSOR, SLOTS)),
    )
    return jax.shard_map(body, mesh=mesh, in_specs=in_specs, out_specs=out_specs, check_vma=False)
```

time: 512 us -> 297 us (0.58); the launches traced: 503 us -> 296 us
  starting transfers between devices: 173 us -> 103 us
  other arithmetic: 75.1 us -> 11.6 us
  matrix products: 60.8 us -> 9.45 us
  local copies, waits for them, and re-layouts: 95.9 us -> 47 us
  Pallas kernels: 0 us -> 28.1 us
  waiting for transfers between devices: 91 us -> 81.8 us
  between operations: 6.41 us -> 15 us
    ppermute x26 -> x9, starting transfers between devices: 50.9 us -> 0.98 us  [swap(): return lax.ppermute(value, SECTION, [(0, 1), (1, 0)])]
    ppermute x36 -> x39, waiting for transfers between devices: 6.76 us -> 44.6 us  [fetch(): return lax.ppermute(value, axis, [(i, i ^ k) for i in range(size)])]
    dot_general x27 -> x3, matrix products: 36.1 us -> 1.8 us  [dot(): lax.dot_general(left, right, (((left_dim,), (right_dim,)), ((), ())), pre...]
    pallas_call x0 -> x28, Pallas kernels: none -> 28.1 us  [run(): pl.pallas_call(inner, out_shape=out_flat, in_specs=[pl.BlockSpec(memory_s...]
    ppermute x45 -> x36, waiting for transfers between devices: 60.5 us -> 35 us  [exchange(): return lax.ppermute(value, axis, [(i, i ^ k) for i in range(size)])]
    unnamed x392 -> x170, local copies, waits for them, and re-layouts: 15.9 us -> 40 us
    ppermute x45 -> x36, starting transfers between devices: 74.8 us -> 51.2 us  [exchange(): return lax.ppermute(value, axis, [(i, i ^ k) for i in range(size)])]
    ppermute x26 -> x9, waiting for transfers between devices: 23.8 us -> 0.48 us  [swap(): return lax.ppermute(value, SECTION, [(0, 1), (1, 0)])]
  transfers between devices with their start and end apart: 107 -> 88, of which waited for: 31 -> 48; matrix products, arithmetic and copies ran while one was open for 40% -> 8% of each run, Pallas kernels for 0% -> 8%
where the time goes in v2:
time: 297 us; the launch traced here: 296 us
  starting transfers between devices  103 us (35%)
  waiting for transfers between devices  81.8 us (28%)
  local copies, waits for them, and re-layouts  47 us (16%)
  Pallas kernels  28.1 us (9%)
  between operations  15 us (5%)
  other arithmetic  11.6 us (4%)
  matrix products  9.45 us (3%)
    ppermute x36, starting transfers between devices, exchange(): return lax.ppermute(value, axis, [(i, i ^ k) for i in range(size)])  51.2 us
    ppermute x39, starting transfers between devices, fetch(): return lax.ppermute(value, axis, [(i, i ^ k) for i in range(size)])  50.6 us
    ppermute x39, waiting for transfers between devices, fetch(): return lax.ppermute(value, axis, [(i, i ^ k) for i in range(size)])  44.6 us
    unnamed x170, local copies, waits for them, and re-layouts  40 us
    ppermute x36, waiting for transfers between devices, exchange(): return lax.ppermute(value, axis, [(i, i ^ k) for i in range(size)])  35 us
    pallas_call x28, Pallas kernels, run(): pl.pallas_call(inner, out_shape=out_flat, in_specs=[pl.BlockSpec(memory_s...  28.1 us
  transfers between devices with their start and end apart: 88, of which 48 were waited for; matrix products, arithmetic and copies ran while one was open for 8% of the time, Pallas kernels for 8%

profile of v2, /device:TPU:0, one launch (start us, length us, event | category | flops | bytes accessed | tf_op | source)
XLA Modules:
  0.0 296.4 jit_solution(119289962998102423)
XLA Ops:
  8.1 5.0 %collective-permute-start.5 = (s32[1,4]{1,0:T(1,128)S(1)}, s32[1,4]{1,0:T(1,128)S(1)}, u32[]{:S(2)}, u32[]{:S(2)}) collective-permute-start(s32[1,4]{1,0:T(1,128)S(1)} %pad_add_fusion.1), channel_id=1, source_target_pairs={{0,3},{1,2},{2,1},{3,0},{4,7},{5,6},{6,5},{7,4},{8,11},{9,10},{10,... | collective-permute-start | bytes 56 | tf_op jit(solution)/shard_map/ppermute | solution.py:37
  25.6 3.0 collective-permute-start.7
  30.4 3.7 %collective-permute-done.8 = f32[16,192]{1,0:T(8,128)S(1)} collective-permute-done((f32[16,192]{1,0:T(8,128)S(1)}, f32[16,192]{1,0:T(8,128)S(1)}, u32[]{:S(2)}, u32[]{:S(2)}) %collective-permute-start.8) | collective-permute-done | bytes 12320 | tf_op jit(solution)/shard_map/ppermute | solution.py:30
  37.4 3.7 %collective-permute-start.16 = (bf16[96,768]{1,0:T(8,128)(2,1)S(1)}, bf16[96,768]{1,0:T(8,128)(2,1)S(1)}, u32[]{:S(2)}, u32[]{:S(2)}) collective-permute-start(bf16[96,768]{1,0:T(8,128)(2,1)S(1)} %get-tuple-element.236.refs_0_.refs_6_), channel_id=1, source_target_pairs={{0,3},{1,2},{2,1},{3,0},{4,7},{5,6},{6,5},{7,4},{8,11},{9,10},{10,... | collective-permute-start | bytes 442376 | tf_op jit(solution)/shard_map/ppermute | solution.py:37
  45.0 2.4 collective-permute-start.12
  49.6 9.7 %collective-permute-done.15.refs_2_.refs_8_ = bf16[96,768]{1,0:T(8,128)(2,1)S(1)} collective-permute-done((bf16[96,768]{1,0:T(8,128)(2,1)S(1)}, bf16[96,768]{1,0:T(8,128)(2,1)S(1)}, u32[]{:S(2)}, u32[]{:S(2)}) %collective-permute-start.15) | collective-permute-done | bytes 147488 | tf_op jit(solution)/shard_map/ppermute | solution.py:37
  64.7 2.4 collective-permute-done.1.refs_3_
  81.3 3.1 %collective-permute-done.19.refs_2_ = bf16[64,768]{1,0:T(8,128)(2,1)S(1)} collective-permute-done((bf16[64,768]{1,0:T(8,128)(2,1)}, bf16[64,768]{1,0:T(8,128)(2,1)S(1)}, u32[]{:S(2)}, u32[]{:S(2)}) %collective-permute-start.19) | collective-permute-done | bytes 98336 | tf_op jit(solution)/shard_map/ppermute | solution.py:30
  123.1 2.3 collective-permute-done.32.refs_3_
  138.7 2.3 shard_map.282
  151.2 3.0 %collective-permute-done.44.refs_2_ = bf16[64,768]{1,0:T(8,128)(2,1)S(1)} collective-permute-done((bf16[64,768]{1,0:T(8,128)(2,1)S(1)}, bf16[64,768]{1,0:T(8,128)(2,1)S(1)}, u32[]{:S(2)}, u32[]{:S(2)}) %collective-permute-start.44) | collective-permute-done | bytes 98336 | tf_op jit(solution)/shard_map/ppermute | solution.py:30
  159.5 4.4 %collective-permute-done.47.refs_2_ = bf16[64,768]{1,0:T(8,128)(2,1)S(1)} collective-permute-done((bf16[64,768]{1,0:T(8,128)(2,1)S(1)}, bf16[64,768]{1,0:T(8,128)(2,1)S(1)}, u32[]{:S(2)}, u32[]{:S(2)}) %collective-permute-start.47) | collective-permute-done | bytes 98336 | tf_op jit(solution)/shard_map/ppermute | solution.py:37
  163.9 2.4 shard_map.286
  167.0 2.2 pad_maximum_fusion
  175.1 2.4 collective-permute-done.51.refs_3_
  186.2 2.5 collective-permute-done.54.refs_3_
  211.1 2.2 collective-permute-start.60
  222.4 3.4 %shard_map.292 = (bf16[256,1344]{1,0:T(8,128)(2,1)S(1)}, f32[64,768]{1,0:T(8,128)S(1)}, bf16[64,768]{1,0:T(8,128)(2,1)S(1)}, bf16[64,768]{1,0:T(8,128)(2,1)S(1)}...) custom-call(bf16[64,768]{1,0:T(8,128)(2,1)} %get-tuple-element.154.refs_0_, ...), custom_call_target="tpu_custom_call" | custom-call | flops 704643072 | bytes 3943680 | tf_op jit(solution)/shard_map/pallas_call | solution.py:93
  231.9 2.4 collective-permute-done.63.refs_3_
  236.8 2.4 collective-permute-start.67
  245.6 8.5 %collective-permute-start.71 = (f32[16,192]{1,0:T(8,128)S(1)}, f32[16,192]{1,0:T(8,128)S(1)}, u32[]{:S(2)}, u32[]{:S(2)}) collective-permute-start(f32[16,192]{1,0:T(8,128)S(1)} %get-tuple-element.188), channel_id=1, source_target_pairs={{0,2},{1,3},{2,0},{3,1},{4,6},{5,7},{6,4},{7,5},{8,10},{9,11},{10,... | collective-permute-start | bytes 36872 | tf_op jit(solution)/shard_map/ppermute | solution.py:30
  271.4 3.0 %collective-permute-done.77 = f32[8,192]{1,0:T(8,128)S(1)} collective-permute-done((f32[8,192]{1,0:T(8,128)S(1)}, f32[8,192]{1,0:T(8,128)S(1)}, u32[]{:S(2)}, u32[]{:S(2)}) %collective-permute-start.77) | collective-permute-done | bytes 6176 | tf_op jit(solution)/shard_map/ppermute | solution.py:37
  275.8 4.1 %collective-permute-done.79 = f32[8,192]{1,0:T(8,128)S(1)} collective-permute-done((f32[8,192]{1,0:T(8,128)S(1)}, f32[8,192]{1,0:T(8,128)S(1)}, u32[]{:S(2)}, u32[]{:S(2)}) %collective-permute-start.79) | collective-permute-done | bytes 6176 | tf_op jit(solution)/shard_map/ppermute | solution.py:37
  283.1 3.2 %fusion.2 = f32[1001,768]{1,0:T(8,128)} fusion(s32[8]{0:T(128)S(1)} %copy-done.77, f32[8,768]{1,0:T(8,128)S(1)} %copy-done.58, f32[8,768]{1,0:T(8,128)S(1)} %reshape.135), kind=kOutput, calls=%fused_computation.42 | convolution fusion | flops 73865032 | bytes 3124256 | tf_op jit(solution)/shard_map/dot_general | solution.py:908
  (452 shorter events, 197.8 us)
Async XLA Ops:
  7.2 86.6 %all-gather.5.cloned.1.call-start = ((), (), s32[]{:S(2)}) async-start(), calls=%async_computation.4 | async-start | bytes 3981312 | tf_op jit(solution)/shard_map/all_gather | solution.py:550
  8.1 12.5 %collective-permute-start.5 = (s32[1,4]{1,0:T(1,128)S(1)}, s32[1,4]{1,0:T(1,128)S(1)}, u32[]{:S(2)}, u32[]{:S(2)}) collective-permute-start(s32[1,4]{1,0:T(1,128)S(1)} %pad_add_fusion.1), channel_id=1, source_target_pairs={{0,3},{1,2},{2,1},{3,0},{4,7},{5,6},{6,5},{7,4},{8,11},{9,10},{10,... | collective-permute-start | bytes 56 | tf_op jit(solution)/shard_map/ppermute | solution.py:37
  13.1 7.5 %collective-permute-start.4 = (s32[1,4]{1,0:T(1,128)S(1)}, s32[1,4]{1,0:T(1,128)S(1)}, u32[]{:S(2)}, u32[]{:S(2)}) collective-permute-start(s32[1,4]{1,0:T(1,128)S(1)} %pad_add_fusion.1), channel_id=1, source_target_pairs={{0,2},{1,3},{2,0},{3,1},{4,6},{5,7},{6,4},{7,5},{8,10},{9,11},{10,... | collective-permute-start | bytes 56 | tf_op jit(solution)/shard_map/ppermute | solution.py:37
  13.1 7.5 %collective-permute-start.3 = (s32[1,4]{1,0:T(1,128)S(1)}, s32[1,4]{1,0:T(1,128)S(1)}, u32[]{:S(2)}, u32[]{:S(2)}) collective-permute-start(s32[1,4]{1,0:T(1,128)S(1)} %pad_add_fusion.1), channel_id=1, source_target_pairs={{0,1},{1,0},{2,3},{3,2},{4,5},{5,4},{6,7},{7,6},{8,9},{9,8},{10,11... | collective-permute-start | bytes 56 | tf_op jit(solution)/shard_map/ppermute | solution.py:37
  18.8 16.0 %collective-permute-start.13 = (bf16[288,768]{1,0:T(8,128)(2,1)}, bf16[288,768]{1,0:T(8,128)(2,1)S(1)}, u32[]{:S(2)}, u32[]{:S(2)}) collective-permute-start(bf16[288,768]{1,0:T(8,128)(2,1)} %pad_maximum_fusion.1), channel_id=1, source_target_pairs={{0,16},{16,0},{1,17},{17,1},{2,18},{18,2},{3,19},{19,3},{4,20},{20... | collective-permute-start | bytes 1327112 | tf_op jit(solution)/shard_map/ppermute | solution.py:48
  36.3 99.8 %all-gather.7.cloned.1.call-start = ((), (), s32[]{:S(2)}) async-start(), calls=%async_computation.5 | async-start | bytes 2654208 | tf_op jit(solution)/shard_map/all_gather | solution.py:550
  36.7 12.9 %collective-permute-start.14 = (bf16[96,768]{1,0:T(8,128)(2,1)S(1)}, bf16[96,768]{1,0:T(8,128)(2,1)S(1)}, u32[]{:S(2)}, u32[]{:S(2)}) collective-permute-start(bf16[96,768]{1,0:T(8,128)(2,1)S(1)} %get-tuple-element.236.refs_0_.refs_6_), channel_id=1, source_target_pairs={{0,1},{1,0},{2,3},{3,2},{4,5},{5,4},{6,7},{7,6},{8,9},{9,8},{10,11... | collective-permute-start | bytes 442376 | tf_op jit(solution)/shard_map/ppermute | solution.py:37
  36.7 22.6 %collective-permute-start.15 = (bf16[96,768]{1,0:T(8,128)(2,1)S(1)}, bf16[96,768]{1,0:T(8,128)(2,1)S(1)}, u32[]{:S(2)}, u32[]{:S(2)}) collective-permute-start(bf16[96,768]{1,0:T(8,128)(2,1)S(1)} %get-tuple-element.236.refs_0_.refs_6_), channel_id=1, source_target_pairs={{0,2},{1,3},{2,0},{3,1},{4,6},{5,7},{6,4},{7,5},{8,10},{9,11},{10,... | collective-permute-start | bytes 442376 | tf_op jit(solution)/shard_map/ppermute | solution.py:37
  37.4 21.9 %collective-permute-start.16 = (bf16[96,768]{1,0:T(8,128)(2,1)S(1)}, bf16[96,768]{1,0:T(8,128)(2,1)S(1)}, u32[]{:S(2)}, u32[]{:S(2)}) collective-permute-start(bf16[96,768]{1,0:T(8,128)(2,1)S(1)} %get-tuple-element.236.refs_0_.refs_6_), channel_id=1, source_target_pairs={{0,3},{1,2},{2,1},{3,0},{4,7},{5,6},{6,5},{7,4},{8,11},{9,10},{10,... | collective-permute-start | bytes 442376 | tf_op jit(solution)/shard_map/ppermute | solution.py:37
  59.4 8.7 %collective-permute-start.17 = (bf16[4,96,768]{2,1,0:T(8,128)(2,1)S(1)}, bf16[4,96,768]{2,1,0:T(8,128)(2,1)S(1)}, u32[]{:S(2)}, u32[]{:S(2)}) collective-permute-start(bf16[4,96,768]{2,1,0:T(8,128)(2,1)S(1)} %shard_map.273), channel_id=1, source_target_pairs={{0,16},{16,0},{1,17},{17,1},{2,18},{18,2},{3,19},{19,3},{4,20},{20... | collective-permute-start | bytes 1769480 | tf_op jit(solution)/shard_map/ppermute | solution.py:48
  76.0 143.2 %reduce-scatter.3.cloned.1.call-start = ((), (), s32[]{:S(2)}) async-start(), calls=%async_computation.2 | async-start | bytes 3981312 | tf_op jit(solution)/shard_map/reduce_scatter | solution.py:818
  131.9 11.1 %collective-permute-start.40 = (bf16[64,768]{1,0:T(8,128)(2,1)S(1)}, bf16[64,768]{1,0:T(8,128)(2,1)}, u32[]{:S(2)}, u32[]{:S(2)}) collective-permute-start(bf16[64,768]{1,0:T(8,128)(2,1)S(1)} %select_bitcast_fusion.4.refs_0_.refs_4_), channel_id=1, source_target_pairs={{0,4},{4,0},{8,12},{12,8},{1,5},{5,1},{9,13},{13,9},{2,6},{6,2},{1... | collective-permute-start | bytes 294920 | tf_op jit(solution)/shard_map/ppermute | solution.py:37
  133.9 10.7 %collective-permute-start.41 = (bf16[64,768]{1,0:T(8,128)(2,1)S(1)}, bf16[64,768]{1,0:T(8,128)(2,1)}, u32[]{:S(2)}, u32[]{:S(2)}) collective-permute-start(bf16[64,768]{1,0:T(8,128)(2,1)S(1)} %select_bitcast_fusion.4.refs_0_.refs_4_), channel_id=1, source_target_pairs={{0,8},{4,12},{8,0},{12,4},{1,9},{5,13},{9,1},{13,5},{2,10},{6,14},... | collective-permute-start | bytes 294920 | tf_op jit(solution)/shard_map/ppermute | solution.py:37
  134.5 10.0 %collective-permute-start.42 = (bf16[64,768]{1,0:T(8,128)(2,1)S(1)}, bf16[64,768]{1,0:T(8,128)(2,1)}, u32[]{:S(2)}, u32[]{:S(2)}) collective-permute-start(bf16[64,768]{1,0:T(8,128)(2,1)S(1)} %select_bitcast_fusion.4.refs_0_.refs_4_), channel_id=1, source_target_pairs={{0,12},{4,8},{8,4},{12,0},{1,13},{5,9},{9,5},{13,1},{2,14},{6,10},... | collective-permute-start | bytes 294920 | tf_op jit(solution)/shard_map/ppermute | solution.py:37
  141.0 7.6 %collective-permute-start.36 = (bf16[64,768]{1,0:T(8,128)(2,1)S(1)}, bf16[64,768]{1,0:T(8,128)(2,1)S(1)}, u32[]{:S(2)}, u32[]{:S(2)}) collective-permute-start(bf16[64,768]{1,0:T(8,128)(2,1)S(1)} %get-tuple-element.128), channel_id=1, source_target_pairs={{0,4},{4,0},{8,12},{12,8},{1,5},{5,1},{9,13},{13,9},{2,6},{6,2},{1... | collective-permute-start | bytes 294920 | tf_op jit(solution)/shard_map/ppermute | solution.py:30
  143.0 7.5 %collective-permute-start.37 = (bf16[64,768]{1,0:T(8,128)(2,1)S(1)}, bf16[64,768]{1,0:T(8,128)(2,1)S(1)}, u32[]{:S(2)}, u32[]{:S(2)}) collective-permute-start(bf16[64,768]{1,0:T(8,128)(2,1)S(1)} %get-tuple-element.129), channel_id=1, source_target_pairs={{0,8},{4,12},{8,0},{12,4},{1,9},{5,13},{9,1},{13,5},{2,10},{6,14},... | collective-permute-start | bytes 294920 | tf_op jit(solution)/shard_map/ppermute | solution.py:30
  156.3 7.5 %collective-permute-start.47 = (bf16[64,768]{1,0:T(8,128)(2,1)S(1)}, bf16[64,768]{1,0:T(8,128)(2,1)S(1)}, u32[]{:S(2)}, u32[]{:S(2)}) collective-permute-start(bf16[64,768]{1,0:T(8,128)(2,1)S(1)} %get-tuple-element.139.refs_0_), channel_id=1, source_target_pairs={{0,8},{4,12},{8,0},{12,4},{1,9},{5,13},{9,1},{13,5},{2,10},{6,14},... | collective-permute-start | bytes 294920 | tf_op jit(solution)/shard_map/ppermute | solution.py:37
  169.3 111.3 %reduce-scatter.5.cloned.1.call-start = ((), (), s32[]{:S(2)}) async-start(), calls=%async_computation.3 | async-start | bytes 2654208 | tf_op jit(solution)/shard_map/reduce_scatter | solution.py:818
  230.7 11.5 %collective-permute-start.69 = (bf16[768,384]{1,0:T(8,128)(2,1)S(1)}, bf16[768,384]{1,0:T(8,128)(2,1)S(1)}, u32[]{:S(2)}, u32[]{:S(2)}) collective-permute-start(bf16[768,384]{1,0:T(8,128)(2,1)S(1)} %get-tuple-element.184), channel_id=1, source_target_pairs={{0,16},{16,0},{1,17},{17,1},{2,18},{18,2},{3,19},{19,3},{4,20},{20... | collective-permute-start | bytes 1769480 | tf_op jit(solution)/shard_map/ppermute | solution.py:48
  243.8 14.6 %collective-permute-start.72 = (f32[16,192]{1,0:T(8,128)S(1)}, f32[16,192]{1,0:T(8,128)S(1)}, u32[]{:S(2)}, u32[]{:S(2)}) collective-permute-start(f32[16,192]{1,0:T(8,128)S(1)} %get-tuple-element.189), channel_id=1, source_target_pairs={{0,3},{1,2},{2,1},{3,0},{4,7},{5,6},{6,5},{7,4},{8,11},{9,10},{10,... | collective-permute-start | bytes 36872 | tf_op jit(solution)/shard_map/ppermute | solution.py:30
  245.6 12.8 %collective-permute-start.71 = (f32[16,192]{1,0:T(8,128)S(1)}, f32[16,192]{1,0:T(8,128)S(1)}, u32[]{:S(2)}, u32[]{:S(2)}) collective-permute-start(f32[16,192]{1,0:T(8,128)S(1)} %get-tuple-element.188), channel_id=1, source_target_pairs={{0,2},{1,3},{2,0},{3,1},{4,6},{5,7},{6,4},{7,5},{8,10},{9,11},{10,... | collective-permute-start | bytes 36872 | tf_op jit(solution)/shard_map/ppermute | solution.py:30
  254.9 25.5 %collective-permute-start.82 = (bf16[192,384]{1,0:T(8,128)(2,1)S(1)}, bf16[192,384]{1,0:T(8,128)(2,1)S(1)}, u32[]{:S(2)}, u32[]{:S(2)}) collective-permute-start(bf16[192,384]{1,0:T(8,128)(2,1)S(1)} %get-tuple-element.193), channel_id=1, source_target_pairs={{0,3},{1,2},{2,1},{3,0},{4,7},{5,6},{6,5},{7,4},{8,11},{9,10},{10,... | collective-permute-start | bytes 442376 | tf_op jit(solution)/shard_map/ppermute | solution.py:30
  256.4 24.1 %collective-permute-start.81 = (bf16[192,384]{1,0:T(8,128)(2,1)S(1)}, bf16[192,384]{1,0:T(8,128)(2,1)S(1)}, u32[]{:S(2)}, u32[]{:S(2)}) collective-permute-start(bf16[192,384]{1,0:T(8,128)(2,1)S(1)} %get-tuple-element.192), channel_id=1, source_target_pairs={{0,2},{1,3},{2,0},{3,1},{4,6},{5,7},{6,4},{7,5},{8,10},{9,11},{10,... | collective-permute-start | bytes 442376 | tf_op jit(solution)/shard_map/ppermute | solution.py:30
  267.0 13.4 %collective-permute-start.80 = (bf16[192,384]{1,0:T(8,128)(2,1)S(1)}, bf16[192,384]{1,0:T(8,128)(2,1)S(1)}, u32[]{:S(2)}, u32[]{:S(2)}) collective-permute-start(bf16[192,384]{1,0:T(8,128)(2,1)S(1)} %get-tuple-element.191), channel_id=1, source_target_pairs={{0,1},{1,0},{2,3},{3,2},{4,5},{5,4},{6,7},{7,6},{8,9},{9,8},{10,11... | collective-permute-start | bytes 442376 | tf_op jit(solution)/shard_map/ppermute | solution.py:30
  (147 other events, 807.3 us)
Sparse Core Ops, SparseCore 0:
  36.4 47.0 all-gather.4
  85.7 30.7 all-gather.6
  169.4 49.8 reduce-scatter.2
  222.1 34.9 reduce-scatter.4

commit v3 on v2

--- a/solution.py
+++ b/solution.py
@@ -14,6 +14,7 @@
 F32 = jnp.float32
 BF16 = jnp.bfloat16
 SECTION, TENSOR, SLOTS = "section", "tensor", "dp"
+LAYER = (SECTION, TENSOR)
 ROWS = (SLOTS, SECTION)
 SPACE = 40 * 1024 * 1024
 
@@ -46,6 +47,10 @@
 
 def swap(value):
     return lax.ppermute(value, SECTION, [(0, 1), (1, 0)])
+
+
+def across(value, axis):
+    return lax.all_to_all(value, axis, 0, 0)
 
 
 def gather_list(value, axis):
@@ -161,9 +166,9 @@
 
 def assemble(spot, pieces, ref):
     own, other = pieces
-    rows = own[0].shape[0]
-    for k, piece in enumerate(own):
-        for half, block in ((spot[0], piece[...]), (1 - spot[0], other[k])):
+    rows = own.shape[1]
+    for k in range(own.shape[0]):
+        for half, block in ((spot[0], own[k]), (1 - spot[0], other[k])):
             at = pl.multiple_of((2 * spot[3 + k] + half) * rows, rows)
             ref[pl.ds(at, rows), :] = block
 
@@ -282,7 +287,7 @@
 
 
 def attend_back_kernel(layer):
-    def kernel(pieces, packed, kept, refs):
+    def kernel(pieces, packed, kept, others, refs):
         outer_grad = joined(pieces)
         wide = outer_grad.shape[1]
         refs.grads[:, :wide] = outer_grad
@@ -306,13 +311,25 @@
         stacked = jnp.concatenate(d_queries + d_keys + d_values, axis=1).astype(BF16)
         refs.grads[:, wide:] = stacked
         terms = dot(stacked, packed[:, : 3 * width], 1, 1)
-        spread_out(terms, refs.terms)
-        refs.out_bias[...] = column_sum(outer_grad)
-        refs.in_bias[...] = column_sum(stacked)
+        if others is None:
+            spread_out(terms, refs.terms)
+        else:
+            refs.terms[...] = terms
+        in_bias, out_bias = column_sum(stacked), column_sum(outer_grad)
+        refs.out_bias[...] = out_bias
+        refs.in_bias[...] = in_bias
         if layer == 0:
             normed = norm_parts(kept[:, 2 * wide :].astype(F32))[0]
-            refs.rows[0:1] = column_sum(terms)
-            refs.rows[1:2] = column_sum(terms * normed)
+            rows = jnp.concatenate([column_sum(terms), column_sum(terms * normed)], axis=0)
+            if others is None:
+                refs.rows[...] = rows
+            else:
+                middle_rows, mlp_bias, other_rows, other_bias = others
+                mods = [
+                    jnp.concatenate([rows, middle_rows[...]], axis=0),
+                    jnp.concatenate([ref[...] for ref in other_rows], axis=0),
+                ]
+                send_rows(mods, [(in_bias, out_bias, mlp_bias), other_bias], refs.sent)
 
     return kernel
 
@@ -343,66 +360,58 @@
         ].astype(BF16)
 
 
-def mlp_grads_kernel(kept, grads, refs):
+def grads_kernel(mlp_kept, mlp_grads, attn_kept, attn_grads, refs):
     wide = 2 * refs.grads.shape[3]
-    size = grads.shape[1] - wide
-    cut(dot(kept[:, :wide], grads[:, wide:], 0, 0), refs.grads, 0)
-    cut(dot(grads[:, :wide], kept[:, wide : wide + size], 0, 0), refs.grads, 1)
-
-
-def packed_grads(kept, grads, wide):
-    width = wide // 4
-    inner = dot(kept[:, :wide], grads[:, wide:], 0, 0)
-    outer = dot(grads[:, :wide], kept[:, wide + 3 * width : 2 * wide], 0, 0)
-    return jnp.concatenate([inner, outer], axis=1)
-
-
-def attend_grads_kernel(kept, grads, refs):
-    cut(packed_grads(kept, grads, 2 * refs.grads.shape[3]), refs.grads, 0)
-
-
-def attend_halves_kernel(spot, kept, grads, refs):
-    half = refs.kept.shape[1]
-    grad = packed_grads(kept, grads, 2 * half)
-    left, right = grad[:, :half], grad[:, half:]
-    refs.kept[...] = jnp.where(spot[0] == 0, left, right)
-    refs.given[...] = jnp.where(spot[0] == 0, right, left).astype(BF16)
-
-
-def share_kernel(spot, kept, received, refs):
-    rows = refs.own.shape[0]
-    for k, ref in enumerate([refs.own] + refs.sent):
-        at = pl.ds(pl.multiple_of(spot[3 + k] * rows, rows), rows)
-        ref[...] = (kept[at, :] + received[at, :].astype(F32)).astype(ref.dtype)
-
-
-def ordered(spot, at, pieces):
-    result = []
-    for j in range(len(pieces)):
-        chosen = pieces[0]
-        for k in range(1, len(pieces)):
-            chosen = jnp.where(spot[at + k] == j, pieces[k], chosen)
-        result.append(chosen)
-    return result
-
-
-def mods_kernel(spot, mod_pieces, kept, got, refs):
-    count = len(kept)
-    refs.mods[...] = jnp.concatenate(
-        ordered(spot, 3 + count, [ref[...] for ref in mod_pieces]), axis=1
-    )
-    mine = ordered(spot, 3, [ref[...] for ref in kept])
-    theirs = ordered(spot, 3, [got[4 * k : 4 * k + 4] for k in range(count)])
+    size, width = mlp_grads.shape[1] - wide, wide // 4
+    cut(dot(mlp_kept[:, :wide], mlp_grads[:, wide:], 0, 0), refs.grads, 0)
+    cut(dot(mlp_grads[:, :wide], mlp_kept[:, wide : wide + size], 0, 0), refs.grads, 1)
+    inner = dot(attn_kept[:, :wide], attn_grads[:, wide:], 0, 0)
+    outer = dot(attn_grads[:, :wide], attn_kept[:, wide + 3 * width : 2 * wide], 0, 0)
+    cut(jnp.concatenate([inner, outer], axis=1), refs.grads, 2)
+
+
+def mods_kernel(spot, got, refs):
+    cuts = got.shape[0] // 2
+    count = (got.shape[1] - 6) // 4
     cols = refs.inner[0].shape[1] // count
     for layer in range(2):
-        pieces = [
-            jnp.where(spot[0] == layer, first, second) for first, second in zip(mine, theirs)
-        ]
+        refs.mods[6 * layer : 6 * layer + 6] = jnp.concatenate(
+            [got[cuts * layer + t, :6] for t in range(cuts)], axis=1
+        )
+        rows = got[cuts * layer + spot[1], 6:]
+        pieces = [rows[4 * k : 4 * k + 4] for k in range(count)]
         refs.biases[layer][...] = jnp.concatenate(pieces, axis=1)
         for k in range(2):
             refs.inner[layer][k : k + 1] = jnp.concatenate(
                 [piece[0:1, k * cols : (k + 1) * cols] for piece in pieces], axis=1
             )
+
+
+def bias_rows_of(part, rows, shards, in_bias, out_bias, mlp_bias):
+    cols = part // shards
+    pieces = []
+    for z in range(shards):
+        start = jnp.concatenate(
+            [
+                in_bias[:, z * cols : (z + 1) * cols],
+                in_bias[:, 2 * part + z * cols : 2 * part + (z + 1) * cols],
+                jnp.zeros((1, rows - 2 * cols), F32),
+            ],
+            axis=1,
+        )
+        at = slice(z * rows, (z + 1) * rows)
+        pieces += [start, mlp_bias[0:1, at], out_bias[:, at], mlp_bias[1:2, at]]
+    return jnp.concatenate(pieces, axis=0)
+
+
+def send_rows(mods, biases, sent):
+    cuts, part = sent.shape[0] // 2, sent.shape[2]
+    shards = (sent.shape[1] - 6) // 4
+    for layer in range(2):
+        rows = bias_rows_of(part, part, shards, *biases[layer])
+        for t in range(cuts):
+            sent[cuts * layer + t, :6] = mods[layer][:, t * part : (t + 1) * part]
+            sent[cuts * layer + t, 6:] = rows
 
 
 def pack_kernel(spot, mod_one, mod_two, bias_one, bias_two, refs):
@@ -417,65 +426,80 @@
         for j in range(1, cuts):
             chosen = jnp.where(index == j, blocks[j], chosen)
         ref[...] = chosen
-    packs = []
-    for in_bias, out_bias, mlp_bias in (bias_one, bias_two):
-        shards = refs.kept.shape[0]
-        rows = refs.kept.shape[2]
-        cols = part // shards
-        pieces = []
+    shards, _, rows = refs.kept.shape
+    first = bias_rows_of(part, rows, shards, *bias_one)
+    second = bias_rows_of(part, rows, shards, *bias_two)
+    for z in range(shards):
+        at = slice(4 * z, 4 * z + 4)
+        refs.kept[z] = jnp.where(core == 0, first[at], second[at])
+        refs.given[z] = jnp.where(core == 0, second[at], first[at])
+
+
+def bundle_kernel(members):
+    def kernel(spot, kept, got, refs):
+        for k, (weight, layer) in enumerate(members):
+            refs.rows[k] = jnp.where(spot[0] == layer, kept[weight], got[weight])
+
+    return kernel
+
+
+def slots_kernel(spot, received, refs):
+    cuts = received.shape[0] // 2
+    shards = (received.shape[1] - 6) // 4
+    mods = []
+    for micro in range(2):
+        total = received[cuts * micro, :6]
+        for t in range(1, cuts):
+            total = total + received[cuts * micro + t, :6]
+        mods.append(total)
+    here = spot[1]
+    biases = received[here, 6:] + received[cuts + here, 6:]
+    for k, ref in enumerate(refs.sent):
+        ref[:6], ref[6:12] = mods
+        total = biases[:4]
+        for z in range(1, shards):
+            total = jnp.where(spot[3 + k] == z, biases[4 * z : 4 * z + 4], total)
+        ref[12:16] = total
+
+
+def modulate_kernel(act, weights, mod_bias, own, refs):
+    shards, _, part = refs.sent.shape
+    micro = act.shape[0] // shards
+    for k in range(6):
+        terms = dot(act[...], weights[k], 1, 0) + mod_bias[k : k + 1]
         for z in range(shards):
-            start = jnp.concatenate(
-                [
-                    in_bias[:, z * cols : (z + 1) * cols],
-                    in_bias[:, 2 * part + z * cols : 2 * part + (z + 1) * cols],
-                    jnp.zeros((1, rows - 2 * cols), F32),
-                ],
-                axis=1,
-            )
-            here_rows = slice(z * rows, (z + 1) * rows)
-            pieces.append(
-                jnp.concatenate(
-                    [start, mlp_bias[0:1, here_rows], out_bias[:, here_rows], mlp_bias[1:2, here_rows]],
-                    axis=0,
-                )
-            )
-        packs.append(pieces)
-    for z in range(refs.kept.shape[0]):
-        refs.kept[z] = jnp.where(core == 0, packs[0][z], packs[1][z])
-        refs.given[z] = jnp.where(core == 0, packs[1][z], packs[0][z])
-
-
-def bundle_kernel(layers):
-    def kernel(spot, kept, got, refs):
-        for k, layer in enumerate(layers):
-            refs.rows[k] = jnp.where(spot[0] == layer, kept[k][...], got[k][...])
-
-    return kernel
-
-
-def stack_kernel(pieces, refs):
-    for k, piece in enumerate(pieces):
-        refs.stack[k] = piece[...]
-
-
-def turn_kernel(spot, mod_pieces, given, refs):
-    total = summed(mod_pieces)
-    first, second = total[:6], total[6:]
-    refs.kept[...] = jnp.where(spot[0] == 0, first, second)
-    refs.given[:6] = jnp.where(spot[0] == 0, second, first)
-    for z in range(given.shape[0]):
-        refs.given[6 + 4 * z : 10 + 4 * z] = given[z]
-
-
-def slots_kernel(spot, mod_kept, kept, received, refs):
-    mine, theirs = mod_kept[...], received[:6]
-    for k, ref in enumerate(refs.sent):
-        ref[:6] = jnp.where(spot[0] == 0, mine, theirs)
-        ref[6:12] = jnp.where(spot[0] == 0, theirs, mine)
-        total = kept[0] + received[6:10]
-        for z in range(1, kept.shape[0]):
-            total = jnp.where(spot[3 + k] == z, kept[z] + received[6 + 4 * z : 10 + 4 * z], total)
-        ref[12:16] = total
+            for m in range(micro):
+                at = z * micro + m
+                refs.sent[z, 6 * m + k : 6 * m + k + 1] = terms[at : at + 1]
+    for z in range(shards):
+        refs.sent[z, 6 * micro :] = own[...]
+
+
+def assemble_kernel(spot, first, second, given, refs):
+    wide = []
+    for k in range(3):
+        own = jnp.where(spot[0] == 0, first[k], second[k]).astype(F32)
+        other = given[k].astype(F32)
+        left, right = jnp.where(spot[0] == 0, own, other), jnp.where(spot[0] == 0, other, own)
+        wide.append(jnp.concatenate([left, right], axis=1))
+    refs.upper[...], refs.lower[...] = wide[0], wide[1]
+    width = wide[2].shape[1] // 4
+    for k in range(3):
+        refs.inner[k] = wide[2][:, k * width : (k + 1) * width]
+    refs.outer[...] = wide[2][:, 3 * width :].T
+
+
+def split_kernel(terms, refs):
+    spread_out(terms[...], refs.terms)
+
+
+def prepare_kernel(spot, inner, outer, upper, lower, refs):
+    half = upper.shape[0] // 2
+    packed = jnp.concatenate([inner[0], inner[1], inner[2], outer[...].T], axis=1)
+    for k, member in enumerate((packed, upper[...], lower[...])):
+        first, second = member[:half], member[half:]
+        refs.kept[k] = jnp.where(spot[0] == 0, first, second)
+        refs.given[k] = jnp.where(spot[0] == 0, second, first)
 
 
 def sinus_features(stamps, columns):
@@ -526,22 +550,36 @@
         + [partner(TENSOR, k) for k in range(cuts)]
     ).astype(jnp.int32)
 
-    packed_own = jnp.concatenate(
-        [project_in[0, :, 0], project_in[0, :, 1], project_in[0, :, 2], project_out[0].T], axis=1
-    )
-    stack = [packed_own, up_weight[0], down_weight[0].T]
     half = rows // 2
-    given = swap(jnp.concatenate([pick(member[half:], member[:half]) for member in stack]))
-    kept_halves = [pick(member[:half], member[half:]) for member in stack]
-    got_halves = [given[k * half : (k + 1) * half] for k in range(3)]
+    if near:
+        inner = jnp.moveaxis(project_in[0], 1, 0)
+        ready = run(
+            prepare_kernel,
+            Named(kept=shaped((3, half, width), BF16), given=shaped((3, half, width), BF16)),
+            spot,
+            inner,
+            project_out[0],
+            up_weight[0],
+            down_weight[0].T,
+        )
+        given = swap(ready.given)
+        kept_halves, got_halves = ready.kept, given
+    else:
+        packed_own = jnp.concatenate(
+            [project_in[0, :, 0], project_in[0, :, 1], project_in[0, :, 2], project_out[0].T], axis=1
+        )
+        stack = [packed_own, up_weight[0], down_weight[0].T]
+        given = swap(jnp.concatenate([pick(member[half:], member[:half]) for member in stack]))
+        kept_halves = [pick(member[:half], member[half:]) for member in stack]
+        got_halves = [given[k * half : (k + 1) * half] for k in range(3)]
 
     def bundle(members, wait):
         return run(
-            bundle_kernel([layer for _, layer in members]),
+            bundle_kernel(members),
             Named(rows=shaped((len(members), half, width), BF16)),
             spot,
-            [kept_halves[k] for k, _ in members],
-            [got_halves[k] for k, _ in members],
+            kept_halves,
+            got_halves,
             wait=wait,
         ).rows
 
@@ -563,7 +601,7 @@
 
     stamps = jnp.concatenate([labels.reshape(1, -1), timesteps.reshape(1, -1)], axis=1)
     if near:
-        stamps = jnp.concatenate(gather_list(stamps, SLOTS), axis=0)
+        stamps = place(gather_list(stamps, SLOTS), SLOTS).reshape(shards, -1)
     else:
         stamps = lax.all_gather(stamps, SLOTS, axis=0, tiled=True)
     flat_labels = stamps[:, :micro_count].reshape(-1)
@@ -604,23 +642,21 @@
         axis=0,
     )
     if near:
-        got = exchange_list(
-            [jnp.concatenate([mod_terms[k], bias_own], axis=0) for k in range(shards)], SLOTS
-        )
-        mod_sum = sum(member[: micro_count * 6] for member in got)
-        bias_list = [member[micro_count * 6 :] for member in got]
-    else:
-        mod_sum = lax.psum_scatter(mod_terms, SLOTS, scatter_dimension=0, tiled=False)
-        bias_all = lax.all_gather(bias_own, SLOTS, axis=0)
-    if near:
-        received = swap(jnp.concatenate([pick(mod_sum[6:], mod_sum[:6])] + bias_list, axis=0))
-        mod_got, bias_got = received[:6], received[6:]
-    else:
-        mod_got, bias_got = swap(pick(mod_sum[6:], mod_sum[:6])), swap(bias_all)
-    mod_kept = pick(mod_sum[:6], mod_sum[6:])
-    mod_both = jnp.concatenate([pick(mod_kept, mod_got), pick(mod_got, mod_kept)], axis=0)
-    mod_list = gather_list(mod_both, TENSOR)
-    if near:
+        sent = run(
+            modulate_kernel,
+            Named(sent=shaped((shards, 6 * micro_count + 4, part), F32)),
+            act_rows,
+            jnp.moveaxis(modulate_weight[0], 1, 0),
+            bias_full,
+            bias_own,
+        ).sent
+        got = across(sent, SLOTS)
+        mod_sum = jnp.sum(got[:, : micro_count * 6], axis=0).reshape(micro_count, 6, part)
+        bias_all = jnp.broadcast_to(
+            got[:, micro_count * 6 :].reshape(1, 4 * shards, part), (micro_count, 4 * shards, part)
+        )
+        sent = jnp.concatenate([mod_sum, bias_all], axis=1)
+        got_all = across(jnp.repeat(sent, cuts, axis=0), LAYER)
         ready = run(
             mods_kernel,
             Named(
@@ -629,12 +665,16 @@
                 inner=[shaped((2, part), F32)] * 2,
             ),
             spot,
-            mod_list,
-            bias_list,
-            bias_got,
+            got_all,
         )
         mods, biases, in_biases = ready.mods, ready.biases, ready.inner
     else:
+        mod_sum = lax.psum_scatter(mod_terms, SLOTS, scatter_dimension=0, tiled=False)
+        bias_all = lax.all_gather(bias_own, SLOTS, axis=0)
+        mod_got, bias_got = swap(pick(mod_sum[6:], mod_sum[:6])), swap(bias_all)
+        mod_kept = pick(mod_sum[:6], mod_sum[6:])
+        mod_both = jnp.concatenate([pick(mod_kept, mod_got), pick(mod_got, mod_kept)], axis=0)
+        mod_list = gather_list(mod_both, TENSOR)
         mods = jnp.moveaxis(place(mod_list, TENSOR), 0, 1).reshape(12, width)
         in_biases, biases = [], []
         for member in (pick(bias_all, bias_got), pick(bias_got, bias_all)):
@@ -643,16 +683,9 @@
             in_biases.append(jnp.moveaxis(columns, 0, 1).reshape(2, part))
             biases.append(jnp.moveaxis(member, 0, 1).reshape(4, width))
     if near:
-        stacked_pieces = run(
-            stack_kernel,
-            Named(stack=shaped((shards, half, width), BF16)),
-            first_pieces,
-            wait=tuple(mod_list[1:]),
-        ).stack
-        first_a = (first_pieces, swap(stacked_pieces))
-    first_u, first_d, second_a = gather_blocks(
-        [(1, 0), (2, 0), (0, 1)], tuple(bias_list[1:]) if near else ()
-    )
+        first_stack = jnp.stack(first_pieces)
+        first_a = (first_stack, swap(first_stack))
+    first_u, first_d, second_a = gather_blocks([(1, 0), (2, 0), (0, 1)], (got, *first_pieces[1:]) if near else ())
     weights = [(first_a, first_u, first_d), None]
 
     def terms_out(count=1):
@@ -685,13 +718,14 @@
             flops=attend_flops,
         )
         packs.append(attn.packed if isinstance(packed, tuple) else packed)
+        terms = exchange_list(attn.terms, TENSOR)
         if layer == 0:
-            second_u, second_d = gather_blocks([(1, 1), (2, 1)], (attn.kept,))
+            second_u, second_d = gather_blocks([(1, 1), (2, 1)], tuple(terms[1:]))
             weights[1] = (second_a, second_u, second_d)
         middle = run(
             middle_kernel(layer),
             Named(kept=both_f32, mlp_in=own_b16),
-            exchange_list(attn.terms, TENSOR),
+            terms,
             inputs,
             mods,
             biases[layer],
@@ -725,7 +759,6 @@
     row = shaped((1, width), F32)
     grad_own, pieces = seed_own, seed_list
     mod_rows, bias_rows, blocks, input_grads = [None] * 2, [None] * 2, [None] * 2, [None] * 2
-    wait = ()
     for layer in (1, 0):
         packed, upper, lower = packs[layer], weights[layer][1], weights[layer][2]
         inputs, attn, middle, mlp, last = kept[layer]
@@ -743,13 +776,6 @@
             mlp.kept,
             flops=mlp_flops,
         )
-        mlp_grads = run(
-            mlp_grads_kernel,
-            Named(grads=shaped((2 * shards, 2, rows, width // 2), BF16)),
-            mlp.kept,
-            mlp_back.grads,
-            flops=mlp_flops,
-        ).grads
         middle_back = run(
             middle_back_kernel(layer),
             Named(
@@ -769,7 +795,12 @@
             out_bias=row,
             in_bias=shaped((1, 3 * part), F32),
         )
-        if layer == 0:
+        others = None
+        if layer == 0 and near:
+            outs.sent = shaped((2 * cuts, 6 + 4 * shards, part), F32)
+            outs.terms = shaped((tokens, width), F32)
+            others = (middle_back.rows, mlp_back.bias, mod_rows[1], bias_rows[1])
+        elif layer == 0:
             outs.rows = shaped((2, width), F32)
         attn_back = run(
             attend_back_kernel(layer),
@@ -777,112 +808,96 @@
             gather_list(middle_back.outer, TENSOR),
             packed,
             attn.kept,
+            others,
             flops=2 * attend_flops,
-            wait=wait,
-        )
-        operands = (attn.kept, attn_back.grads)
-        if layer == 1 or not near:
-            attn_grads = run(
-                attend_grads_kernel,
-                Named(grads=shaped((2 * shards, 1, rows, width // 2), BF16)),
-                *operands,
-                flops=2 * tokens * width * width,
-            ).grads
-        else:
-            attn_grads = run(
-                attend_halves_kernel,
-                Named(kept=shaped((width, width // 2), F32), given=shaped((width, width // 2), BF16)),
+        )
+        grads = run(
+            grads_kernel,
+            Named(grads=shaped((2 * shards, 3, rows, width // 2), BF16)),
+            mlp.kept,
+            mlp_back.grads,
+            attn.kept,
+            attn_back.grads,
+            flops=mlp_flops + 2 * tokens * width * width,
+        ).grads
+        blocks[layer] = lax.psum_scatter(grads, ROWS, scatter_dimension=0, tiled=False)
+        terms = attn_back.terms
+        if layer == 0 and near:
+            sent = run(
+                slots_kernel,
+                Named(sent=[shaped((16, part), F32)] * shards),
                 spot,
-                *operands,
-                flops=2 * tokens * width * width,
-            )
+                across(attn_back.sent, LAYER),
+            ).sent
+            got = exchange_list(sent, SLOTS)
+            terms = run(
+                split_kernel, Named(terms=terms_out()), terms, wait=(*got[1:], blocks[1])
+            ).terms
         outs = Named(input_grad=own_f32)
         if layer == 1:
             outs.rows, outs.grad, outs.lower = shaped((2, width), F32), own_b16, own_b16
         first_back = run(
             first_back_kernel(layer),
             outs,
-            exchange_list(attn_back.terms, TENSOR),
+            exchange_list(terms, TENSOR),
             middle_back.middle_grad,
             inputs,
             mods,
         )
         input_grads[layer] = first_back.input_grad
-        mod_rows[layer] = [
-            attn_back.rows if layer == 0 else first_back.rows,
-            middle_back.rows,
-        ]
+        if layer == 1 or not near:
+            mod_rows[layer] = [
+                attn_back.rows if layer == 0 else first_back.rows,
+                middle_back.rows,
+            ]
         bias_rows[layer] = (attn_back.in_bias, attn_back.out_bias, mlp_back.bias)
 
-        def scatter(grads):
-            return lax.psum_scatter(grads, ROWS, scatter_dimension=0, tiled=False)
-
         if layer == 1:
-            blocks[1] = scatter(jnp.concatenate([mlp_grads, attn_grads], axis=1))
             grad_own = first_back.grad
             pieces = gather_list(first_back.lower, TENSOR)
-            wait = (blocks[1],)
-        else:
-            mlp_block = scatter(mlp_grads)
-            if near:
-                shares = run(
-                    share_kernel,
-                    Named(
-                        own=shaped((rows, width // 2), F32),
-                        sent=[shaped((rows, width // 2), BF16)] * (shards - 1),
-                    ),
-                    spot,
-                    attn_grads.kept,
-                    swap(attn_grads.given),
-                )
-                got = exchange_list([shares.own] + shares.sent, SLOTS)
-                attn_block = sum(member.astype(F32) for member in got)[None].astype(BF16)
-            else:
-                attn_block = scatter(attn_grads)
-            blocks[0] = jnp.concatenate([mlp_block, attn_block], axis=0)
 
     given = swap(pick(blocks[1], blocks[0]))
-    own = pick(blocks[0], blocks[1])
-    grads = jnp.concatenate([pick(own, given), pick(given, own)], axis=2).astype(F32)
-    grad_upper, grad_lower = grads[0], grads[1].T
-    grad_inner = grads[2, :, : 3 * part].reshape(rows, 3, part)
-    grad_outer = grads[2, :, 3 * part :].T
-
-    tail = run(
-        pack_kernel,
-        Named(mods=[shaped((12, part), F32) for k in range(cuts)],
-            kept=shaped((shards, 4, rows), F32),
-            given=shaped((shards, 4, rows), F32),
-        ),
-        spot,
-        mod_rows[0],
-        mod_rows[1],
-        bias_rows[0],
-        bias_rows[1],
-    )
-    mod_list = exchange_list(tail.mods, TENSOR)
     if near:
-        turned = run(
-            turn_kernel,
-            Named(kept=shaped((6, part), F32), given=shaped((6 + 4 * shards, part), F32)),
+        ready = run(
+            assemble_kernel,
+            Named(
+                upper=shaped((rows, hidden_part), F32),
+                lower=shaped((rows, hidden_part), F32),
+                inner=shaped((3, rows, part), F32),
+                outer=shaped((part, rows), F32),
+            ),
             spot,
-            mod_list,
-            tail.given,
-        )
-        sent = run(
-            slots_kernel,
-            Named(sent=[shaped((16, part), F32)] * shards),
-            spot,
-            turned.kept,
-            tail.kept,
-            swap(turned.given),
-            wait=(shares.own,),
-        ).sent
-        got = exchange_list(sent, SLOTS)
-        mod_slots = jnp.concatenate([member[:12] for member in got], axis=0)
+            blocks[0],
+            blocks[1],
+            given,
+        )
+        grad_upper, grad_lower, grad_outer = ready.upper, ready.lower.T, ready.outer
+        grad_inner = jnp.moveaxis(ready.inner, 0, 1)
+    else:
+        own = pick(blocks[0], blocks[1])
+        grads = jnp.concatenate([pick(own, given), pick(given, own)], axis=2).astype(F32)
+        grad_upper, grad_lower = grads[0], grads[1].T
+        grad_inner = grads[2, :, : 3 * part].reshape(rows, 3, part)
+        grad_outer = grads[2, :, 3 * part :].T
+
+    if near:
+        mod_slots = place([member[:12] for member in got], SLOTS)
         bias_total = sum(member[12:] for member in got)
     else:
-        mod_shard = sum(mod_list)
+        tail = run(
+            pack_kernel,
+            Named(
+                mods=[shaped((12, part), F32) for k in range(cuts)],
+                kept=shaped((shards, 4, rows), F32),
+                given=shaped((shards, 4, rows), F32),
+            ),
+            spot,
+            mod_rows[0],
+            mod_rows[1],
+            bias_rows[0],
+            bias_rows[1],
+        )
+        mod_shard = sum(exchange_list(tail.mods, TENSOR))
         mod_given, mod_kept = pick(mod_shard[6:], mod_shard[:6]), pick(mod_shard[:6], mod_shard[6:])
         mod_got, bias_got = swap(mod_given), swap(tail.given)
         mod_micro = jnp.concatenate([pick(mod_kept, mod_got), pick(mod_got, mod_kept)], axis=0)
@@ -893,24 +908,25 @@
     act_grad = lax.dot_general(
         mod_slots, mod_weight.astype(F32), (((1,), (1,)), ((), ())), precision=HIGH
     )
-    act_grad = act_grad + swap(act_grad)
-    act_grad = sum(gather_list(act_grad, TENSOR))
+    mod_slots = mod_slots + jnp.minimum(jnp.abs(act_grad[:1, :1]), 0.0)
     if near:
-        act_list = []
-        for k, member in enumerate(gather_list(act_grad, SLOTS)):
-            member = member.reshape(shards, micro_count, rows)
-            act_list.append(jnp.concatenate([member[j ^ k] for j in range(shards)], axis=0))
-        act_all = place(act_list, SLOTS)
+        spread = jnp.broadcast_to(act_grad, (2 * cuts, *act_grad.shape))
+        act_grad = jnp.sum(across(spread, LAYER), axis=0)
+        act_all = place(gather_list(act_grad, SLOTS), SLOTS)
     else:
+        act_grad = act_grad + swap(act_grad)
+        act_grad = sum(gather_list(act_grad, TENSOR))
         act_all = lax.all_gather(act_grad, SLOTS, axis=0)
     act_all = jnp.moveaxis(act_all, 0, 1).reshape(-1, width)
     cond_grad = jax.vjp(jax.nn.silu, condition)[1](act_all)[0]
-    table_grad = lax.dot_general(
-        class_hot.astype(F32), cond_grad, (((0,), (0,)), ((), ())), precision=HIGH
-    )
-    time_grad = lax.dot_general(
-        time_feats.astype(F32), cond_grad, (((0,), (0,)), ((), ())), precision=HIGH
-    )
+    pieces = []
+    rest = cond_grad
+    for _ in range(3):
+        pieces.append(rest.astype(BF16))
+        rest = rest - pieces[-1].astype(F32)
+    pieces = jnp.concatenate(pieces, axis=0)
+    table_grad = dot(jnp.concatenate([class_hot.astype(BF16)] * 3, axis=0), pieces, 0, 0)
+    time_grad = dot(jnp.concatenate([time_feats] * 3, axis=0), pieces, 0, 0)
     grad_mod_weight = lax.dot_general(
         act_rows.astype(F32), mod_slots, (((0,), (0,)), ((), ())), precision=HIGH
     ).reshape(rows, 6, part)

time: 297 us -> 279 us (0.939)
  waiting for transfers between devices: 81.8 us -> 65.1 us
  starting transfers between devices: 103 us -> 88.7 us
  blocking collectives: 0 us -> 12.7 us
  local copies, waits for them, and re-layouts: 47 us -> 51.1 us
  other arithmetic: 11.6 us -> 7.86 us
    ppermute x39 -> x33, waiting for transfers between devices: 44.6 us -> 24.1 us  [fetch(): return lax.ppermute(value, axis, [(i, i ^ k) for i in range(size)])]
    ppermute x36 -> x27, starting transfers between devices: 51.2 us -> 33.2 us  [exchange(): return lax.ppermute(value, axis, [(i, i ^ k) for i in range(size)])]
    all_to_all x0 -> x1, blocking collectives: none -> 12.7 us  [across(): return lax.all_to_all(value, axis, 0, 0)]
    all_to_all x0 -> x3, starting transfers between devices: none -> 11.5 us  [across(): return lax.all_to_all(value, axis, 0, 0)]
    all_to_all x0 -> x3, waiting for transfers between devices: none -> 9.44 us  [across(): return lax.all_to_all(value, axis, 0, 0)]
    ppermute x39 -> x33, starting transfers between devices: 50.6 us -> 42.7 us  [fetch(): return lax.ppermute(value, axis, [(i, i ^ k) for i in range(size)])]
    unnamed x170 -> x141, local copies, waits for them, and re-layouts: 40 us -> 44.7 us
    dot_general x2 -> x0, matrix products: 4.55 us -> none  [the longest x1 3.15 us: body(): lax.dot_general(class_hot.astype(F32), cond_grad, (((0,), (0,)), ((), ())...]
  transfers between devices with their start and end apart: 88 -> 72, of which waited for: 48 -> 41; matrix products, arithmetic and copies ran while one was open for 8% -> 8% of each run, Pallas kernels for 8% -> 8%
where the time goes in v3:
time: 279 us; the launch traced here: 278 us
  starting transfers between devices  88.7 us (32%)
  waiting for transfers between devices  65.1 us (23%)
  local copies, waits for them, and re-layouts  51.1 us (18%)
  Pallas kernels  28.9 us (10%)
  between operations  15.2 us (5%)
  blocking collectives  12.7 us (5%)
  matrix products  8.07 us (3%)
  other arithmetic  7.86 us (3%)
    unnamed x141, local copies, waits for them, and re-layouts  44.7 us
    ppermute x33, starting transfers between devices, fetch(): return lax.ppermute(value, axis, [(i, i ^ k) for i in range(size)])  42.7 us
    ppermute x27, starting transfers between devices, exchange(): return lax.ppermute(value, axis, [(i, i ^ k) for i in range(size)])  33.2 us
    ppermute x27, waiting for transfers between devices, exchange(): return lax.ppermute(value, axis, [(i, i ^ k) for i in range(size)])  31.4 us
    pallas_call x26, Pallas kernels, run(): pl.pallas_call(inner, out_shape=out_flat, in_specs=[pl.BlockSpec(memory_s...  28.9 us
    ppermute x33, waiting for transfers between devices, fetch(): return lax.ppermute(value, axis, [(i, i ^ k) for i in range(size)])  24.1 us
    all_to_all x1, blocking collectives, across(): return lax.all_to_all(value, axis, 0, 0)  12.7 us
    all_to_all x3, starting transfers between devices, across(): return lax.all_to_all(value, axis, 0, 0)  11.5 us
  transfers between devices with their start and end apart: 72, of which 41 were waited for; matrix products, arithmetic and copies ran while one was open for 8% of the time, Pallas kernels for 8%

profile of v3, /device:TPU:0, one launch (start us, length us, event | category | flops | bytes accessed | tf_op | source)
XLA Modules:
  0.0 277.7 jit_solution(13119562918727787873)
XLA Ops:
  8.1 3.0 %collective-permute-start.3 = (s32[1,4]{1,0:T(1,128)S(1)}, s32[1,4]{1,0:T(1,128)S(1)}, u32[]{:S(2)}, u32[]{:S(2)}) collective-permute-start(s32[1,4]{1,0:T(1,128)S(1)} %pad_add_fusion), channel_id=1, source_target_pairs={{0,1},{1,0},{2,3},{3,2},{4,5},{5,4},{6,7},{7,6},{8,9},{9,8},{10,11... | collective-permute-start | bytes 56 | tf_op jit(solution)/shard_map/ppermute | solution.py:38
  11.1 2.6 collective-permute-start.4
  23.7 3.9 %collective-permute-start.9 = (bf16[96,768]{1,0:T(8,128)(2,1)S(1)}, bf16[96,768]{1,0:T(8,128)(2,1)S(1)}, u32[]{:S(2)}, u32[]{:S(2)}) collective-permute-start(bf16[96,768]{1,0:T(8,128)(2,1)S(1)} %bitcast.122), channel_id=1, source_target_pairs={{0,3},{1,2},{2,1},{3,0},{4,7},{5,6},{6,5},{7,4},{8,11},{9,10},{10,... | collective-permute-start | bytes 442376 | tf_op jit(solution)/shard_map/ppermute | solution.py:38
  28.6 12.7 %all_to_all.20.refs_3_ = f32[4,16,192]{2,1,0:T(8,128)S(1)} all-to-all(f32[4,16,192]{2,1,0:T(8,128)S(1)} %shard_map.272), channel_id=1, replica_groups=mesh['section'=2,'tensor'=4,'dp'=4] {'dp'}, dimensions={0} | all-to-all | bytes 98304 | tf_op jit(solution)/shard_map/all_to_all | solution.py:53
  45.4 3.8 %all-to-all-start.1 = ((f32[8,22,192]{2,1,0:T(8,128)}), f32[8,22,192]{2,1,0:T(8,128)S(1)}, u32[]{:S(2)}, u32[]{:S(2)}) async-start(f32[8,22,192]{2,1,0:T(8,128)} %bitcast.15), calls=%async_computation.1 | async-start | bytes 393216 | tf_op jit(solution)/shard_map/all_to_all | solution.py:53
  52.8 2.5 all-to-all-done.1.refs_1_
  63.1 2.7 shard_map.275
  68.4 2.5 collective-permute-start.13
  109.1 3.1 %collective-permute-done.22.refs_4_ = bf16[64,768]{1,0:T(8,128)(2,1)S(1)} collective-permute-done((bf16[64,768]{1,0:T(8,128)(2,1)S(1)}, bf16[64,768]{1,0:T(8,128)(2,1)S(1)}, u32[]{:S(2)}, u32[]{:S(2)}) %collective-permute-start.22) | collective-permute-done | bytes 98336 | tf_op jit(solution)/shard_map/ppermute | solution.py:38
  115.5 2.9 %collective-permute-start.25 = (bf16[64,768]{1,0:T(8,128)(2,1)S(1)}, bf16[64,768]{1,0:T(8,128)(2,1)S(1)}, u32[]{:S(2)}, u32[]{:S(2)}) collective-permute-start(bf16[64,768]{1,0:T(8,128)(2,1)S(1)} %get-tuple-element.116), channel_id=1, source_target_pairs={{0,12},{4,8},{8,4},{12,0},{1,13},{5,9},{9,5},{13,1},{2,14},{6,10},... | collective-permute-start | bytes 294920 | tf_op jit(solution)/shard_map/ppermute | solution.py:31
  135.3 2.3 shard_map.283
  149.1 2.9 %collective-permute-done.38.refs_3_ = bf16[64,768]{1,0:T(8,128)(2,1)S(1)} collective-permute-done((bf16[64,768]{1,0:T(8,128)(2,1)S(1)}, bf16[64,768]{1,0:T(8,128)(2,1)S(1)}, u32[]{:S(2)}, u32[]{:S(2)}) %collective-permute-start.38) | collective-permute-done | bytes 98336 | tf_op jit(solution)/shard_map/ppermute | solution.py:31
  154.0 2.5 collective-permute-start.41
  159.6 2.4 shard_map.287
  174.9 2.7 collective-permute-done.44.refs_3_
  181.0 2.9 %collective-permute-start.47 = (bf16[64,768]{1,0:T(8,128)(2,1)S(1)}, bf16[64,768]{1,0:T(8,128)(2,1)S(1)}, u32[]{:S(2)}, u32[]{:S(2)}) collective-permute-start(bf16[64,768]{1,0:T(8,128)(2,1)S(1)} %get-tuple-element.138.refs_0_), channel_id=1, source_target_pairs={{0,12},{4,8},{8,4},{12,0},{1,13},{5,9},{9,5},{13,1},{2,14},{6,10},... | collective-permute-start | bytes 294920 | tf_op jit(solution)/shard_map/ppermute | solution.py:38
  198.3 2.5 collective-permute-done.50.refs_3_
  202.4 2.9 %collective-permute-start.53 = (bf16[64,768]{1,0:T(8,128)(2,1)S(1)}, bf16[64,768]{1,0:T(8,128)(2,1)S(1)}, u32[]{:S(2)}, u32[]{:S(2)}) collective-permute-start(bf16[64,768]{1,0:T(8,128)(2,1)S(1)} %get-tuple-element.146.refs_0_), channel_id=1, source_target_pairs={{0,12},{4,8},{8,4},{12,0},{1,13},{5,9},{9,5},{13,1},{2,14},{6,10},... | collective-permute-start | bytes 294920 | tf_op jit(solution)/shard_map/ppermute | solution.py:38
  207.9 3.3 %shard_map.291 = (bf16[256,1344]{1,0:T(8,128)(2,1)S(1)}, f32[256,768]{1,0:T(8,128)S(1)}, f32[1,768]{1,0:T(1,128)}, f32[1,576]{1,0:T(1,128)}, f32[8,22,192]{2,1,0:T(8,128)}) custom-call(bf16[64,768]{1,0:T(8,128)(2,1)S(1)} %get-tuple-element.146.refs_0_, bf16[64,768]{1,0:T(8,128)(2,1)S(1)} %collective-permute-done.51.refs_1_, ...), custom_call_target="tpu_custom_call" | custom-call | flops 704643072 | bytes 4416000 | tf_op jit(solution)/shard_map/pallas_call | solution.py:98
  217.5 4.3 %all-to-all-start.2 = ((f32[8,22,192]{2,1,0:T(8,128)}), f32[8,22,192]{2,1,0:T(8,128)S(1)}, u32[]{:S(2)}, u32[]{:S(2)}) async-start(f32[8,22,192]{2,1,0:T(8,128)} %get-tuple-element.157), calls=%async_computation.2 | async-start | bytes 393216 | tf_op jit(solution)/shard_map/all_to_all | solution.py:53
  222.5 5.2 %all-to-all-done.2.refs_1_ = f32[8,22,192]{2,1,0:T(8,128)S(1)} async-done(((f32[8,22,192]{2,1,0:T(8,128)}), f32[8,22,192]{2,1,0:T(8,128)S(1)}, u32[]{:S(2)}, u32[]{:S(2)}) %all-to-all-start.2) | async-done | bytes 135200 | tf_op jit(solution)/shard_map/all_to_all | solution.py:53
  232.9 3.2 %collective-permute-done.55.refs_2_ = f32[16,192]{1,0:T(8,128)S(1)} collective-permute-done((f32[16,192]{1,0:T(8,128)S(1)}, f32[16,192]{1,0:T(8,128)S(1)}, u32[]{:S(2)}, u32[]{:S(2)}) %collective-permute-start.55) | collective-permute-done | bytes 12320 | tf_op jit(solution)/shard_map/ppermute | solution.py:31
  239.8 3.4 %all-to-all-start.3 = ((f32[8,8,192]{2,1,0:T(8,128)}), f32[8,8,192]{2,1,0:T(8,128)S(1)}, u32[]{:S(2)}, u32[]{:S(2)}) async-start(f32[8,8,192]{2,1,0:T(8,128)} %broadcast_in_dim.89), calls=%async_computation.4 | async-start | bytes 131072 | tf_op jit(solution)/shard_map/all_to_all | solution.py:53
  253.9 2.4 collective-permute-done.63
  (367 shorter events, 179.8 us)
Async XLA Ops:
  7.2 82.9 %all-gather.5.cloned.1.call-start = ((), (), s32[]{:S(2)}) async-start(), calls=%async_computation.8 | async-start | bytes 3981312 | tf_op jit(solution)/shard_map/all_gather | solution.py:588
  8.1 13.5 %collective-permute-start.3 = (s32[1,4]{1,0:T(1,128)S(1)}, s32[1,4]{1,0:T(1,128)S(1)}, u32[]{:S(2)}, u32[]{:S(2)}) collective-permute-start(s32[1,4]{1,0:T(1,128)S(1)} %pad_add_fusion), channel_id=1, source_target_pairs={{0,1},{1,0},{2,3},{3,2},{4,5},{5,4},{6,7},{7,6},{8,9},{9,8},{10,11... | collective-permute-start | bytes 56 | tf_op jit(solution)/shard_map/ppermute | solution.py:38
  11.1 10.6 %collective-permute-start.4 = (s32[1,4]{1,0:T(1,128)S(1)}, s32[1,4]{1,0:T(1,128)S(1)}, u32[]{:S(2)}, u32[]{:S(2)}) collective-permute-start(s32[1,4]{1,0:T(1,128)S(1)} %pad_add_fusion), channel_id=1, source_target_pairs={{0,2},{1,3},{2,0},{3,1},{4,6},{5,7},{6,4},{7,5},{8,10},{9,11},{10,... | collective-permute-start | bytes 56 | tf_op jit(solution)/shard_map/ppermute | solution.py:38
  13.7 8.0 %collective-permute-start.5 = (s32[1,4]{1,0:T(1,128)S(1)}, s32[1,4]{1,0:T(1,128)S(1)}, u32[]{:S(2)}, u32[]{:S(2)}) collective-permute-start(s32[1,4]{1,0:T(1,128)S(1)} %pad_add_fusion), channel_id=1, source_target_pairs={{0,3},{1,2},{2,1},{3,0},{4,7},{5,6},{6,5},{7,4},{8,11},{9,10},{10,... | collective-permute-start | bytes 56 | tf_op jit(solution)/shard_map/ppermute | solution.py:38
  23.7 17.6 %collective-permute-start.9 = (bf16[96,768]{1,0:T(8,128)(2,1)S(1)}, bf16[96,768]{1,0:T(8,128)(2,1)S(1)}, u32[]{:S(2)}, u32[]{:S(2)}) collective-permute-start(bf16[96,768]{1,0:T(8,128)(2,1)S(1)} %bitcast.122), channel_id=1, source_target_pairs={{0,3},{1,2},{2,1},{3,0},{4,7},{5,6},{6,5},{7,4},{8,11},{9,10},{10,... | collective-permute-start | bytes 442376 | tf_op jit(solution)/shard_map/ppermute | solution.py:38
  27.6 13.7 %collective-permute-start.8 = (bf16[96,768]{1,0:T(8,128)(2,1)S(1)}, bf16[96,768]{1,0:T(8,128)(2,1)S(1)}, u32[]{:S(2)}, u32[]{:S(2)}) collective-permute-start(bf16[96,768]{1,0:T(8,128)(2,1)S(1)} %bitcast.123), channel_id=1, source_target_pairs={{0,2},{1,3},{2,0},{3,1},{4,6},{5,7},{6,4},{7,5},{8,10},{9,11},{10,... | collective-permute-start | bytes 442376 | tf_op jit(solution)/shard_map/ppermute | solution.py:38
  27.6 13.7 %collective-permute-start.7 = (bf16[96,768]{1,0:T(8,128)(2,1)S(1)}, bf16[96,768]{1,0:T(8,128)(2,1)S(1)}, u32[]{:S(2)}, u32[]{:S(2)}) collective-permute-start(bf16[96,768]{1,0:T(8,128)(2,1)S(1)} %bitcast.124), channel_id=1, source_target_pairs={{0,1},{1,0},{2,3},{3,2},{4,5},{5,4},{6,7},{7,6},{8,9},{9,8},{10,11... | collective-permute-start | bytes 442376 | tf_op jit(solution)/shard_map/ppermute | solution.py:38
  44.5 15.8 %collective-permute-start.10 = (bf16[4,96,768]{2,1,0:T(8,128)(2,1)S(1)}, bf16[4,96,768]{2,1,0:T(8,128)(2,1)}, u32[]{:S(2)}, u32[]{:S(2)}) collective-permute-start(bf16[4,96,768]{2,1,0:T(8,128)(2,1)S(1)} %pad_maximum_fusion.refs_6_), channel_id=1, source_target_pairs={{0,16},{16,0},{1,17},{17,1},{2,18},{18,2},{3,19},{19,3},{4,20},{20... | collective-permute-start | bytes 1769480 | tf_op jit(solution)/shard_map/ppermute | solution.py:49
  45.4 10.0 %all-to-all-start.1 = ((f32[8,22,192]{2,1,0:T(8,128)}), f32[8,22,192]{2,1,0:T(8,128)S(1)}, u32[]{:S(2)}, u32[]{:S(2)}) async-start(f32[8,22,192]{2,1,0:T(8,128)} %bitcast.15), calls=%async_computation.1 | async-start | bytes 393216 | tf_op jit(solution)/shard_map/all_to_all | solution.py:53
  49.2 83.3 %all-gather.7.cloned.1.call-start = ((), (), s32[]{:S(2)}) async-start(), calls=%async_computation.9 | async-start | bytes 2654208 | tf_op jit(solution)/shard_map/all_gather | solution.py:588
  49.2 7.8 %collective-permute-start = (bf16[64,768]{1,0:T(8,128)(2,1)S(1)}, bf16[64,768]{1,0:T(8,128)(2,1)S(1)}, u32[]{:S(2)}, u32[]{:S(2)}) collective-permute-start(bf16[64,768]{1,0:T(8,128)(2,1)S(1)} %select_bitcast_fusion.5.refs_1_.refs_4_.refs_5_), channel_id=1, source_target_pairs={{0,4},{4,0},{8,12},{12,8},{1,5},{5,1},{9,13},{13,9},{2,6},{6,2},{1... | collective-permute-start | bytes 294920 | tf_op jit(solution)/shard_map/ppermute | solution.py:38
  52.7 6.9 %collective-permute-start.2 = (bf16[64,768]{1,0:T(8,128)(2,1)S(1)}, bf16[64,768]{1,0:T(8,128)(2,1)S(1)}, u32[]{:S(2)}, u32[]{:S(2)}) collective-permute-start(bf16[64,768]{1,0:T(8,128)(2,1)S(1)} %select_bitcast_fusion.5.refs_1_.refs_4_.refs_5_), channel_id=1, source_target_pairs={{0,12},{4,8},{8,4},{12,0},{1,13},{5,9},{9,5},{13,1},{2,14},{6,10},... | collective-permute-start | bytes 294920 | tf_op jit(solution)/shard_map/ppermute | solution.py:38
  68.0 6.6 %collective-permute-start.12 = (bf16[64,768]{1,0:T(8,128)(2,1)S(1)}, bf16[64,768]{1,0:T(8,128)(2,1)S(1)}, u32[]{:S(2)}, u32[]{:S(2)}) collective-permute-start(bf16[64,768]{1,0:T(8,128)(2,1)S(1)} %get-tuple-element.101), channel_id=1, source_target_pairs={{0,8},{4,12},{8,0},{12,4},{1,9},{5,13},{9,1},{13,5},{2,10},{6,14},... | collective-permute-start | bytes 294920 | tf_op jit(solution)/shard_map/ppermute | solution.py:31
  78.2 178.4 %reduce-scatter.3.cloned.1.call-start = ((), (), s32[]{:S(2)}) async-start(), calls=%async_computation.6 | async-start | bytes 3981312 | tf_op jit(solution)/shard_map/reduce_scatter | solution.py:823
  123.4 8.2 %collective-permute-start.26 = (bf16[64,768]{1,0:T(8,128)(2,1)}, bf16[64,768]{1,0:T(8,128)(2,1)S(1)}, u32[]{:S(2)}, u32[]{:S(2)}) collective-permute-start(bf16[64,768]{1,0:T(8,128)(2,1)} %get-tuple-element.118.refs_0_), channel_id=1, source_target_pairs={{0,4},{4,0},{8,12},{12,8},{1,5},{5,1},{9,13},{13,9},{2,6},{6,2},{1... | collective-permute-start | bytes 294920 | tf_op jit(solution)/shard_map/ppermute | solution.py:38
  124.5 8.0 %collective-permute-start.27 = (bf16[64,768]{1,0:T(8,128)(2,1)}, bf16[64,768]{1,0:T(8,128)(2,1)}, u32[]{:S(2)}, u32[]{:S(2)}) collective-permute-start(bf16[64,768]{1,0:T(8,128)(2,1)} %get-tuple-element.118.refs_0_), channel_id=1, source_target_pairs={{0,8},{4,12},{8,0},{12,4},{1,9},{5,13},{9,1},{13,5},{2,10},{6,14},... | collective-permute-start | bytes 294920 | tf_op jit(solution)/shard_map/ppermute | solution.py:38
  128.2 12.5 %collective-permute-start.33 = (bf16[64,768]{1,0:T(8,128)(2,1)S(1)}, bf16[64,768]{1,0:T(8,128)(2,1)}, u32[]{:S(2)}, u32[]{:S(2)}) collective-permute-start(bf16[64,768]{1,0:T(8,128)(2,1)S(1)} %select_bitcast_fusion.2.refs_0_.refs_4_), channel_id=1, source_target_pairs={{0,4},{4,0},{8,12},{12,8},{1,5},{5,1},{9,13},{13,9},{2,6},{6,2},{1... | collective-permute-start | bytes 294920 | tf_op jit(solution)/shard_map/ppermute | solution.py:38
  129.6 11.6 %collective-permute-start.34 = (bf16[64,768]{1,0:T(8,128)(2,1)S(1)}, bf16[64,768]{1,0:T(8,128)(2,1)}, u32[]{:S(2)}, u32[]{:S(2)}) collective-permute-start(bf16[64,768]{1,0:T(8,128)(2,1)S(1)} %select_bitcast_fusion.2.refs_0_.refs_4_), channel_id=1, source_target_pairs={{0,8},{4,12},{8,0},{12,4},{1,9},{5,13},{9,1},{13,5},{2,10},{6,14},... | collective-permute-start | bytes 294920 | tf_op jit(solution)/shard_map/ppermute | solution.py:38
  132.3 8.9 %collective-permute-start.35 = (bf16[64,768]{1,0:T(8,128)(2,1)S(1)}, bf16[64,768]{1,0:T(8,128)(2,1)}, u32[]{:S(2)}, u32[]{:S(2)}) collective-permute-start(bf16[64,768]{1,0:T(8,128)(2,1)S(1)} %select_bitcast_fusion.2.refs_0_.refs_4_), channel_id=1, source_target_pairs={{0,12},{4,8},{8,4},{12,0},{1,13},{5,9},{9,5},{13,1},{2,14},{6,10},... | collective-permute-start | bytes 294920 | tf_op jit(solution)/shard_map/ppermute | solution.py:38
  137.6 8.8 %collective-permute-start.29 = (bf16[64,768]{1,0:T(8,128)(2,1)S(1)}, bf16[64,768]{1,0:T(8,128)(2,1)S(1)}, u32[]{:S(2)}, u32[]{:S(2)}) collective-permute-start(bf16[64,768]{1,0:T(8,128)(2,1)S(1)} %get-tuple-element.120), channel_id=1, source_target_pairs={{0,4},{4,0},{8,12},{12,8},{1,5},{5,1},{9,13},{13,9},{2,6},{6,2},{1... | collective-permute-start | bytes 294920 | tf_op jit(solution)/shard_map/ppermute | solution.py:31
  138.7 8.1 %collective-permute-start.30 = (bf16[64,768]{1,0:T(8,128)(2,1)S(1)}, bf16[64,768]{1,0:T(8,128)(2,1)S(1)}, u32[]{:S(2)}, u32[]{:S(2)}) collective-permute-start(bf16[64,768]{1,0:T(8,128)(2,1)S(1)} %get-tuple-element.121), channel_id=1, source_target_pairs={{0,8},{4,12},{8,0},{12,4},{1,9},{5,13},{9,1},{13,5},{2,10},{6,14},... | collective-permute-start | bytes 294920 | tf_op jit(solution)/shard_map/ppermute | solution.py:31
  167.8 97.7 %reduce-scatter.5.cloned.1.call-start = ((), (), s32[]{:S(2)}) async-start(), calls=%async_computation.7 | async-start | bytes 3981312 | tf_op jit(solution)/shard_map/reduce_scatter | solution.py:823
  217.5 10.3 %all-to-all-start.2 = ((f32[8,22,192]{2,1,0:T(8,128)}), f32[8,22,192]{2,1,0:T(8,128)S(1)}, u32[]{:S(2)}, u32[]{:S(2)}) async-start(f32[8,22,192]{2,1,0:T(8,128)} %get-tuple-element.157), calls=%async_computation.2 | async-start | bytes 393216 | tf_op jit(solution)/shard_map/all_to_all | solution.py:53
  239.8 8.2 %all-to-all-start.3 = ((f32[8,8,192]{2,1,0:T(8,128)}), f32[8,8,192]{2,1,0:T(8,128)S(1)}, u32[]{:S(2)}, u32[]{:S(2)}) async-start(f32[8,8,192]{2,1,0:T(8,128)} %broadcast_in_dim.89), calls=%async_computation.4 | async-start | bytes 131072 | tf_op jit(solution)/shard_map/all_to_all | solution.py:53
  (118 other events, 565.6 us)
Sparse Core Ops, SparseCore 0:
  43.5 41.6 all-gather.4
  87.4 30.4 all-gather.6
  167.9 44.1 reduce-scatter.2
  215.3 45.6 reduce-scatter.4

commit v4 on v3

--- a/solution.py
+++ b/solution.py
@@ -54,11 +54,13 @@
 
 
 def gather_list(value, axis):
-    return [value] + [fetch(value, axis, k) for k in range(1, lax.axis_size(axis))]
+    got = {k: fetch(value, axis, k) for k in reversed(range(1, lax.axis_size(axis)))}
+    return [value] + [got[k] for k in range(1, lax.axis_size(axis))]
 
 
 def exchange_list(values, axis):
-    return [values[0]] + [exchange(values[k], axis, k) for k in range(1, lax.axis_size(axis))]
+    got = {k: exchange(values[k], axis, k) for k in reversed(range(1, lax.axis_size(axis)))}
+    return [values[0]] + [got[k] for k in range(1, lax.axis_size(axis))]
 
 
 def place(pieces, axis):
@@ -475,6 +477,29 @@
         refs.sent[z, 6 * micro :] = own[...]
 
 
+def act_kernel(spot, pieces, weights, refs):
+    shards = len(pieces)
+    blocks = []
+    for z in range(shards):
+        chosen = pieces[0][...]
+        for k in range(1, shards):
+            chosen = jnp.where(spot[3 + k] == z, pieces[k][...], chosen)
+        blocks.append(chosen)
+    total = jnp.zeros(refs.sent.shape[1:], F32)
+    for k in range(6):
+        rest = jnp.concatenate([b[at : at + 1] for b in blocks for at in (k, 6 + k)], axis=0)
+        for _ in range(3):
+            rounded = rest.astype(BF16)
+            total = total + dot(rounded, weights[k], 1, 1)
+            rest = rest - rounded.astype(F32)
+    repeat_rows(total, refs.sent)
+
+
+def repeat_rows(values, ref):
+    for k in range(ref.shape[0]):
+        ref[k] = values
+
+
 def assemble_kernel(spot, first, second, given, refs):
     wide = []
     for k in range(3):
@@ -583,9 +608,13 @@
             wait=wait,
         ).rows
 
+    bundles = []
+
     def gather_blocks(members, wait=()):
         if near:
-            whole = lax.all_gather(bundle(members, wait), ROWS, axis=0)
+            own = bundle(members, wait)
+            bundles.append(own)
+            whole = lax.all_gather(own, ROWS, axis=0)
             return [Part(whole, k) for k in range(len(members))]
         return [
             gather_rows(
@@ -686,7 +715,8 @@
         first_stack = jnp.stack(first_pieces)
         first_a = (first_stack, swap(first_stack))
     first_u, first_d, second_a = gather_blocks([(1, 0), (2, 0), (0, 1)], (got, *first_pieces[1:]) if near else ())
-    weights = [(first_a, first_u, first_d), None]
+    second_u, second_d = gather_blocks([(1, 1), (2, 1)], tuple(bundles))
+    weights = [(first_a, first_u, first_d), (second_a, second_u, second_d)]
 
     def terms_out(count=1):
         return [shaped((own_tokens, width), F32)] + [
@@ -719,9 +749,6 @@
         )
         packs.append(attn.packed if isinstance(packed, tuple) else packed)
         terms = exchange_list(attn.terms, TENSOR)
-        if layer == 0:
-            second_u, second_d = gather_blocks([(1, 1), (2, 1)], tuple(terms[1:]))
-            weights[1] = (second_a, second_u, second_d)
         middle = run(
             middle_kernel(layer),
             Named(kept=both_f32, mlp_in=own_b16),
@@ -831,7 +858,7 @@
             ).sent
             got = exchange_list(sent, SLOTS)
             terms = run(
-                split_kernel, Named(terms=terms_out()), terms, wait=(*got[1:], blocks[1])
+                split_kernel, Named(terms=terms_out()), terms, wait=tuple(got[1:])
             ).terms
         outs = Named(input_grad=own_f32)
         if layer == 1:
@@ -905,15 +932,20 @@
         mod_slots = lax.all_gather(mod_micro, SLOTS, axis=0, tiled=True)
         bias_total = lax.psum_scatter(bias_sum, SLOTS, scatter_dimension=0, tiled=False)
     mod_slots = mod_slots.reshape(shards * micro_count, 6 * part)
-    act_grad = lax.dot_general(
-        mod_slots, mod_weight.astype(F32), (((1,), (1,)), ((), ())), precision=HIGH
-    )
-    mod_slots = mod_slots + jnp.minimum(jnp.abs(act_grad[:1, :1]), 0.0)
     if near:
-        spread = jnp.broadcast_to(act_grad, (2 * cuts, *act_grad.shape))
-        act_grad = jnp.sum(across(spread, LAYER), axis=0)
+        sent = run(
+            act_kernel,
+            Named(sent=shaped((2 * cuts, shards * micro_count, rows), F32)),
+            spot,
+            got,
+            jnp.moveaxis(modulate_weight[0], 1, 0),
+        ).sent
+        act_grad = jnp.sum(across(sent, LAYER), axis=0)
         act_all = place(gather_list(act_grad, SLOTS), SLOTS)
     else:
+        act_grad = lax.dot_general(
+            mod_slots, mod_weight.astype(F32), (((1,), (1,)), ((), ())), precision=HIGH
+        )
         act_grad = act_grad + swap(act_grad)
         act_grad = sum(gather_list(act_grad, TENSOR))
         act_all = lax.all_gather(act_grad, SLOTS, axis=0)

time: 279 us -> 275 us (0.986)
  waiting for transfers between devices: 65.1 us -> 60.8 us
  Pallas kernels: 28.9 us -> 32.6 us
    ppermute x27, waiting for transfers between devices: 31.4 us -> 27.4 us  [exchange(): return lax.ppermute(value, axis, [(i, i ^ k) for i in range(size)])]
    pallas_call x26 -> x27, Pallas kernels: 28.9 us -> 32.6 us  [run(): pl.pallas_call(inner, out_shape=out_flat, in_specs=[pl.BlockSpec(memory_s...]
    unnamed x141 -> x156, local copies, waits for them, and re-layouts: 44.7 us -> 43.9 us
  transfers between devices with their start and end apart: 72 -> 72, of which waited for: 41 -> 41; matrix products, arithmetic and copies ran while one was open for 8% -> 7% of each run, Pallas kernels for 8% -> 9%
where the time goes in v4:
time: 275 us; the launch traced here: 274 us
  starting transfers between devices  86.7 us (32%)
  waiting for transfers between devices  60.8 us (22%)
  local copies, waits for them, and re-layouts  49.1 us (18%)
  Pallas kernels  32.6 us (12%)
  blocking collectives  14.8 us (5%)
  between operations  14.6 us (5%)
  other arithmetic  8.75 us (3%)
  matrix products  6.66 us (2%)
    unnamed x156, local copies, waits for them, and re-layouts  43.9 us
    ppermute x33, starting transfers between devices, fetch(): return lax.ppermute(value, axis, [(i, i ^ k) for i in range(size)])  42.5 us
    ppermute x27, starting transfers between devices, exchange(): return lax.ppermute(value, axis, [(i, i ^ k) for i in range(size)])  32.8 us
    pallas_call x27, Pallas kernels, run(): pl.pallas_call(inner, out_shape=out_flat, in_specs=[pl.BlockSpec(memory_s...  32.6 us
    ppermute x27, waiting for transfers between devices, exchange(): return lax.ppermute(value, axis, [(i, i ^ k) for i in range(size)])  27.4 us
    ppermute x33, waiting for transfers between devices, fetch(): return lax.ppermute(value, axis, [(i, i ^ k) for i in range(size)])  23 us
    all_to_all x1, blocking collectives, across(): return lax.all_to_all(value, axis, 0, 0)  14.8 us
    all_to_all x3, starting transfers between devices, across(): return lax.all_to_all(value, axis, 0, 0)  10.6 us
  transfers between devices with their start and end apart: 72, of which 41 were waited for; matrix products, arithmetic and copies ran while one was open for 7% of the time, Pallas kernels for 9%

profile of v4, /device:TPU:0, one launch (start us, length us, event | category | flops | bytes accessed | tf_op | source)
XLA Modules:
  0.0 274.1 jit_solution(15440885748523915127)
XLA Ops:
  8.1 3.0 %collective-permute-start.3 = (s32[1,4]{1,0:T(1,128)S(1)}, s32[1,4]{1,0:T(1,128)S(1)}, u32[]{:S(2)}, u32[]{:S(2)}) collective-permute-start(s32[1,4]{1,0:T(1,128)S(1)} %pad_add_fusion), channel_id=1, source_target_pairs={{0,1},{1,0},{2,3},{3,2},{4,5},{5,4},{6,7},{7,6},{8,9},{9,8},{10,11... | collective-permute-start | bytes 56 | tf_op jit(solution)/shard_map/ppermute | solution.py:38
  11.1 2.6 collective-permute-start.4
  24.7 3.5 %collective-permute-start.8 = (bf16[96,768]{1,0:T(8,128)(2,1)S(1)}, bf16[96,768]{1,0:T(8,128)(2,1)S(1)}, u32[]{:S(2)}, u32[]{:S(2)}) collective-permute-start(bf16[96,768]{1,0:T(8,128)(2,1)S(1)} %bitcast.116), channel_id=1, source_target_pairs={{0,2},{1,3},{2,0},{3,1},{4,6},{5,7},{6,4},{7,5},{8,10},{9,11},{10,... | collective-permute-start | bytes 442376 | tf_op jit(solution)/shard_map/ppermute | solution.py:38
  28.5 14.8 %all_to_all.20.refs_3_ = f32[4,16,192]{2,1,0:T(8,128)S(1)} all-to-all(f32[4,16,192]{2,1,0:T(8,128)S(1)} %shard_map.272), channel_id=1, replica_groups=mesh['section'=2,'tensor'=4,'dp'=4] {'dp'}, dimensions={0} | all-to-all | bytes 98304 | tf_op jit(solution)/shard_map/all_to_all | solution.py:53
  50.2 3.8 %all-to-all-start.1 = ((f32[8,22,192]{2,1,0:T(8,128)}), f32[8,22,192]{2,1,0:T(8,128)S(1)}, u32[]{:S(2)}, u32[]{:S(2)}) async-start(f32[8,22,192]{2,1,0:T(8,128)} %bitcast.15), calls=%async_computation.1 | async-start | bytes 393216 | tf_op jit(solution)/shard_map/all_to_all | solution.py:53
  57.8 2.4 all-to-all-done.1.refs_1_
  68.9 2.6 shard_map.275
  73.4 2.6 collective-permute-start.13
  136.3 2.3 shard_map.283
  142.2 2.1 shard_map.285
  150.2 2.2 collective-permute-done.38.refs_3_
  162.1 2.4 shard_map.287
  176.8 2.3 collective-permute-done.44.refs_3_
  188.6 2.4 collective-permute-done.47.refs_3_
  211.4 3.3 %shard_map.291 = (bf16[256,1344]{1,0:T(8,128)(2,1)S(1)}, f32[256,768]{1,0:T(8,128)S(1)}, f32[1,768]{1,0:T(1,128)}, f32[1,576]{1,0:T(1,128)}, f32[8,22,192]{2,1,0:T(8,128)}) custom-call(bf16[64,768]{1,0:T(8,128)(2,1)S(1)} %get-tuple-element.146.refs_0_, bf16[64,768]{1,0:T(8,128)(2,1)S(1)} %collective-permute-done.51.refs_1_, ...), custom_call_target="tpu_custom_call" | custom-call | flops 704643072 | bytes 4416000 | tf_op jit(solution)/shard_map/pallas_call | solution.py:100
  219.8 3.4 %all-to-all-start.2 = ((f32[8,22,192]{2,1,0:T(8,128)}), f32[8,22,192]{2,1,0:T(8,128)S(1)}, u32[]{:S(2)}, u32[]{:S(2)}) async-start(f32[8,22,192]{2,1,0:T(8,128)} %get-tuple-element.157), calls=%async_computation.2 | async-start | bytes 393216 | tf_op jit(solution)/shard_map/all_to_all | solution.py:53
  223.9 5.2 %all-to-all-done.2.refs_1_ = f32[8,22,192]{2,1,0:T(8,128)S(1)} async-done(((f32[8,22,192]{2,1,0:T(8,128)}), f32[8,22,192]{2,1,0:T(8,128)S(1)}, u32[]{:S(2)}, u32[]{:S(2)}) %all-to-all-start.2) | async-done | bytes 135200 | tf_op jit(solution)/shard_map/all_to_all | solution.py:53
  231.0 3.1 %collective-permute-start.56 = (f32[16,192]{1,0:T(8,128)S(1)}, f32[16,192]{1,0:T(8,128)S(1)}, u32[]{:S(2)}, u32[]{:S(2)}) collective-permute-start(f32[16,192]{1,0:T(8,128)S(1)} %get-tuple-element.160), channel_id=1, source_target_pairs={{0,3},{1,2},{2,1},{3,0},{4,7},{5,6},{6,5},{7,4},{8,11},{9,10},{10,... | collective-permute-start | bytes 36872 | tf_op jit(solution)/shard_map/ppermute | solution.py:31
  239.1 3.4 %all-to-all-start.3 = ((f32[8,8,192]{2,1,0:T(8,128)}), f32[8,8,192]{2,1,0:T(8,128)S(1)}, u32[]{:S(2)}, u32[]{:S(2)}) async-start(f32[8,8,192]{2,1,0:T(8,128)} %shard_map.295), calls=%async_computation.3 | async-start | bytes 131072 | tf_op jit(solution)/shard_map/all_to_all | solution.py:53
  244.7 2.5 all-to-all-done.3
  248.0 3.0 %collective-permute-start.62 = (f32[8,192]{1,0:T(8,128)S(1)}, f32[8,192]{1,0:T(8,128)S(1)}, u32[]{:S(2)}, u32[]{:S(2)}) collective-permute-start(f32[8,192]{1,0:T(8,128)S(1)} %reduce_sum.28), channel_id=1, source_target_pairs={{0,2},{1,3},{2,0},{3,1},{4,6},{5,7},{6,4},{7,5},{8,10},{9,11},{10,... | collective-permute-start | bytes 18440 | tf_op jit(solution)/shard_map/ppermute | solution.py:38
  255.5 2.4 collective-permute-start.59
  258.3 2.3 fusion
  265.4 2.1 shard_map.298
  (380 shorter events, 179.9 us)
Async XLA Ops:
  7.2 82.1 %all-gather.5.cloned.1.call-start = ((), (), s32[]{:S(2)}) async-start(), calls=%async_computation.8 | async-start | bytes 3981312 | tf_op jit(solution)/shard_map/all_gather | solution.py:617
  8.1 13.5 %collective-permute-start.3 = (s32[1,4]{1,0:T(1,128)S(1)}, s32[1,4]{1,0:T(1,128)S(1)}, u32[]{:S(2)}, u32[]{:S(2)}) collective-permute-start(s32[1,4]{1,0:T(1,128)S(1)} %pad_add_fusion), channel_id=1, source_target_pairs={{0,1},{1,0},{2,3},{3,2},{4,5},{5,4},{6,7},{7,6},{8,9},{9,8},{10,11... | collective-permute-start | bytes 56 | tf_op jit(solution)/shard_map/ppermute | solution.py:38
  11.1 10.5 %collective-permute-start.4 = (s32[1,4]{1,0:T(1,128)S(1)}, s32[1,4]{1,0:T(1,128)S(1)}, u32[]{:S(2)}, u32[]{:S(2)}) collective-permute-start(s32[1,4]{1,0:T(1,128)S(1)} %pad_add_fusion), channel_id=1, source_target_pairs={{0,2},{1,3},{2,0},{3,1},{4,6},{5,7},{6,4},{7,5},{8,10},{9,11},{10,... | collective-permute-start | bytes 56 | tf_op jit(solution)/shard_map/ppermute | solution.py:38
  13.7 8.0 %collective-permute-start.5 = (s32[1,4]{1,0:T(1,128)S(1)}, s32[1,4]{1,0:T(1,128)S(1)}, u32[]{:S(2)}, u32[]{:S(2)}) collective-permute-start(s32[1,4]{1,0:T(1,128)S(1)} %pad_add_fusion), channel_id=1, source_target_pairs={{0,3},{1,2},{2,1},{3,0},{4,7},{5,6},{6,5},{7,4},{8,11},{9,10},{10,... | collective-permute-start | bytes 56 | tf_op jit(solution)/shard_map/ppermute | solution.py:38
  23.7 19.6 %collective-permute-start.7 = (bf16[96,768]{1,0:T(8,128)(2,1)S(1)}, bf16[96,768]{1,0:T(8,128)(2,1)S(1)}, u32[]{:S(2)}, u32[]{:S(2)}) collective-permute-start(bf16[96,768]{1,0:T(8,128)(2,1)S(1)} %bitcast.115), channel_id=1, source_target_pairs={{0,1},{1,0},{2,3},{3,2},{4,5},{5,4},{6,7},{7,6},{8,9},{9,8},{10,11... | collective-permute-start | bytes 442376 | tf_op jit(solution)/shard_map/ppermute | solution.py:38
  24.7 18.6 %collective-permute-start.8 = (bf16[96,768]{1,0:T(8,128)(2,1)S(1)}, bf16[96,768]{1,0:T(8,128)(2,1)S(1)}, u32[]{:S(2)}, u32[]{:S(2)}) collective-permute-start(bf16[96,768]{1,0:T(8,128)(2,1)S(1)} %bitcast.116), channel_id=1, source_target_pairs={{0,2},{1,3},{2,0},{3,1},{4,6},{5,7},{6,4},{7,5},{8,10},{9,11},{10,... | collective-permute-start | bytes 442376 | tf_op jit(solution)/shard_map/ppermute | solution.py:38
  28.2 15.2 %collective-permute-start.9 = (bf16[96,768]{1,0:T(8,128)(2,1)S(1)}, bf16[96,768]{1,0:T(8,128)(2,1)S(1)}, u32[]{:S(2)}, u32[]{:S(2)}) collective-permute-start(bf16[96,768]{1,0:T(8,128)(2,1)S(1)} %bitcast.117), channel_id=1, source_target_pairs={{0,3},{1,2},{2,1},{3,0},{4,7},{5,6},{6,5},{7,4},{8,11},{9,10},{10,... | collective-permute-start | bytes 442376 | tf_op jit(solution)/shard_map/ppermute | solution.py:38
  46.7 87.0 %all-gather.7.cloned.1.call-start = ((), (), s32[]{:S(2)}) async-start(), calls=%async_computation.9 | async-start | bytes 2654208 | tf_op jit(solution)/shard_map/all_gather | solution.py:617
  49.3 15.8 %collective-permute-start.10 = (bf16[4,96,768]{2,1,0:T(8,128)(2,1)S(1)}, bf16[4,96,768]{2,1,0:T(8,128)(2,1)}, u32[]{:S(2)}, u32[]{:S(2)}) collective-permute-start(bf16[4,96,768]{2,1,0:T(8,128)(2,1)S(1)} %pad_maximum_fusion.refs_6_), channel_id=1, source_target_pairs={{0,16},{16,0},{1,17},{17,1},{2,18},{18,2},{3,19},{19,3},{4,20},{20... | collective-permute-start | bytes 1769480 | tf_op jit(solution)/shard_map/ppermute | solution.py:49
  50.2 10.0 %all-to-all-start.1 = ((f32[8,22,192]{2,1,0:T(8,128)}), f32[8,22,192]{2,1,0:T(8,128)S(1)}, u32[]{:S(2)}, u32[]{:S(2)}) async-start(f32[8,22,192]{2,1,0:T(8,128)} %bitcast.15), calls=%async_computation.1 | async-start | bytes 393216 | tf_op jit(solution)/shard_map/all_to_all | solution.py:53
  54.0 207.7 %reduce-scatter.5.cloned.1.call-start = ((), (), s32[]{:S(2)}) async-start(), calls=%async_computation.7 | async-start | bytes 3981312 | tf_op jit(solution)/shard_map/reduce_scatter | solution.py:850
  54.3 7.6 %collective-permute-start = (bf16[64,768]{1,0:T(8,128)(2,1)S(1)}, bf16[64,768]{1,0:T(8,128)(2,1)S(1)}, u32[]{:S(2)}, u32[]{:S(2)}) collective-permute-start(bf16[64,768]{1,0:T(8,128)(2,1)S(1)} %select_bitcast_fusion.5.refs_1_.refs_4_.refs_5_), channel_id=1, source_target_pairs={{0,4},{4,0},{8,12},{12,8},{1,5},{5,1},{9,13},{13,9},{2,6},{6,2},{1... | collective-permute-start | bytes 294920 | tf_op jit(solution)/shard_map/ppermute | solution.py:38
  125.3 8.4 %collective-permute-start.27 = (bf16[64,768]{1,0:T(8,128)(2,1)}, bf16[64,768]{1,0:T(8,128)(2,1)}, u32[]{:S(2)}, u32[]{:S(2)}) collective-permute-start(bf16[64,768]{1,0:T(8,128)(2,1)} %get-tuple-element.118.refs_0_), channel_id=1, source_target_pairs={{0,8},{4,12},{8,0},{12,4},{1,9},{5,13},{9,1},{13,5},{2,10},{6,14},... | collective-permute-start | bytes 294920 | tf_op jit(solution)/shard_map/ppermute | solution.py:38
  126.1 7.6 %collective-permute-start.28 = (bf16[64,768]{1,0:T(8,128)(2,1)}, bf16[64,768]{1,0:T(8,128)(2,1)}, u32[]{:S(2)}, u32[]{:S(2)}) collective-permute-start(bf16[64,768]{1,0:T(8,128)(2,1)} %get-tuple-element.118.refs_0_), channel_id=1, source_target_pairs={{0,12},{4,8},{8,4},{12,0},{1,13},{5,9},{9,5},{13,1},{2,14},{6,10},... | collective-permute-start | bytes 294920 | tf_op jit(solution)/shard_map/ppermute | solution.py:38
  129.6 11.1 %collective-permute-start.33 = (bf16[64,768]{1,0:T(8,128)(2,1)}, bf16[64,768]{1,0:T(8,128)(2,1)}, u32[]{:S(2)}, u32[]{:S(2)}) collective-permute-start(bf16[64,768]{1,0:T(8,128)(2,1)} %select_bitcast_fusion.2.refs_0_.refs_4_), channel_id=1, source_target_pairs={{0,4},{4,0},{8,12},{12,8},{1,5},{5,1},{9,13},{13,9},{2,6},{6,2},{1... | collective-permute-start | bytes 294920 | tf_op jit(solution)/shard_map/ppermute | solution.py:38
  130.7 11.5 %collective-permute-start.34 = (bf16[64,768]{1,0:T(8,128)(2,1)}, bf16[64,768]{1,0:T(8,128)(2,1)}, u32[]{:S(2)}, u32[]{:S(2)}) collective-permute-start(bf16[64,768]{1,0:T(8,128)(2,1)} %select_bitcast_fusion.2.refs_0_.refs_4_), channel_id=1, source_target_pairs={{0,8},{4,12},{8,0},{12,4},{1,9},{5,13},{9,1},{13,5},{2,10},{6,14},... | collective-permute-start | bytes 294920 | tf_op jit(solution)/shard_map/ppermute | solution.py:38
  132.2 10.0 %collective-permute-start.35 = (bf16[64,768]{1,0:T(8,128)(2,1)}, bf16[64,768]{1,0:T(8,128)(2,1)}, u32[]{:S(2)}, u32[]{:S(2)}) collective-permute-start(bf16[64,768]{1,0:T(8,128)(2,1)} %select_bitcast_fusion.2.refs_0_.refs_4_), channel_id=1, source_target_pairs={{0,12},{4,8},{8,4},{12,0},{1,13},{5,9},{9,5},{13,1},{2,14},{6,10},... | collective-permute-start | bytes 294920 | tf_op jit(solution)/shard_map/ppermute | solution.py:38
  138.6 7.8 %collective-permute-start.29 = (bf16[64,768]{1,0:T(8,128)(2,1)S(1)}, bf16[64,768]{1,0:T(8,128)(2,1)S(1)}, u32[]{:S(2)}, u32[]{:S(2)}) collective-permute-start(bf16[64,768]{1,0:T(8,128)(2,1)S(1)} %get-tuple-element.120), channel_id=1, source_target_pairs={{0,4},{4,0},{8,12},{12,8},{1,5},{5,1},{9,13},{13,9},{2,6},{6,2},{1... | collective-permute-start | bytes 294920 | tf_op jit(solution)/shard_map/ppermute | solution.py:31
  139.8 8.1 %collective-permute-start.30 = (bf16[64,768]{1,0:T(8,128)(2,1)S(1)}, bf16[64,768]{1,0:T(8,128)(2,1)S(1)}, u32[]{:S(2)}, u32[]{:S(2)}) collective-permute-start(bf16[64,768]{1,0:T(8,128)(2,1)S(1)} %get-tuple-element.121), channel_id=1, source_target_pairs={{0,8},{4,12},{8,0},{12,4},{1,9},{5,13},{9,1},{13,5},{2,10},{6,14},... | collective-permute-start | bytes 294920 | tf_op jit(solution)/shard_map/ppermute | solution.py:31
  170.5 91.5 %reduce-scatter.3.cloned.1.call-start = ((), (), s32[]{:S(2)}) async-start(), calls=%async_computation.6 | async-start | bytes 3981312 | tf_op jit(solution)/shard_map/reduce_scatter | solution.py:850
  219.8 9.3 %all-to-all-start.2 = ((f32[8,22,192]{2,1,0:T(8,128)}), f32[8,22,192]{2,1,0:T(8,128)S(1)}, u32[]{:S(2)}, u32[]{:S(2)}) async-start(f32[8,22,192]{2,1,0:T(8,128)} %get-tuple-element.157), calls=%async_computation.2 | async-start | bytes 393216 | tf_op jit(solution)/shard_map/all_to_all | solution.py:53
  239.1 8.2 %all-to-all-start.3 = ((f32[8,8,192]{2,1,0:T(8,128)}), f32[8,8,192]{2,1,0:T(8,128)S(1)}, u32[]{:S(2)}, u32[]{:S(2)}) async-start(f32[8,8,192]{2,1,0:T(8,128)} %shard_map.295), calls=%async_computation.3 | async-start | bytes 131072 | tf_op jit(solution)/shard_map/all_to_all | solution.py:53
  247.3 8.2 %collective-permute-start.61 = (f32[8,192]{1,0:T(8,128)S(1)}, f32[8,192]{1,0:T(8,128)S(1)}, u32[]{:S(2)}, u32[]{:S(2)}) collective-permute-start(f32[8,192]{1,0:T(8,128)S(1)} %reduce_sum.28), channel_id=1, source_target_pairs={{0,1},{1,0},{2,3},{3,2},{4,5},{5,4},{6,7},{7,6},{8,9},{9,8},{10,11... | collective-permute-start | bytes 18440 | tf_op jit(solution)/shard_map/ppermute | solution.py:38
  248.0 9.9 %collective-permute-start.62 = (f32[8,192]{1,0:T(8,128)S(1)}, f32[8,192]{1,0:T(8,128)S(1)}, u32[]{:S(2)}, u32[]{:S(2)}) collective-permute-start(f32[8,192]{1,0:T(8,128)S(1)} %reduce_sum.28), channel_id=1, source_target_pairs={{0,2},{1,3},{2,0},{3,1},{4,6},{5,7},{6,4},{7,5},{8,10},{9,11},{10,... | collective-permute-start | bytes 18440 | tf_op jit(solution)/shard_map/ppermute | solution.py:38
  (126 other events, 622.2 us)
Sparse Core Ops, SparseCore 0:
  46.8 41.5 all-gather.4
  90.6 30.4 all-gather.6
  170.6 42.7 reduce-scatter.4
  218.8 43.0 reduce-scatter.2

commit v5 on v4

--- a/solution.py
+++ b/solution.py
@@ -714,7 +714,7 @@
     if near:
         first_stack = jnp.stack(first_pieces)
         first_a = (first_stack, swap(first_stack))
-    first_u, first_d, second_a = gather_blocks([(1, 0), (2, 0), (0, 1)], (got, *first_pieces[1:]) if near else ())
+    first_u, first_d, second_a = gather_blocks([(1, 0), (2, 0), (0, 1)], (got, first_stack) if near else ())
     second_u, second_d = gather_blocks([(1, 1), (2, 1)], tuple(bundles))
     weights = [(first_a, first_u, first_d), (second_a, second_u, second_d)]
 
@@ -731,7 +731,7 @@
 
     kept, packs = [], []
     inputs = tokens_own
-    first = token_list
+    first = [jnp.concatenate(token_list)]
     for layer in range(2):
         packed, upper, lower = weights[layer]
         outs = Named(kept=shaped((tokens, (3 - layer) * width), BF16), terms=terms_out())
@@ -760,7 +760,9 @@
         mlp = run(
             mlp_kernel,
             Named(kept=shaped((tokens, width + 2 * hidden_part), BF16), terms=terms_out()),
-            gather_list(middle.mlp_in, TENSOR),
+            [jnp.concatenate(gather_list(middle.mlp_in, TENSOR))]
+            if layer == 0
+            else gather_list(middle.mlp_in, TENSOR),
             upper,
             lower,
             biases[layer],
@@ -781,7 +783,7 @@
         inputs = last.output
         if layer == 0:
             first = gather_list(last.attn_in, TENSOR)
-            seed_list = gather_list(seed_own, TENSOR)
+            seed_list = [jnp.concatenate(gather_list(seed_own, TENSOR))]
 
     row = shaped((1, width), F32)
     grad_own, pieces = seed_own, seed_list

time: 275 us -> 263 us (0.956)
  blocking collectives: 14.8 us -> 0 us
  local copies, waits for them, and re-layouts: 49.1 us -> 35.4 us
  waiting for transfers between devices: 60.8 us -> 72.1 us
  starting transfers between devices: 86.7 us -> 92.1 us
  Pallas kernels: 32.6 us -> 29.7 us
  other arithmetic: 8.75 us -> 11.6 us
    unnamed x156 -> x104, local copies, waits for them, and re-layouts: 43.9 us -> 28.1 us
    all_to_all x1 -> x0, blocking collectives: 14.8 us -> none  [across(): return lax.all_to_all(value, axis, 0, 0)]
    all_to_all x3 -> x4, starting transfers between devices: 10.6 us -> 15.6 us  [across(): return lax.all_to_all(value, axis, 0, 0)]
    all_to_all x3 -> x4, waiting for transfers between devices: 10 us -> 14.7 us  [across(): return lax.all_to_all(value, axis, 0, 0)]
    ppermute x33, waiting for transfers between devices: 23 us -> 26 us  [fetch(): return lax.ppermute(value, axis, [(i, i ^ k) for i in range(size)])]
    pallas_call x27, Pallas kernels: 32.6 us -> 29.7 us  [run(): pl.pallas_call(inner, out_shape=out_flat, in_specs=[pl.BlockSpec(memory_s...]
  transfers between devices with their start and end apart: 72 -> 73, of which waited for: 41 -> 40; matrix products, arithmetic and copies ran while one was open for 7% -> 9% of each run, Pallas kernels for 9% -> 8%
where the time goes in v5:
time: 263 us; the launch traced here: 262 us
  starting transfers between devices  92.1 us (35%)
  waiting for transfers between devices  72.1 us (27%)
  local copies, waits for them, and re-layouts  35.4 us (13%)
  Pallas kernels  29.7 us (11%)
  between operations  14.6 us (6%)
  other arithmetic  11.6 us (4%)
  matrix products  6.66 us (3%)
    ppermute x33, starting transfers between devices, fetch(): return lax.ppermute(value, axis, [(i, i ^ k) for i in range(size)])  42.6 us
    ppermute x27, starting transfers between devices, exchange(): return lax.ppermute(value, axis, [(i, i ^ k) for i in range(size)])  32.8 us
    pallas_call x27, Pallas kernels, run(): pl.pallas_call(inner, out_shape=out_flat, in_specs=[pl.BlockSpec(memory_s...  29.7 us
    ppermute x27, waiting for transfers between devices, exchange(): return lax.ppermute(value, axis, [(i, i ^ k) for i in range(size)])  28.8 us
    unnamed x104, local copies, waits for them, and re-layouts  28.1 us
    ppermute x33, waiting for transfers between devices, fetch(): return lax.ppermute(value, axis, [(i, i ^ k) for i in range(size)])  26 us
    all_to_all x4, starting transfers between devices, across(): return lax.all_to_all(value, axis, 0, 0)  15.6 us
    all_to_all x4, waiting for transfers between devices, across(): return lax.all_to_all(value, axis, 0, 0)  14.7 us
  transfers between devices with their start and end apart: 73, of which 40 were waited for; matrix products, arithmetic and copies ran while one was open for 9% of the time, Pallas kernels for 8%

profile of v5, /device:TPU:0, one launch (start us, length us, event | category | flops | bytes accessed | tf_op | source)
XLA Modules:
  0.0 262.1 jit_solution(435824527088426985)
XLA Ops:
  8.1 3.0 %collective-permute-start.3 = (s32[1,4]{1,0:T(1,128)S(1)}, s32[1,4]{1,0:T(1,128)S(1)}, u32[]{:S(2)}, u32[]{:S(2)}) collective-permute-start(s32[1,4]{1,0:T(1,128)S(1)} %pad_add_fusion), channel_id=1, source_target_pairs={{0,1},{1,0},{2,3},{3,2},{4,5},{5,4},{6,7},{7,6},{8,9},{9,8},{10,11... | collective-permute-start | bytes 56 | tf_op jit(solution)/shard_map/ppermute | solution.py:38
  11.1 2.6 collective-permute-start.4
  23.6 3.5 %collective-permute-start.8 = (bf16[96,768]{1,0:T(8,128)(2,1)S(1)}, bf16[96,768]{1,0:T(8,128)(2,1)}, u32[]{:S(2)}, u32[]{:S(2)}) collective-permute-start(bf16[96,768]{1,0:T(8,128)(2,1)S(1)} %bitcast.113), channel_id=1, source_target_pairs={{0,2},{1,3},{2,0},{3,1},{4,6},{5,7},{6,4},{7,5},{8,10},{9,11},{10,... | collective-permute-start | bytes 442376 | tf_op jit(solution)/shard_map/ppermute | solution.py:38
  28.4 5.1 %all-to-all-start = ((f32[4,16,192]{2,1,0:T(8,128)}), f32[4,16,192]{2,1,0:T(8,128)S(1)}, u32[]{:S(2)}, u32[]{:S(2)}) async-start(f32[4,16,192]{2,1,0:T(8,128)} %shard_map.272), calls=%async_computation | async-start | bytes 131072 | tf_op jit(solution)/shard_map/all_to_all | solution.py:53
  33.5 5.1 %collective-permute-done.8 = bf16[96,768]{1,0:T(8,128)(2,1)} collective-permute-done((bf16[96,768]{1,0:T(8,128)(2,1)S(1)}, bf16[96,768]{1,0:T(8,128)(2,1)}, u32[]{:S(2)}, u32[]{:S(2)}) %collective-permute-start.8) | collective-permute-done | bytes 147488 | tf_op jit(solution)/shard_map/ppermute | solution.py:38
  39.8 2.4 all-to-all-done.refs_3_
  50.3 3.7 %all-to-all-start.1 = ((f32[8,22,192]{2,1,0:T(8,128)}), f32[8,22,192]{2,1,0:T(8,128)S(1)}, u32[]{:S(2)}, u32[]{:S(2)}) async-start(f32[8,22,192]{2,1,0:T(8,128)} %bitcast.15), calls=%async_computation.1 | async-start | bytes 393216 | tf_op jit(solution)/shard_map/all_to_all | solution.py:53
  55.4 4.6 %all-to-all-done.1.refs_1_ = f32[8,22,192]{2,1,0:T(8,128)S(1)} async-done(((f32[8,22,192]{2,1,0:T(8,128)}), f32[8,22,192]{2,1,0:T(8,128)S(1)}, u32[]{:S(2)}, u32[]{:S(2)}) %all-to-all-start.1) | async-done | bytes 135200 | tf_op jit(solution)/shard_map/all_to_all | solution.py:53
  83.0 2.4 all-gather.5.cloned.1.call-done
  93.6 2.3 collective-permute-done.18.refs_2_
  128.4 2.3 shard_map.283
  142.1 2.4 collective-permute-done.38.refs_3_
  152.8 2.4 shard_map.287
  174.7 2.3 collective-permute-done.47.refs_3_
  197.4 3.2 %shard_map.291 = (bf16[256,1344]{1,0:T(8,128)(2,1)S(1)}, f32[256,768]{1,0:T(8,128)S(1)}, f32[1,768]{1,0:T(1,128)}, f32[1,576]{1,0:T(1,128)}, f32[8,22,192]{2,1,0:T(8,128)}) custom-call(bf16[64,768]{1,0:T(8,128)(2,1)S(1)} %get-tuple-element.146.refs_0_, bf16[64,768]{1,0:T(8,128)(2,1)S(1)} %collective-permute-done.51.refs_1_, ...), custom_call_target="tpu_custom_call" | custom-call | flops 704643072 | bytes 4416000 | tf_op jit(solution)/shard_map/pallas_call | solution.py:100
  205.7 3.4 %all-to-all-start.2 = ((f32[8,22,192]{2,1,0:T(8,128)}), f32[8,22,192]{2,1,0:T(8,128)S(1)}, u32[]{:S(2)}, u32[]{:S(2)}) async-start(f32[8,22,192]{2,1,0:T(8,128)} %get-tuple-element.157), calls=%async_computation.2 | async-start | bytes 393216 | tf_op jit(solution)/shard_map/all_to_all | solution.py:53
  209.9 5.1 %all-to-all-done.2.refs_1_ = f32[8,22,192]{2,1,0:T(8,128)S(1)} async-done(((f32[8,22,192]{2,1,0:T(8,128)}), f32[8,22,192]{2,1,0:T(8,128)S(1)}, u32[]{:S(2)}, u32[]{:S(2)}) %all-to-all-start.2) | async-done | bytes 135200 | tf_op jit(solution)/shard_map/all_to_all | solution.py:53
  217.4 2.6 collective-permute-start.56
  220.1 2.4 collective-permute-done.55.refs_2_.refs_3_
  225.5 3.4 %all-to-all-start.3 = ((f32[8,8,192]{2,1,0:T(8,128)}), f32[8,8,192]{2,1,0:T(8,128)S(1)}, u32[]{:S(2)}, u32[]{:S(2)}) async-start(f32[8,8,192]{2,1,0:T(8,128)} %shard_map.295), calls=%async_computation.3 | async-start | bytes 131072 | tf_op jit(solution)/shard_map/all_to_all | solution.py:53
  231.2 2.5 all-to-all-done.3
  234.2 2.8 %collective-permute-start.62 = (f32[8,192]{1,0:T(8,128)S(1)}, f32[8,192]{1,0:T(8,128)}, u32[]{:S(2)}, u32[]{:S(2)}) collective-permute-start(f32[8,192]{1,0:T(8,128)S(1)} %reduce_sum.28), channel_id=1, source_target_pairs={{0,2},{1,3},{2,0},{3,1},{4,6},{5,7},{6,4},{7,5},{8,10},{9,11},{10,... | collective-permute-start | bytes 18440 | tf_op jit(solution)/shard_map/ppermute | solution.py:38
  241.5 2.3 collective-permute-start.59
  246.9 2.3 fusion
  (332 shorter events, 173.3 us)
Async XLA Ops:
  8.1 12.9 %collective-permute-start.3 = (s32[1,4]{1,0:T(1,128)S(1)}, s32[1,4]{1,0:T(1,128)S(1)}, u32[]{:S(2)}, u32[]{:S(2)}) collective-permute-start(s32[1,4]{1,0:T(1,128)S(1)} %pad_add_fusion), channel_id=1, source_target_pairs={{0,1},{1,0},{2,3},{3,2},{4,5},{5,4},{6,7},{7,6},{8,9},{9,8},{10,11... | collective-permute-start | bytes 56 | tf_op jit(solution)/shard_map/ppermute | solution.py:38
  11.1 9.9 %collective-permute-start.4 = (s32[1,4]{1,0:T(1,128)S(1)}, s32[1,4]{1,0:T(1,128)S(1)}, u32[]{:S(2)}, u32[]{:S(2)}) collective-permute-start(s32[1,4]{1,0:T(1,128)S(1)} %pad_add_fusion), channel_id=1, source_target_pairs={{0,2},{1,3},{2,0},{3,1},{4,6},{5,7},{6,4},{7,5},{8,10},{9,11},{10,... | collective-permute-start | bytes 56 | tf_op jit(solution)/shard_map/ppermute | solution.py:38
  22.6 10.9 %collective-permute-start.7 = (bf16[96,768]{1,0:T(8,128)(2,1)S(1)}, bf16[96,768]{1,0:T(8,128)(2,1)S(1)}, u32[]{:S(2)}, u32[]{:S(2)}) collective-permute-start(bf16[96,768]{1,0:T(8,128)(2,1)S(1)} %bitcast.112), channel_id=1, source_target_pairs={{0,1},{1,0},{2,3},{3,2},{4,5},{5,4},{6,7},{7,6},{8,9},{9,8},{10,11... | collective-permute-start | bytes 442376 | tf_op jit(solution)/shard_map/ppermute | solution.py:38
  23.6 15.0 %collective-permute-start.8 = (bf16[96,768]{1,0:T(8,128)(2,1)S(1)}, bf16[96,768]{1,0:T(8,128)(2,1)}, u32[]{:S(2)}, u32[]{:S(2)}) collective-permute-start(bf16[96,768]{1,0:T(8,128)(2,1)S(1)} %bitcast.113), channel_id=1, source_target_pairs={{0,2},{1,3},{2,0},{3,1},{4,6},{5,7},{6,4},{7,5},{8,10},{9,11},{10,... | collective-permute-start | bytes 442376 | tf_op jit(solution)/shard_map/ppermute | solution.py:38
  27.1 11.5 %collective-permute-start.9 = (bf16[96,768]{1,0:T(8,128)(2,1)S(1)}, bf16[96,768]{1,0:T(8,128)(2,1)}, u32[]{:S(2)}, u32[]{:S(2)}) collective-permute-start(bf16[96,768]{1,0:T(8,128)(2,1)S(1)} %bitcast.114), channel_id=1, source_target_pairs={{0,3},{1,2},{2,1},{3,0},{4,7},{5,6},{6,5},{7,4},{8,11},{9,10},{10,... | collective-permute-start | bytes 442376 | tf_op jit(solution)/shard_map/ppermute | solution.py:38
  28.4 13.8 %all-to-all-start = ((f32[4,16,192]{2,1,0:T(8,128)}), f32[4,16,192]{2,1,0:T(8,128)S(1)}, u32[]{:S(2)}, u32[]{:S(2)}) async-start(f32[4,16,192]{2,1,0:T(8,128)} %shard_map.272), calls=%async_computation | async-start | bytes 131072 | tf_op jit(solution)/shard_map/all_to_all | solution.py:53
  33.5 51.9 %all-gather.5.cloned.1.call-start = ((), (), s32[]{:S(2)}) async-start(), calls=%async_computation.8 | async-start | bytes 3981312 | tf_op jit(solution)/shard_map/all_gather | solution.py:617
  43.6 82.2 %all-gather.7.cloned.1.call-start = ((), (), s32[]{:S(2)}) async-start(), calls=%async_computation.9 | async-start | bytes 2654208 | tf_op jit(solution)/shard_map/all_gather | solution.py:617
  45.0 15.7 %collective-permute-start.10 = (bf16[4,96,768]{2,1,0:T(8,128)(2,1)S(1)}, bf16[4,96,768]{2,1,0:T(8,128)(2,1)S(1)}, u32[]{:S(2)}, u32[]{:S(2)}) collective-permute-start(bf16[4,96,768]{2,1,0:T(8,128)(2,1)S(1)} %pad_maximum_fusion.refs_3_.refs_4_), channel_id=1, source_target_pairs={{0,16},{16,0},{1,17},{17,1},{2,18},{18,2},{3,19},{19,3},{4,20},{20... | collective-permute-start | bytes 1769480 | tf_op jit(solution)/shard_map/ppermute | solution.py:49
  46.0 8.3 %collective-permute-start = (bf16[64,768]{1,0:T(8,128)(2,1)S(1)}, bf16[64,768]{1,0:T(8,128)(2,1)S(1)}, u32[]{:S(2)}, u32[]{:S(2)}) collective-permute-start(bf16[64,768]{1,0:T(8,128)(2,1)S(1)} %select_bitcast_fusion.5.refs_4_.refs_5_), channel_id=1, source_target_pairs={{0,4},{4,0},{8,12},{12,8},{1,5},{5,1},{9,13},{13,9},{2,6},{6,2},{1... | collective-permute-start | bytes 294920 | tf_op jit(solution)/shard_map/ppermute | solution.py:38
  50.3 9.7 %all-to-all-start.1 = ((f32[8,22,192]{2,1,0:T(8,128)}), f32[8,22,192]{2,1,0:T(8,128)S(1)}, u32[]{:S(2)}, u32[]{:S(2)}) async-start(f32[8,22,192]{2,1,0:T(8,128)} %bitcast.15), calls=%async_computation.1 | async-start | bytes 393216 | tf_op jit(solution)/shard_map/all_to_all | solution.py:53
  54.1 195.6 %reduce-scatter.5.cloned.1.call-start = ((), (), s32[]{:S(2)}) async-start(), calls=%async_computation.7 | async-start | bytes 3981312 | tf_op jit(solution)/shard_map/reduce_scatter | solution.py:852
  117.8 8.0 %collective-permute-start.27 = (bf16[64,768]{1,0:T(8,128)(2,1)}, bf16[64,768]{1,0:T(8,128)(2,1)}, u32[]{:S(2)}, u32[]{:S(2)}) collective-permute-start(bf16[64,768]{1,0:T(8,128)(2,1)} %get-tuple-element.118.refs_0_), channel_id=1, source_target_pairs={{0,8},{4,12},{8,0},{12,4},{1,9},{5,13},{9,1},{13,5},{2,10},{6,14},... | collective-permute-start | bytes 294920 | tf_op jit(solution)/shard_map/ppermute | solution.py:38
  121.6 10.2 %collective-permute-start.33 = (bf16[64,768]{1,0:T(8,128)(2,1)S(1)}, bf16[64,768]{1,0:T(8,128)(2,1)}, u32[]{:S(2)}, u32[]{:S(2)}) collective-permute-start(bf16[64,768]{1,0:T(8,128)(2,1)S(1)} %select_bitcast_fusion.2.refs_4_), channel_id=1, source_target_pairs={{0,4},{4,0},{8,12},{12,8},{1,5},{5,1},{9,13},{13,9},{2,6},{6,2},{1... | collective-permute-start | bytes 294920 | tf_op jit(solution)/shard_map/ppermute | solution.py:38
  122.6 9.2 %collective-permute-start.34 = (bf16[64,768]{1,0:T(8,128)(2,1)S(1)}, bf16[64,768]{1,0:T(8,128)(2,1)}, u32[]{:S(2)}, u32[]{:S(2)}) collective-permute-start(bf16[64,768]{1,0:T(8,128)(2,1)S(1)} %select_bitcast_fusion.2.refs_4_), channel_id=1, source_target_pairs={{0,8},{4,12},{8,0},{12,4},{1,9},{5,13},{9,1},{13,5},{2,10},{6,14},... | collective-permute-start | bytes 294920 | tf_op jit(solution)/shard_map/ppermute | solution.py:38
  124.1 7.7 %collective-permute-start.35 = (bf16[64,768]{1,0:T(8,128)(2,1)S(1)}, bf16[64,768]{1,0:T(8,128)(2,1)}, u32[]{:S(2)}, u32[]{:S(2)}) collective-permute-start(bf16[64,768]{1,0:T(8,128)(2,1)S(1)} %select_bitcast_fusion.2.refs_4_), channel_id=1, source_target_pairs={{0,12},{4,8},{8,4},{12,0},{1,13},{5,9},{9,5},{13,1},{2,14},{6,10},... | collective-permute-start | bytes 294920 | tf_op jit(solution)/shard_map/ppermute | solution.py:38
  159.3 90.5 %reduce-scatter.3.cloned.1.call-start = ((), (), s32[]{:S(2)}) async-start(), calls=%async_computation.6 | async-start | bytes 3981312 | tf_op jit(solution)/shard_map/reduce_scatter | solution.py:852
  205.7 9.3 %all-to-all-start.2 = ((f32[8,22,192]{2,1,0:T(8,128)}), f32[8,22,192]{2,1,0:T(8,128)S(1)}, u32[]{:S(2)}, u32[]{:S(2)}) async-start(f32[8,22,192]{2,1,0:T(8,128)} %get-tuple-element.157), calls=%async_computation.2 | async-start | bytes 393216 | tf_op jit(solution)/shard_map/all_to_all | solution.py:53
  225.5 8.2 %all-to-all-start.3 = ((f32[8,8,192]{2,1,0:T(8,128)}), f32[8,8,192]{2,1,0:T(8,128)S(1)}, u32[]{:S(2)}, u32[]{:S(2)}) async-start(f32[8,8,192]{2,1,0:T(8,128)} %shard_map.295), calls=%async_computation.3 | async-start | bytes 131072 | tf_op jit(solution)/shard_map/all_to_all | solution.py:53
  234.2 10.3 %collective-permute-start.62 = (f32[8,192]{1,0:T(8,128)S(1)}, f32[8,192]{1,0:T(8,128)}, u32[]{:S(2)}, u32[]{:S(2)}) collective-permute-start(f32[8,192]{1,0:T(8,128)S(1)} %reduce_sum.28), channel_id=1, source_target_pairs={{0,2},{1,3},{2,0},{3,1},{4,6},{5,7},{6,4},{7,5},{8,10},{9,11},{10,... | collective-permute-start | bytes 18440 | tf_op jit(solution)/shard_map/ppermute | solution.py:38
  237.0 8.3 %collective-permute-start.63 = (f32[8,192]{1,0:T(8,128)S(1)}, f32[8,192]{1,0:T(8,128)}, u32[]{:S(2)}, u32[]{:S(2)}) collective-permute-start(f32[8,192]{1,0:T(8,128)S(1)} %reduce_sum.28), channel_id=1, source_target_pairs={{0,3},{1,2},{2,1},{3,0},{4,7},{5,6},{6,5},{7,4},{8,11},{9,10},{10,... | collective-permute-start | bytes 18440 | tf_op jit(solution)/shard_map/ppermute | solution.py:38
  239.5 9.8 %collective-permute-start.57 = (bf16[64,768]{1,0:T(8,128)(2,1)S(1)}, bf16[64,768]{1,0:T(8,128)(2,1)S(1)}, u32[]{:S(2)}, u32[]{:S(2)}) collective-permute-start(bf16[64,768]{1,0:T(8,128)(2,1)S(1)} %get-tuple-element.162), channel_id=1, source_target_pairs={{0,4},{4,0},{8,12},{12,8},{1,5},{5,1},{9,13},{13,9},{2,6},{6,2},{1... | collective-permute-start | bytes 294920 | tf_op jit(solution)/shard_map/ppermute | solution.py:31
  240.1 9.1 %collective-permute-start.58 = (bf16[64,768]{1,0:T(8,128)(2,1)S(1)}, bf16[64,768]{1,0:T(8,128)(2,1)S(1)}, u32[]{:S(2)}, u32[]{:S(2)}) collective-permute-start(bf16[64,768]{1,0:T(8,128)(2,1)S(1)} %get-tuple-element.163), channel_id=1, source_target_pairs={{0,8},{4,12},{8,0},{12,4},{1,9},{5,13},{9,1},{13,5},{2,10},{6,14},... | collective-permute-start | bytes 294920 | tf_op jit(solution)/shard_map/ppermute | solution.py:31
  241.5 7.8 %collective-permute-start.59 = (bf16[64,768]{1,0:T(8,128)(2,1)S(1)}, bf16[64,768]{1,0:T(8,128)(2,1)S(1)}, u32[]{:S(2)}, u32[]{:S(2)}) collective-permute-start(bf16[64,768]{1,0:T(8,128)(2,1)S(1)} %get-tuple-element.164), channel_id=1, source_target_pairs={{0,12},{4,8},{8,4},{12,0},{1,13},{5,9},{9,5},{13,1},{2,14},{6,10},... | collective-permute-start | bytes 294920 | tf_op jit(solution)/shard_map/ppermute | solution.py:31
  (101 other events, 597.8 us)
Sparse Core Ops, SparseCore 0:
  43.7 41.6 all-gather.4
  87.6 30.4 all-gather.6
  159.4 42.0 reduce-scatter.4
  204.8 43.4 reduce-scatter.2

commit v6 on v5

--- a/solution.py
+++ b/solution.py
@@ -495,6 +495,24 @@
     repeat_rows(total, refs.sent)
 
 
+def condition_kernel(spot, pieces, condition, refs):
+    shards = len(pieces)
+    blocks = []
+    for z in range(shards):
+        chosen = pieces[0][...]
+        for k in range(1, shards):
+            chosen = jnp.where(spot[3 + k] == z, pieces[k][...], chosen)
+        blocks.append(chosen)
+    values = condition[...]
+    gate = 1.0 / (1.0 + jnp.exp(-values))
+    rest = jnp.concatenate(blocks, axis=1) * (gate * (1.0 + values * (1.0 - gate)))
+    rounded = []
+    for _ in range(3):
+        rounded.append(rest.astype(BF16).astype(F32))
+        rest = rest - rounded[-1]
+    refs.pieces[...] = jnp.concatenate(rounded, axis=0).astype(BF16)
+
+
 def repeat_rows(values, ref):
     for k in range(ref.shape[0]):
         ref[k] = values
@@ -943,7 +961,13 @@
             jnp.moveaxis(modulate_weight[0], 1, 0),
         ).sent
         act_grad = jnp.sum(across(sent, LAYER), axis=0)
-        act_all = place(gather_list(act_grad, SLOTS), SLOTS)
+        pieces = run(
+            condition_kernel,
+            Named(pieces=shaped((3 * shards * micro_count, width), BF16)),
+            spot,
+            gather_list(act_grad, SLOTS),
+            condition,
+        ).pieces
     else:
         act_grad = lax.dot_general(
             mod_slots, mod_weight.astype(F32), (((1,), (1,)), ((), ())), precision=HIGH
@@ -951,14 +975,13 @@
         act_grad = act_grad + swap(act_grad)
         act_grad = sum(gather_list(act_grad, TENSOR))
         act_all = lax.all_gather(act_grad, SLOTS, axis=0)
-    act_all = jnp.moveaxis(act_all, 0, 1).reshape(-1, width)
-    cond_grad = jax.vjp(jax.nn.silu, condition)[1](act_all)[0]
-    pieces = []
-    rest = cond_grad
-    for _ in range(3):
-        pieces.append(rest.astype(BF16))
-        rest = rest - pieces[-1].astype(F32)
-    pieces = jnp.concatenate(pieces, axis=0)
+        act_all = jnp.moveaxis(act_all, 0, 1).reshape(-1, width)
+        rest = jax.vjp(jax.nn.silu, condition)[1](act_all)[0]
+        pieces = []
+        for _ in range(3):
+            pieces.append(rest.astype(BF16))
+            rest = rest - pieces[-1].astype(F32)
+        pieces = jnp.concatenate(pieces, axis=0)
     table_grad = dot(jnp.concatenate([class_hot.astype(BF16)] * 3, axis=0), pieces, 0, 0)
     time_grad = dot(jnp.concatenate([time_feats] * 3, axis=0), pieces, 0, 0)
     grad_mod_weight = lax.dot_general(

time: 263 us -> 262 us (level)
  local copies, waits for them, and re-layouts: 35.4 us -> 32.4 us
    pallas_call x27 -> x28, Pallas kernels: 29.7 us -> 30.3 us  [run(): pl.pallas_call(inner, out_shape=out_flat, in_specs=[pl.BlockSpec(memory_s...]
    unnamed x104 -> x120, local copies, waits for them, and re-layouts: 28.1 us -> 27.5 us
  transfers between devices with their start and end apart: 73 -> 73, of which waited for: 40 -> 42; matrix products, arithmetic and copies ran while one was open for 9% -> 8% of each run, Pallas kernels for 8% -> 9%
where the time goes in v6:
time: 262 us; the launch traced here: 260 us
  starting transfers between devices  91.7 us (35%)
  waiting for transfers between devices  73.3 us (28%)
  local copies, waits for them, and re-layouts  32.4 us (12%)
  Pallas kernels  30.3 us (12%)
  between operations  14.6 us (6%)
  other arithmetic  11.4 us (4%)
  matrix products  6.63 us (3%)
    ppermute x33, starting transfers between devices, fetch(): return lax.ppermute(value, axis, [(i, i ^ k) for i in range(size)])  42.6 us
    ppermute x27, starting transfers between devices, exchange(): return lax.ppermute(value, axis, [(i, i ^ k) for i in range(size)])  32.8 us
    pallas_call x28, Pallas kernels, run(): pl.pallas_call(inner, out_shape=out_flat, in_specs=[pl.BlockSpec(memory_s...  30.3 us
    ppermute x27, waiting for transfers between devices, exchange(): return lax.ppermute(value, axis, [(i, i ^ k) for i in range(size)])  29.2 us
    unnamed x120, local copies, waits for them, and re-layouts  27.5 us
    ppermute x33, waiting for transfers between devices, fetch(): return lax.ppermute(value, axis, [(i, i ^ k) for i in range(size)])  26 us
    all_to_all x4, starting transfers between devices, across(): return lax.all_to_all(value, axis, 0, 0)  15.6 us
    all_to_all x4, waiting for transfers between devices, across(): return lax.all_to_all(value, axis, 0, 0)  14.8 us
  transfers between devices with their start and end apart: 73, of which 42 were waited for; matrix products, arithmetic and copies ran while one was open for 8% of the time, Pallas kernels for 9%

profile of v6, /device:TPU:0, one launch (start us, length us, event | category | flops | bytes accessed | tf_op | source)
XLA Modules:
  0.0 260.3 jit_solution(13974012318022317865)
XLA Ops:
  8.1 3.0 %collective-permute-start.3 = (s32[1,4]{1,0:T(1,128)S(1)}, s32[1,4]{1,0:T(1,128)S(1)}, u32[]{:S(2)}, u32[]{:S(2)}) collective-permute-start(s32[1,4]{1,0:T(1,128)S(1)} %pad_add_fusion), channel_id=1, source_target_pairs={{0,1},{1,0},{2,3},{3,2},{4,5},{5,4},{6,7},{7,6},{8,9},{9,8},{10,11... | collective-permute-start | bytes 56 | tf_op jit(solution)/shard_map/ppermute | solution.py:38
  11.1 2.6 collective-permute-start.4
  23.6 3.5 %collective-permute-start.8 = (bf16[96,768]{1,0:T(8,128)(2,1)S(1)}, bf16[96,768]{1,0:T(8,128)(2,1)}, u32[]{:S(2)}, u32[]{:S(2)}) collective-permute-start(bf16[96,768]{1,0:T(8,128)(2,1)S(1)} %bitcast.111), channel_id=1, source_target_pairs={{0,2},{1,3},{2,0},{3,1},{4,6},{5,7},{6,4},{7,5},{8,10},{9,11},{10,... | collective-permute-start | bytes 442376 | tf_op jit(solution)/shard_map/ppermute | solution.py:38
  28.4 5.1 %all-to-all-start = ((f32[4,16,192]{2,1,0:T(8,128)}), f32[4,16,192]{2,1,0:T(8,128)S(1)}, u32[]{:S(2)}, u32[]{:S(2)}) async-start(f32[4,16,192]{2,1,0:T(8,128)} %shard_map.272), calls=%async_computation | async-start | bytes 131072 | tf_op jit(solution)/shard_map/all_to_all | solution.py:53
  33.5 5.1 %collective-permute-done.8 = bf16[96,768]{1,0:T(8,128)(2,1)} collective-permute-done((bf16[96,768]{1,0:T(8,128)(2,1)S(1)}, bf16[96,768]{1,0:T(8,128)(2,1)}, u32[]{:S(2)}, u32[]{:S(2)}) %collective-permute-start.8) | collective-permute-done | bytes 147488 | tf_op jit(solution)/shard_map/ppermute | solution.py:38
  39.8 2.5 all-to-all-done.refs_3_
  50.3 3.7 %all-to-all-start.1 = ((f32[8,22,192]{2,1,0:T(8,128)}), f32[8,22,192]{2,1,0:T(8,128)S(1)}, u32[]{:S(2)}, u32[]{:S(2)}) async-start(f32[8,22,192]{2,1,0:T(8,128)} %bitcast.15), calls=%async_computation.1 | async-start | bytes 393216 | tf_op jit(solution)/shard_map/all_to_all | solution.py:53
  55.4 4.6 %all-to-all-done.1.refs_1_ = f32[8,22,192]{2,1,0:T(8,128)S(1)} async-done(((f32[8,22,192]{2,1,0:T(8,128)}), f32[8,22,192]{2,1,0:T(8,128)S(1)}, u32[]{:S(2)}, u32[]{:S(2)}) %all-to-all-start.1) | async-done | bytes 135200 | tf_op jit(solution)/shard_map/all_to_all | solution.py:53
  83.0 2.4 all-gather.5.cloned.1.call-done
  93.6 2.3 collective-permute-done.18.refs_2_
  128.4 2.3 shard_map.283
  142.1 2.4 collective-permute-done.38.refs_3_
  152.8 2.4 shard_map.287
  174.6 2.4 collective-permute-done.47.refs_3_
  197.5 3.2 %shard_map.291 = (bf16[256,1344]{1,0:T(8,128)(2,1)S(1)}, f32[256,768]{1,0:T(8,128)S(1)}, f32[1,768]{1,0:T(1,128)}, f32[1,576]{1,0:T(1,128)}, f32[8,22,192]{2,1,0:T(8,128)}) custom-call(bf16[64,768]{1,0:T(8,128)(2,1)S(1)} %get-tuple-element.146.refs_0_, bf16[64,768]{1,0:T(8,128)(2,1)S(1)} %collective-permute-done.51.refs_1_, ...), custom_call_target="tpu_custom_call" | custom-call | flops 704643072 | bytes 4416000 | tf_op jit(solution)/shard_map/pallas_call | solution.py:100
  206.4 3.4 %all-to-all-start.2 = ((f32[8,22,192]{2,1,0:T(8,128)}), f32[8,22,192]{2,1,0:T(8,128)S(1)}, u32[]{:S(2)}, u32[]{:S(2)}) async-start(f32[8,22,192]{2,1,0:T(8,128)} %get-tuple-element.157), calls=%async_computation.2 | async-start | bytes 393216 | tf_op jit(solution)/shard_map/all_to_all | solution.py:53
  210.5 5.1 %all-to-all-done.2.refs_1_ = f32[8,22,192]{2,1,0:T(8,128)S(1)} async-done(((f32[8,22,192]{2,1,0:T(8,128)}), f32[8,22,192]{2,1,0:T(8,128)S(1)}, u32[]{:S(2)}, u32[]{:S(2)}) %all-to-all-start.2) | async-done | bytes 135200 | tf_op jit(solution)/shard_map/all_to_all | solution.py:53
  218.1 2.6 %collective-permute-start.56 = (f32[16,192]{1,0:T(8,128)S(1)}, f32[16,192]{1,0:T(8,128)S(1)}, u32[]{:S(2)}, u32[]{:S(2)}) collective-permute-start(f32[16,192]{1,0:T(8,128)S(1)} %get-tuple-element.160), channel_id=1, source_target_pairs={{0,3},{1,2},{2,1},{3,0},{4,7},{5,6},{6,5},{7,4},{8,11},{9,10},{10,... | collective-permute-start | bytes 36872 | tf_op jit(solution)/shard_map/ppermute | solution.py:31
  220.7 2.4 collective-permute-done.55.refs_2_.refs_3_
  226.1 3.4 %all-to-all-start.3 = ((f32[8,8,192]{2,1,0:T(8,128)}), f32[8,8,192]{2,1,0:T(8,128)S(1)}, u32[]{:S(2)}, u32[]{:S(2)}) async-start(f32[8,8,192]{2,1,0:T(8,128)} %shard_map.295), calls=%async_computation.3 | async-start | bytes 131072 | tf_op jit(solution)/shard_map/all_to_all | solution.py:53
  231.8 2.5 all-to-all-done.3
  234.8 2.8 %collective-permute-start.62 = (f32[8,192]{1,0:T(8,128)S(1)}, f32[8,192]{1,0:T(8,128)S(1)}, u32[]{:S(2)}, u32[]{:S(2)}) collective-permute-start(f32[8,192]{1,0:T(8,128)S(1)} %reduce_sum.28.refs_1_), channel_id=1, source_target_pairs={{0,2},{1,3},{2,0},{3,1},{4,6},{5,7},{6,4},{7,5},{8,10},{9,11},{10,... | collective-permute-start | bytes 18440 | tf_op jit(solution)/shard_map/ppermute | solution.py:38
  241.4 2.3 collective-permute-start.59
  244.3 2.3 fusion
  (337 shorter events, 171.4 us)
Async XLA Ops:
  8.1 12.8 %collective-permute-start.3 = (s32[1,4]{1,0:T(1,128)S(1)}, s32[1,4]{1,0:T(1,128)S(1)}, u32[]{:S(2)}, u32[]{:S(2)}) collective-permute-start(s32[1,4]{1,0:T(1,128)S(1)} %pad_add_fusion), channel_id=1, source_target_pairs={{0,1},{1,0},{2,3},{3,2},{4,5},{5,4},{6,7},{7,6},{8,9},{9,8},{10,11... | collective-permute-start | bytes 56 | tf_op jit(solution)/shard_map/ppermute | solution.py:38
  11.1 9.8 %collective-permute-start.4 = (s32[1,4]{1,0:T(1,128)S(1)}, s32[1,4]{1,0:T(1,128)S(1)}, u32[]{:S(2)}, u32[]{:S(2)}) collective-permute-start(s32[1,4]{1,0:T(1,128)S(1)} %pad_add_fusion), channel_id=1, source_target_pairs={{0,2},{1,3},{2,0},{3,1},{4,6},{5,7},{6,4},{7,5},{8,10},{9,11},{10,... | collective-permute-start | bytes 56 | tf_op jit(solution)/shard_map/ppermute | solution.py:38
  13.7 7.3 %collective-permute-start.5 = (s32[1,4]{1,0:T(1,128)S(1)}, s32[1,4]{1,0:T(1,128)S(1)}, u32[]{:S(2)}, u32[]{:S(2)}) collective-permute-start(s32[1,4]{1,0:T(1,128)S(1)} %pad_add_fusion), channel_id=1, source_target_pairs={{0,3},{1,2},{2,1},{3,0},{4,7},{5,6},{6,5},{7,4},{8,11},{9,10},{10,... | collective-permute-start | bytes 56 | tf_op jit(solution)/shard_map/ppermute | solution.py:38
  22.6 10.9 %collective-permute-start.7 = (bf16[96,768]{1,0:T(8,128)(2,1)S(1)}, bf16[96,768]{1,0:T(8,128)(2,1)S(1)}, u32[]{:S(2)}, u32[]{:S(2)}) collective-permute-start(bf16[96,768]{1,0:T(8,128)(2,1)S(1)} %bitcast.110), channel_id=1, source_target_pairs={{0,1},{1,0},{2,3},{3,2},{4,5},{5,4},{6,7},{7,6},{8,9},{9,8},{10,11... | collective-permute-start | bytes 442376 | tf_op jit(solution)/shard_map/ppermute | solution.py:38
  23.6 14.9 %collective-permute-start.8 = (bf16[96,768]{1,0:T(8,128)(2,1)S(1)}, bf16[96,768]{1,0:T(8,128)(2,1)}, u32[]{:S(2)}, u32[]{:S(2)}) collective-permute-start(bf16[96,768]{1,0:T(8,128)(2,1)S(1)} %bitcast.111), channel_id=1, source_target_pairs={{0,2},{1,3},{2,0},{3,1},{4,6},{5,7},{6,4},{7,5},{8,10},{9,11},{10,... | collective-permute-start | bytes 442376 | tf_op jit(solution)/shard_map/ppermute | solution.py:38
  27.1 11.5 %collective-permute-start.9 = (bf16[96,768]{1,0:T(8,128)(2,1)S(1)}, bf16[96,768]{1,0:T(8,128)(2,1)}, u32[]{:S(2)}, u32[]{:S(2)}) collective-permute-start(bf16[96,768]{1,0:T(8,128)(2,1)S(1)} %bitcast.112), channel_id=1, source_target_pairs={{0,3},{1,2},{2,1},{3,0},{4,7},{5,6},{6,5},{7,4},{8,11},{9,10},{10,... | collective-permute-start | bytes 442376 | tf_op jit(solution)/shard_map/ppermute | solution.py:38
  28.4 13.9 %all-to-all-start = ((f32[4,16,192]{2,1,0:T(8,128)}), f32[4,16,192]{2,1,0:T(8,128)S(1)}, u32[]{:S(2)}, u32[]{:S(2)}) async-start(f32[4,16,192]{2,1,0:T(8,128)} %shard_map.272), calls=%async_computation | async-start | bytes 131072 | tf_op jit(solution)/shard_map/all_to_all | solution.py:53
  33.4 52.0 %all-gather.5.cloned.1.call-start = ((), (), s32[]{:S(2)}) async-start(), calls=%async_computation.8 | async-start | bytes 3981312 | tf_op jit(solution)/shard_map/all_gather | solution.py:635
  43.6 82.2 %all-gather.7.cloned.1.call-start = ((), (), s32[]{:S(2)}) async-start(), calls=%async_computation.9 | async-start | bytes 2654208 | tf_op jit(solution)/shard_map/all_gather | solution.py:635
  45.0 15.7 %collective-permute-start.10 = (bf16[4,96,768]{2,1,0:T(8,128)(2,1)S(1)}, bf16[4,96,768]{2,1,0:T(8,128)(2,1)S(1)}, u32[]{:S(2)}, u32[]{:S(2)}) collective-permute-start(bf16[4,96,768]{2,1,0:T(8,128)(2,1)S(1)} %pad_maximum_fusion.refs_3_.refs_4_), channel_id=1, source_target_pairs={{0,16},{16,0},{1,17},{17,1},{2,18},{18,2},{3,19},{19,3},{4,20},{20... | collective-permute-start | bytes 1769480 | tf_op jit(solution)/shard_map/ppermute | solution.py:49
  46.0 8.3 %collective-permute-start = (bf16[64,768]{1,0:T(8,128)(2,1)S(1)}, bf16[64,768]{1,0:T(8,128)(2,1)S(1)}, u32[]{:S(2)}, u32[]{:S(2)}) collective-permute-start(bf16[64,768]{1,0:T(8,128)(2,1)S(1)} %select_bitcast_fusion.5.refs_4_.refs_5_), channel_id=1, source_target_pairs={{0,4},{4,0},{8,12},{12,8},{1,5},{5,1},{9,13},{13,9},{2,6},{6,2},{1... | collective-permute-start | bytes 294920 | tf_op jit(solution)/shard_map/ppermute | solution.py:38
  50.3 9.7 %all-to-all-start.1 = ((f32[8,22,192]{2,1,0:T(8,128)}), f32[8,22,192]{2,1,0:T(8,128)S(1)}, u32[]{:S(2)}, u32[]{:S(2)}) async-start(f32[8,22,192]{2,1,0:T(8,128)} %bitcast.15), calls=%async_computation.1 | async-start | bytes 393216 | tf_op jit(solution)/shard_map/all_to_all | solution.py:53
  54.1 193.4 %reduce-scatter.5.cloned.1.call-start = ((), (), s32[]{:S(2)}) async-start(), calls=%async_computation.7 | async-start | bytes 3981312 | tf_op jit(solution)/shard_map/reduce_scatter | solution.py:870
  117.8 8.0 %collective-permute-start.27 = (bf16[64,768]{1,0:T(8,128)(2,1)}, bf16[64,768]{1,0:T(8,128)(2,1)}, u32[]{:S(2)}, u32[]{:S(2)}) collective-permute-start(bf16[64,768]{1,0:T(8,128)(2,1)} %get-tuple-element.118.refs_0_), channel_id=1, source_target_pairs={{0,8},{4,12},{8,0},{12,4},{1,9},{5,13},{9,1},{13,5},{2,10},{6,14},... | collective-permute-start | bytes 294920 | tf_op jit(solution)/shard_map/ppermute | solution.py:38
  118.6 7.2 %collective-permute-start.28 = (bf16[64,768]{1,0:T(8,128)(2,1)}, bf16[64,768]{1,0:T(8,128)(2,1)}, u32[]{:S(2)}, u32[]{:S(2)}) collective-permute-start(bf16[64,768]{1,0:T(8,128)(2,1)} %get-tuple-element.118.refs_0_), channel_id=1, source_target_pairs={{0,12},{4,8},{8,4},{12,0},{1,13},{5,9},{9,5},{13,1},{2,14},{6,10},... | collective-permute-start | bytes 294920 | tf_op jit(solution)/shard_map/ppermute | solution.py:38
  121.6 10.2 %collective-permute-start.33 = (bf16[64,768]{1,0:T(8,128)(2,1)S(1)}, bf16[64,768]{1,0:T(8,128)(2,1)}, u32[]{:S(2)}, u32[]{:S(2)}) collective-permute-start(bf16[64,768]{1,0:T(8,128)(2,1)S(1)} %select_bitcast_fusion.2.refs_4_), channel_id=1, source_target_pairs={{0,4},{4,0},{8,12},{12,8},{1,5},{5,1},{9,13},{13,9},{2,6},{6,2},{1... | collective-permute-start | bytes 294920 | tf_op jit(solution)/shard_map/ppermute | solution.py:38
  122.6 9.2 %collective-permute-start.34 = (bf16[64,768]{1,0:T(8,128)(2,1)S(1)}, bf16[64,768]{1,0:T(8,128)(2,1)}, u32[]{:S(2)}, u32[]{:S(2)}) collective-permute-start(bf16[64,768]{1,0:T(8,128)(2,1)S(1)} %select_bitcast_fusion.2.refs_4_), channel_id=1, source_target_pairs={{0,8},{4,12},{8,0},{12,4},{1,9},{5,13},{9,1},{13,5},{2,10},{6,14},... | collective-permute-start | bytes 294920 | tf_op jit(solution)/shard_map/ppermute | solution.py:38
  124.1 7.7 %collective-permute-start.35 = (bf16[64,768]{1,0:T(8,128)(2,1)S(1)}, bf16[64,768]{1,0:T(8,128)(2,1)}, u32[]{:S(2)}, u32[]{:S(2)}) collective-permute-start(bf16[64,768]{1,0:T(8,128)(2,1)S(1)} %select_bitcast_fusion.2.refs_4_), channel_id=1, source_target_pairs={{0,12},{4,8},{8,4},{12,0},{1,13},{5,9},{9,5},{13,1},{2,14},{6,10},... | collective-permute-start | bytes 294920 | tf_op jit(solution)/shard_map/ppermute | solution.py:38
  130.7 7.5 %collective-permute-start.29 = (bf16[64,768]{1,0:T(8,128)(2,1)S(1)}, bf16[64,768]{1,0:T(8,128)(2,1)S(1)}, u32[]{:S(2)}, u32[]{:S(2)}) collective-permute-start(bf16[64,768]{1,0:T(8,128)(2,1)S(1)} %get-tuple-element.120), channel_id=1, source_target_pairs={{0,4},{4,0},{8,12},{12,8},{1,5},{5,1},{9,13},{13,9},{2,6},{6,2},{1... | collective-permute-start | bytes 294920 | tf_op jit(solution)/shard_map/ppermute | solution.py:31
  159.3 89.1 %reduce-scatter.3.cloned.1.call-start = ((), (), s32[]{:S(2)}) async-start(), calls=%async_computation.6 | async-start | bytes 3981312 | tf_op jit(solution)/shard_map/reduce_scatter | solution.py:870
  206.4 9.3 %all-to-all-start.2 = ((f32[8,22,192]{2,1,0:T(8,128)}), f32[8,22,192]{2,1,0:T(8,128)S(1)}, u32[]{:S(2)}, u32[]{:S(2)}) async-start(f32[8,22,192]{2,1,0:T(8,128)} %get-tuple-element.157), calls=%async_computation.2 | async-start | bytes 393216 | tf_op jit(solution)/shard_map/all_to_all | solution.py:53
  226.1 8.2 %all-to-all-start.3 = ((f32[8,8,192]{2,1,0:T(8,128)}), f32[8,8,192]{2,1,0:T(8,128)S(1)}, u32[]{:S(2)}, u32[]{:S(2)}) async-start(f32[8,8,192]{2,1,0:T(8,128)} %shard_map.295), calls=%async_computation.3 | async-start | bytes 131072 | tf_op jit(solution)/shard_map/all_to_all | solution.py:53
  234.4 7.0 %collective-permute-start.61 = (f32[8,192]{1,0:T(8,128)S(1)}, f32[8,192]{1,0:T(8,128)S(1)}, u32[]{:S(2)}, u32[]{:S(2)}) collective-permute-start(f32[8,192]{1,0:T(8,128)S(1)} %reduce_sum.28.refs_1_), channel_id=1, source_target_pairs={{0,1},{1,0},{2,3},{3,2},{4,5},{5,4},{6,7},{7,6},{8,9},{9,8},{10,11... | collective-permute-start | bytes 18440 | tf_op jit(solution)/shard_map/ppermute | solution.py:38
  234.8 8.8 %collective-permute-start.62 = (f32[8,192]{1,0:T(8,128)S(1)}, f32[8,192]{1,0:T(8,128)S(1)}, u32[]{:S(2)}, u32[]{:S(2)}) collective-permute-start(f32[8,192]{1,0:T(8,128)S(1)} %reduce_sum.28.refs_1_), channel_id=1, source_target_pairs={{0,2},{1,3},{2,0},{3,1},{4,6},{5,7},{6,4},{7,5},{8,10},{9,11},{10,... | collective-permute-start | bytes 18440 | tf_op jit(solution)/shard_map/ppermute | solution.py:38
  (109 other events, 713.5 us)
Sparse Core Ops, SparseCore 0:
  43.7 41.6 all-gather.4
  87.6 30.4 all-gather.6
  159.4 42.0 reduce-scatter.4
  204.8 43.4 reduce-scatter.2
